TPU v7x, 32 devices: a whole 2x2x4 slice. The times are simulated.
32 devices in a mesh: ctx: 16 (over z, y, x), tp: 2 (over core).
Axes of the slice: x: 2, y: 2, z: 4, core: 2. Of those that a mesh axis runs over, the one named last changes fastest.
Arguments:
- k_feature: bfloat16 [8, 524288], P('tp', 'ctx'), may hold values from -6 to 6
- v_feature: bfloat16 [8, 524288], P('tp', 'ctx'), may hold values from -6 to 6
- q_feature: bfloat16 [8, 524288], P('tp', 'ctx'), may hold values from -6 to 6
- spectrum: bfloat16 [2, 8, 1024, 1024], P(None, 'tp', 'ctx'), may hold values from -6 to 6
- skip_gain: float32 [8], P('tp'), may hold values from -1 to 1
- out_weight: bfloat16 [8, 16], replicated, may hold values from -2 to 2
Outputs:
- mixed: bfloat16 [16, 524288], P('tp', 'ctx')
All inputs are finite; a program needn't handle non-finite values.
Results may differ from a plain program's by a relative error of at most 0.015.
Values may be sent and summed in bfloat16 or wider, within the bound.
No kernel may reach another device: no remote copies, remote signals or barrier semaphores. Data moves between devices by JAX's collectives and lax.ppermute only.
A program may use at most 64 MiB of HBM per device.

v0:
```python
import functools
import math

import numpy as np
import ml_dtypes
import jax
import jax.numpy as jnp
from jax import lax
from jax.experimental import pallas as pl
from jax.experimental.pallas import tpu as pltpu
from jax.sharding import PartitionSpec as P

F32 = jnp.float32
BF16 = jnp.bfloat16
VMEM = pl.BlockSpec(memory_space=pltpu.VMEM)
MIB = 1 << 20


def fourier_tables(length_all):
    positions = jnp.arange(length_all, dtype=jnp.int32)
    phase_index = positions[:, None] * positions[None, :] % length_all
    angles = phase_index.astype(jnp.float32) * (2.0 * math.pi / length_all)
    return (jnp.cos(angles).astype(jnp.bfloat16), jnp.sin(angles).astype(jnp.bfloat16))


def twist_tables(left_index, right_index, length_all):
    phase_index = left_index[:, None] * right_index[None, :] % length_all
    angles = phase_index.astype(jnp.float32) * (2.0 * math.pi / length_all)
    return (jnp.cos(angles), jnp.sin(angles))


def contract(form, left, right):
    return jnp.einsum(form, left, right, preferred_element_type=jnp.float32)


def local_general(k_feature, v_feature, q_feature, spectrum, skip_gain, out_weight):
    channels, tokens = k_feature.shape
    block_order = spectrum.shape[3]
    length_all = block_order * block_order
    ctx_count = lax.axis_size("ctx")
    slab_width = block_order // ctx_count
    rows_here = tokens // block_order
    ctx_index = lax.axis_index("ctx")
    product = (k_feature.astype(jnp.float32) * v_feature.astype(jnp.float32)).astype(jnp.bfloat16)
    cosine_full, sine_full = fourier_tables(block_order)
    cosine_half = cosine_full[: block_order // 2]
    sine_half = sine_full[: block_order // 2]
    positions = jnp.arange(block_order, dtype=jnp.int32)
    local_ticks = ctx_index * slab_width + jnp.arange(slab_width, dtype=jnp.int32)
    grid_rows = lax.all_to_all(
        product.reshape(channels, rows_here, block_order),
        "ctx",
        split_axis=2,
        concat_axis=1,
        tiled=True,
    )
    first_real = contract("cij,ia->caj", grid_rows, cosine_half)
    first_imag = -contract("cij,ia->caj", grid_rows, sine_half)
    twist_cosine, twist_sine = twist_tables(positions, local_ticks, length_all)
    spread_real = (first_real * twist_cosine + first_imag * twist_sine).astype(jnp.bfloat16)
    spread_imag = (first_imag * twist_cosine - first_real * twist_sine).astype(jnp.bfloat16)
    block_real, block_imag = (
        lax.all_to_all(spread_real, "ctx", split_axis=1, concat_axis=2, tiled=True),
        lax.all_to_all(spread_imag, "ctx", split_axis=1, concat_axis=2, tiled=True),
    )
    freq_real = contract("caj,jb->cab", block_real, cosine_full) + contract(
        "caj,jb->cab", block_imag, sine_full
    )
    freq_imag = contract("caj,jb->cab", block_imag, cosine_full) - contract(
        "caj,jb->cab", block_real, sine_full
    )
    resp_real = spectrum[0].astype(jnp.float32)
    resp_imag = spectrum[1].astype(jnp.float32)
    shaped_real = (freq_real * resp_real - freq_imag * resp_imag).astype(jnp.bfloat16)
    shaped_imag = (freq_real * resp_imag + freq_imag * resp_real).astype(jnp.bfloat16)
    inner_real = contract("cab,bj->caj", shaped_real, cosine_full) - contract(
        "cab,bj->caj", shaped_imag, sine_full
    )
    inner_imag = contract("cab,bj->caj", shaped_imag, cosine_full) + contract(
        "cab,bj->caj", shaped_real, sine_full
    )
    twist_cosine, twist_sine = twist_tables(local_ticks, positions, length_all)
    back_real = (inner_real * twist_cosine - inner_imag * twist_sine).astype(jnp.bfloat16)
    back_imag = (inner_imag * twist_cosine + inner_real * twist_sine).astype(jnp.bfloat16)
    summed = contract(
        "ia,caj->cij",
        cosine_half,
        lax.all_to_all(back_real, "ctx", split_axis=2, concat_axis=1, tiled=True),
    ) - contract(
        "ia,caj->cij",
        sine_half,
        lax.all_to_all(back_imag, "ctx", split_axis=2, concat_axis=1, tiled=True),
    )
    spatial = (summed * (1.0 / length_all)).astype(jnp.bfloat16)
    convolved = lax.all_to_all(spatial, "ctx", split_axis=1, concat_axis=2, tiled=True).reshape(
        channels, tokens
    )
    gated_rows = (
        q_feature.astype(jnp.float32)
        * (convolved.astype(jnp.float32) + skip_gain[:, None] * product.astype(jnp.float32))
    ).astype(jnp.bfloat16)
    tp_index = lax.axis_index("tp")
    my_weight = lax.dynamic_slice_in_dim(out_weight, tp_index * channels, channels, 0)
    return lax.psum_scatter(
        jnp.dot(my_weight.T, gated_rows, preferred_element_type=jnp.float32).astype(jnp.bfloat16),
        "tp",
        scatter_dimension=0,
        tiled=True,
    )


def cosine_sine(product, length):
    angles = (product % length).astype(np.float64) * (2.0 * np.pi / length)
    return np.cos(angles), np.sin(angles)


@functools.lru_cache(maxsize=None)
def constant_tables(block, members, rows_half, a_half):
    quarter = block // 4
    firsts, lasts, twists = [], [], []
    part = np.arange(members)
    for g in range(2):
        for s in range(2):
            a = (
                (g * members + part)[:, None] * 2 * a_half
                + s * a_half
                + np.arange(a_half)[None, :]
            ).reshape(-1)

            def rows(group, core):
                device = group * members + part
                i = device[:, None] * 2 * rows_half + core * rows_half
                return (i + np.arange(rows_half)[None, :]).reshape(-1)

            i_in = np.concatenate([rows(g, s), rows(g, 1 - s), rows(1 - g, s), rows(1 - g, 1 - s)])
            cosine, sine = cosine_sine(a[:, None] * i_in[None, :], block)
            firsts.append(np.concatenate([cosine, -sine], 0))
            i_out = np.concatenate([rows(0, 1 - s), rows(1, 1 - s), rows(0, s), rows(1, s)])
            cosine, sine = cosine_sine(i_out[:, None] * a[None, :], block)
            lasts.append(np.concatenate([cosine, -sine], 1))
            twists.append(np.stack(cosine_sine(a[:, None] * np.arange(block)[None, :], block * block)))
    inner, outer = [], []
    for rho in range(4):
        cosine, sine = cosine_sine(
            np.arange(quarter)[:, None] * (4 * np.arange(quarter) + rho)[None, :], block
        )
        inner.append(np.block([[cosine, -sine], [sine, cosine]]))
        outer.append(np.block([[cosine.T, sine.T], [-sine.T, cosine.T]]))
    order = np.zeros((block, block), np.float32)
    b = np.arange(block)
    order[b, (b % 4) * quarter + b // 4] = 1.0
    narrow = lambda x: np.asarray(x, np.float32).astype(ml_dtypes.bfloat16)
    return dict(
        first=narrow(np.stack(firsts)),
        last=narrow(np.stack(lasts)),
        twist=np.stack(twists).astype(np.float32),
        inner=narrow(np.stack(inner)),
        outer=narrow(np.stack(outer)),
        order=narrow(order),
    )


def rows_order(channels, rows):
    table = np.zeros((channels * rows, channels * rows), np.float32)
    half = rows // 2
    for i in range(rows):
        for c in range(channels):
            table[(i // half) * channels * half + c * half + i % half, i * channels + c] = 1.0
    return table.astype(ml_dtypes.bfloat16)


def rows_kernel(block, *refs):
    *ins, order_ref, out_ref = refs
    tokens = ins[0].shape[1]
    pieces = []
    for i in range(tokens // block):
        cut = slice(i * block, (i + 1) * block)
        piece = ins[0][:, cut].astype(F32)
        for other in ins[1:]:
            piece = piece * other[:, cut].astype(F32)
        pieces.append(piece)
    stacked = jnp.concatenate(pieces, axis=0).astype(BF16)
    ordered = jnp.dot(order_ref[...], stacked, preferred_element_type=F32)
    out_ref[...] = ordered.astype(BF16).reshape(out_ref.shape)


def as_rows(block, *arrays):
    channels, tokens = arrays[0].shape
    rows = tokens // block
    return pl.pallas_call(
        functools.partial(rows_kernel, block),
        out_shape=jax.ShapeDtypeStruct((2, channels, rows // 2, block), BF16),
        in_specs=[VMEM] * (len(arrays) + 1),
        out_specs=VMEM,
        compiler_params=pltpu.CompilerParams(vmem_limit_bytes=16 * MIB),
        cost_estimate=pl.CostEstimate(flops=40_000_000, bytes_accessed=MIB, transcendentals=0),
    )(*arrays, jnp.asarray(rows_order(channels, rows)))


def spectrum_kernel(in_ref, order_ref, out_ref):
    block = order_ref.shape[0]
    rows = in_ref[...].reshape(-1, block)
    moved = jnp.dot(rows, order_ref[...], preferred_element_type=F32)
    out_ref[...] = moved.astype(BF16).reshape(out_ref.shape)


def arrange_spectrum(spectrum, order):
    two, channels, a_here, block = spectrum.shape
    a_half = a_here // 2
    return pl.pallas_call(
        spectrum_kernel,
        grid=(2, channels),
        out_shape=jax.ShapeDtypeStruct((2, channels, two, a_half, block), BF16),
        in_specs=[
            pl.BlockSpec((two, 1, a_half, block), lambda h, c: (0, c, h, 0)),
            pl.BlockSpec((block, block), lambda h, c: (0, 0)),
        ],
        out_specs=pl.BlockSpec((1, 1, two, a_half, block), lambda h, c: (h, c, 0, 0, 0)),
        compiler_params=pltpu.CompilerParams(vmem_limit_bytes=16 * MIB),
        cost_estimate=pl.CostEstimate(
            flops=1_100_000_000, bytes_accessed=4 * MIB, transcendentals=0
        ),
    )(spectrum, order)


def transform_kernel(
    place_ref, xa, xb, za1, za2, zb1, zb2, first, twist, spec, inner, outer, last, send, keep
):
    block = xa.shape[-1]
    quarter = block // 4
    flat = lambda ref: ref[...].reshape(-1, block)
    signal = jnp.concatenate([flat(xa), flat(xb), flat(za1), flat(za2), flat(zb1), flat(zb2)], 0)
    a_rows = first.shape[1] // 2
    turned = []
    for q in range(4):
        cut = slice(q * quarter, (q + 1) * quarter)
        both = jnp.dot(first[0], signal[:, cut], preferred_element_type=F32)
        real, imag = both[:a_rows], both[a_rows:]
        cosine, sine = twist[0, 0, :, cut], twist[0, 1, :, cut]
        turned.append((real * cosine + imag * sine, imag * cosine - real * sine))
    (r0, i0), (r1, i1), (r2, i2), (r3, i3) = turned
    er, ei, dr, di = r0 + r2, i0 + i2, r0 - r2, i0 - i2
    fr, fi, hr, hi = r1 + r3, i1 + i3, r1 - r3, i1 - i3
    mixes = [(er + fr, ei + fi), (dr + hi, di - hr), (er - fr, ei - fi), (dr - hi, di + hr)]
    backs = []
    for rho in range(4):
        real, imag = mixes[rho]
        pair = jnp.concatenate([real.astype(BF16), imag.astype(BF16)], axis=1)
        freq = jnp.dot(pair, inner[rho], preferred_element_type=F32)
        zr, zi = freq[:, :quarter], freq[:, quarter:]
        cut = slice(rho * quarter, (rho + 1) * quarter)
        gr = spec[:, 0, :, cut].reshape(-1, quarter).astype(F32)
        gi = spec[:, 1, :, cut].reshape(-1, quarter).astype(F32)
        pair = jnp.concatenate(
            [(zr * gr - zi * gi).astype(BF16), (zr * gi + zi * gr).astype(BF16)], axis=1
        )
        out = jnp.dot(pair, outer[rho], preferred_element_type=F32)
        backs.append((out[:, :quarter], out[:, quarter:]))
    (r0, i0), (r1, i1), (r2, i2), (r3, i3) = backs
    er, ei, dr, di = r0 + r2, i0 + i2, r0 - r2, i0 - i2
    fr, fi, hr, hi = r1 + r3, i1 + i3, r1 - r3, i1 - i3
    mixes = [(er + fr, ei + fi), (dr - hi, di + hr), (er - fr, ei - fi), (dr + hi, di - hr)]
    scale = 1.0 / (block * block)
    half = last.shape[1] // 2
    for q in range(4):
        cut = slice(q * quarter, (q + 1) * quarter)
        real, imag = mixes[q]
        cosine, sine = twist[0, 0, :, cut], twist[0, 1, :, cut]
        pair = jnp.concatenate(
            [
                (real * cosine - imag * sine).astype(BF16),
                (imag * cosine + real * sine).astype(BF16),
            ],
            axis=0,
        )
        out = jnp.dot(last[0], pair, preferred_element_type=F32) * scale
        send[:, :, cut] = out[:half].astype(BF16).reshape(send.shape[0], send.shape[1], quarter)
        keep[:, :, cut] = out[half:].reshape(keep.shape[0], keep.shape[1], quarter)


def transform(place, pieces, spec, tables):
    members, rows_half, block = pieces[0].shape
    whole = lambda x: pl.BlockSpec(x.shape, lambda n, p: (0,) * x.ndim)
    picked = lambda x: pl.BlockSpec((1,) + x.shape[1:], lambda n, p: (p[0],) + (0,) * (x.ndim - 1))
    first, twist, last = tables["first"], tables["twist"], tables["last"]
    inner, outer = tables["inner"], tables["outer"]
    out = (2 * members, rows_half, block)
    return pl.pallas_call(
        transform_kernel,
        grid_spec=pltpu.PrefetchScalarGridSpec(
            num_scalar_prefetch=1,
            grid=(1,),
            in_specs=[whole(x) for x in pieces]
            + [picked(first), picked(twist), whole(spec), whole(inner), whole(outer), picked(last)],
            out_specs=[pl.BlockSpec(out, lambda n, p: (0, 0, 0))] * 2,
        ),
        out_shape=[jax.ShapeDtypeStruct(out, BF16), jax.ShapeDtypeStruct(out, F32)],
        compiler_params=pltpu.CompilerParams(vmem_limit_bytes=48 * MIB),
        cost_estimate=pl.CostEstimate(
            flops=2_200_000_000, bytes_accessed=12 * MIB, transcendentals=0
        ),
    )(place, *pieces, first, twist, spec, inner, outer, last)


def gate_kernel(conv, prod, gate, skip, weight, keep, send):
    _, channels, rows, block = conv.shape
    pieces = []
    for c in range(channels):
        total = conv[0, c].astype(F32) + conv[1, c].astype(F32)
        total = total + skip[c] * prod[c].astype(F32)
        pieces.append((gate[c].astype(F32) * total).astype(BF16))
    gated = jnp.concatenate(pieces, axis=0)
    mixed = jnp.dot(weight[...], gated, preferred_element_type=F32)
    outs = keep.shape[0]
    for r in range(rows):
        cut = slice(r * block, (r + 1) * block)
        keep[:, cut] = mixed[r * outs : (r + 1) * outs].astype(BF16)
        send[:, cut] = mixed[(rows + r) * outs : (rows + r + 1) * outs].astype(BF16)


def gate_and_project(conv, prod, gate, skip, weight, outs):
    _, channels, rows, block = conv.shape
    return pl.pallas_call(
        gate_kernel,
        out_shape=[jax.ShapeDtypeStruct((outs, rows * block), BF16)] * 2,
        in_specs=[VMEM, VMEM, VMEM, pl.BlockSpec(memory_space=pltpu.SMEM), VMEM],
        out_specs=[VMEM, VMEM],
        compiler_params=pltpu.CompilerParams(vmem_limit_bytes=16 * MIB),
        cost_estimate=pl.CostEstimate(
            flops=80_000_000, bytes_accessed=2 * MIB, transcendentals=0
        ),
    )(conv, prod, gate, skip, weight)


def local_channels(k_feature, v_feature, q_feature, spectrum, skip_gain, out_weight):
    channels, tokens = k_feature.shape
    block = spectrum.shape[3]
    ctx_count = lax.axis_size("ctx")
    members = ctx_count // 2
    rows_half = tokens // block // 2
    a_half = spectrum.shape[2] // 2
    outs = out_weight.shape[1] // 2
    ctx, tp = lax.axis_index("ctx"), lax.axis_index("tp")
    tables = {
        name: jnp.asarray(table)
        for name, table in constant_tables(block, members, rows_half, a_half).items()
    }
    halves = [list(range(members)), list(range(members, 2 * members))]
    spread = lambda x: lax.all_to_all(x, "ctx", 0, 0, axis_index_groups=halves, tiled=True)
    across = lambda x: lax.ppermute(
        x, "ctx", [(d, (d + members) % ctx_count) for d in range(ctx_count)]
    )
    swap = lambda x: lax.ppermute(x, "tp", [(0, 1), (1, 0)])
    regroup = lambda x: lax.all_to_all(x, "tp", 0, 0, tiled=True)

    product = regroup(as_rows(block, k_feature, v_feature)).reshape(members, rows_half, block)
    xa = spread(product)
    xb = swap(xa)
    cut = members // 2
    za1, za2 = across(xa[:cut]), across(xa[cut:])
    zb1, zb2 = swap(za1), swap(za2)
    gate = regroup(as_rows(block, q_feature)).reshape(members, rows_half, block)
    skip = regroup(jnp.broadcast_to(skip_gain[None], (2, channels))).reshape(-1)
    spec = regroup(arrange_spectrum(spectrum, tables["order"]))
    spec = spread(spec.reshape(members, 2, a_half, block))

    place = (ctx // members * 2 + tp).astype(jnp.int32).reshape(1)
    send, keep = transform(place, (xa, xb, za1, za2, zb1, zb2), spec, tables)
    total = (keep + swap(send).astype(F32)).astype(BF16)
    conv = lax.all_to_all(total, "ctx", 0, 0, tiled=True).reshape(2, members, rows_half, block)

    mine = lax.dynamic_slice_in_dim(out_weight, tp * outs, outs, 1)
    other = lax.dynamic_slice_in_dim(out_weight, (1 - tp) * outs, outs, 1)
    weight = jnp.stack([mine, other]).astype(F32)
    weight = jnp.einsum("hce,rs->hrecs", weight, jnp.eye(rows_half, dtype=F32))
    weight = weight.astype(BF16).reshape(2 * rows_half * outs, members * rows_half)
    kept, sent = gate_and_project(conv, product, gate, skip, weight, outs)
    came = swap(sent)
    low = jnp.where(tp == 0, kept, came)
    high = jnp.where(tp == 0, came, kept)
    return jnp.concatenate([low, high], axis=1)


def local(k_feature, v_feature, q_feature, spectrum, skip_gain, out_weight):
    channels, tokens = k_feature.shape
    block = spectrum.shape[3]
    ctx_count, tp_count = lax.axis_size("ctx"), lax.axis_size("tp")
    by_channels = (
        tp_count == 2
        and ctx_count == 2 * channels * tp_count
        and tokens * ctx_count * 2 == block * block
        and tokens % (32 * block) == 0
        and spectrum.shape[2] % 32 == 0
        and block % 512 == 0
        and out_weight.shape[1] % 16 == 0
    )
    plan = local_channels if by_channels else local_general
    return plan(k_feature, v_feature, q_feature, spectrum, skip_gain, out_weight)


def solution(mesh):
    placed = (
        P("tp", "ctx"),
        P("tp", "ctx"),
        P("tp", "ctx"),
        P(None, "tp", "ctx", None),
        P("tp"),
        P(),
    )
    return jax.shard_map(
        local, mesh=mesh, in_specs=placed, out_specs=P("tp", "ctx"), check_vma=False
    )
```

profile of v0, /device:TPU:0, one launch (start us, length us, event | category | flops | bytes accessed | tf_op | source)
XLA Modules:
  0.0 98.5 jit_solution(13238535582328357107)
XLA Ops:
  0.0 0.9 copy-done.3
  1.0 0.9 copy-done.4
  1.9 0.8 copy-done.6
  2.7 1.0 shard_map.136
  3.6 3.4 %all-to-all-start = ((bf16[2,4,16,1024]{3,2,1,0:T(8,128)(2,1)}), bf16[2,4,16,1024]{3,2,1,0:T(8,128)(2,1)S(1)}, u32[]{:S(2)}, u32[]{:S(2)}) async-start(bf16[2,4,16,1024]{3,2,1,0:T(8,128)(2,1)} %shard_map.136), calls=%async_computation | async-start | bytes 524288 | tf_op jit(solution)/shard_map/all_to_all | solution.py:354
  7.1 0.0 copy-start
  7.1 1.6 %copy-done = bf16[1024,1024]{1,0:T(8,128)(2,1)S(1)} copy-done((bf16[1024,1024]{1,0:T(8,128)(2,1)S(1)}, bf16[1024,1024]{1,0:T(8,128)(2,1)}, u32[]{:S(2)}) %copy-start) | copy-done | bytes 2097176
  8.7 1.2 %copy-done.2 = bf16[2,4,64,1024]{3,2,1,0:T(8,128)(2,1)S(1)} copy-done((bf16[2,4,64,1024]{3,2,1,0:T(8,128)(2,1)S(1)}, bf16[2,4,64,1024]{3,2,1,0:T(8,128)(2,1)}, u32[]{:S(2)}) %copy-start.2) | copy-done | bytes 1048600
  9.9 4.0 %shard_map.137 = bf16[2,4,2,32,1024]{4,3,2,1,0:T(8,128)(2,1)S(1)} custom-call(bf16[2,4,64,1024]{3,2,1,0:T(8,128)(2,1)S(1)} %copy-done.2, bf16[1024,1024]{1,0:T(8,128)(2,1)S(1)} %copy-done), custom_call_target="tpu_custom_call" | custom-call | flops 1100000000 | bytes 4194304 | tf_op jit(solution)/shard_map/pallas_call | solution.py:210
  14.0 0.0 all-to-all-done
  14.0 5.4 %all_to_all.36 = bf16[2,4,2,32,1024]{4,3,2,1,0:T(8,128)(2,1)} all-to-all(bf16[2,4,2,32,1024]{4,3,2,1,0:T(8,128)(2,1)S(1)} %shard_map.137), channel_id=1, replica_groups=mesh['ctx'=16,'tp'=2] {'tp'}, dimensions={0} | all-to-all | bytes 2097152 | tf_op jit(solution)/shard_map/all_to_all | solution.py:354
  19.3 12.9 %all_to_all.37.xa = bf16[8,16,1024]{2,1,0:T(8,128)(2,1)S(1)} all-to-all(bf16[8,16,1024]{2,1,0:T(8,128)(2,1)S(1)} %bitcast.13), channel_id=1, replica_groups={{0,2,4,6,8,10,12,14},{16,18,20,22,24,26,28,30},{1,3,5,7,9,11,13,15},{17..., dimensions={0} | all-to-all | bytes 524288 | tf_op jit(solution)/shard_map/all_to_all | solution.py:349
  32.2 3.6 %all-to-all-start.3 = ((bf16[8,2,32,1024]{3,2,1,0:T(8,128)(2,1)}), bf16[8,2,32,1024]{3,2,1,0:T(8,128)(2,1)S(1)}, u32[]{:S(2)}, u32[]{:S(2)}) async-start(bf16[8,2,32,1024]{3,2,1,0:T(8,128)(2,1)} %bitcast.2), calls=%async_computation.3 | async-start | bytes 2097152 | tf_op jit(solution)/shard_map/all_to_all | solution.py:349
  35.8 2.7 %collective-permute-start.1 = (bf16[4,16,1024]{2,1,0:T(8,128)(2,1)S(1)}, bf16[4,16,1024]{2,1,0:T(8,128)(2,1)S(1)}, u32[]{:S(2)}, u32[]{:S(2)}) collective-permute-start(bf16[4,16,1024]{2,1,0:T(8,128)(2,1)S(1)} %get-tuple-element.16), channel_id=1, source_target_pairs={{0,16},{2,18},{4,20},{6,22},{8,24},{10,26},{12,28},{14,30},{16,0},... | collective-permute-start | bytes 393224 | tf_op jit(solution)/shard_map/ppermute | solution.py:350
  38.5 0.3 collective-permute-start.2
  38.8 0.0 collective-permute-start
  38.8 11.6 %collective-permute-done.1.za1 = bf16[4,16,1024]{2,1,0:T(8,128)(2,1)S(1)} collective-permute-done((bf16[4,16,1024]{2,1,0:T(8,128)(2,1)S(1)}, bf16[4,16,1024]{2,1,0:T(8,128)(2,1)S(1)}, u32[]{:S(2)}, u32[]{:S(2)}) %collective-permute-start.1) | collective-permute-done | bytes 131104 | tf_op jit(solution)/shard_map/ppermute | solution.py:350
  50.4 0.0 collective-permute-start.3
  50.4 1.4 %collective-permute-done.2.za2 = bf16[4,16,1024]{2,1,0:T(8,128)(2,1)S(1)} collective-permute-done((bf16[4,16,1024]{2,1,0:T(8,128)(2,1)S(1)}, bf16[4,16,1024]{2,1,0:T(8,128)(2,1)S(1)}, u32[]{:S(2)}, u32[]{:S(2)}) %collective-permute-start.2) | collective-permute-done | bytes 131104 | tf_op jit(solution)/shard_map/ppermute | solution.py:350
  51.8 0.0 collective-permute-start.4
  51.8 0.0 collective-permute-done.3.zb1
  51.8 1.3 %collective-permute-done.4.zb2 = bf16[4,16,1024]{2,1,0:T(8,128)(2,1)S(1)} collective-permute-done((bf16[4,16,1024]{2,1,0:T(8,128)(2,1)S(1)}, bf16[4,16,1024]{2,1,0:T(8,128)(2,1)S(1)}, u32[]{:S(2)}, u32[]{:S(2)}) %collective-permute-start.4) | collective-permute-done | bytes 131104 | tf_op jit(solution)/shard_map/ppermute | solution.py:353
  53.2 0.0 collective-permute-done.xb
  53.2 1.0 %all-to-all-done.3.spec = bf16[8,2,32,1024]{3,2,1,0:T(8,128)(2,1)S(1)} async-done(((bf16[8,2,32,1024]{3,2,1,0:T(8,128)(2,1)}), bf16[8,2,32,1024]{3,2,1,0:T(8,128)(2,1)S(1)}, u32[]{:S(2)}, u32[]{:S(2)}) %all-to-all-start.3) | async-done | bytes 1048608 | tf_op jit(solution)/shard_map/all_to_all | solution.py:349
  54.2 1.6 %copy-done.1 = bf16[4,512,512]{2,1,0:T(8,128)(2,1)S(1)} copy-done((bf16[4,512,512]{2,1,0:T(8,128)(2,1)S(1)}, bf16[4,512,512]{2,1,0:T(8,128)(2,1)}, u32[]{:S(2)}) %copy-start.1) | copy-done | bytes 2097176
  55.8 7.1 %shard_map.138 = (bf16[16,16,1024]{2,1,0:T(8,128)(2,1)}, f32[16,16,1024]{2,1,0:T(8,128)S(1)}) custom-call(s32[1]{0:T(128)} %bitcast.place_ref, bf16[8,16,1024]{2,1,0:T(8,128)(2,1)S(1)} %all_to_all.37.xa, bf16[8,16,1024]{2,1,0:T(8,128)(2,1)S(1)} %collective-permute-done.xb, bf16[4,16,1024]{2,1,0:T(8,128)(2,1)S(1)} %collective-permute-done.1.za1, ...), custom_call_target="tpu_custom_call" | custom-call | flops 2200000000 | bytes 12582912 | tf_op jit(solution)/shard_map/pallas_call | solution.py:288
  62.9 0.0 collective-permute-start.5
  62.9 0.0 copy-done.5
  62.9 0.0 copy-done.7
  62.9 0.9 shard_map.139
  63.9 3.4 %all-to-all-start.5 = ((bf16[2,4,16,1024]{3,2,1,0:T(8,128)(2,1)}), bf16[2,4,16,1024]{3,2,1,0:T(8,128)(2,1)S(1)}, u32[]{:S(2)}, u32[]{:S(2)}) async-start(bf16[2,4,16,1024]{3,2,1,0:T(8,128)(2,1)} %shard_map.139), calls=%async_computation.5 | async-start | bytes 524288 | tf_op jit(solution)/shard_map/all_to_all | solution.py:354
  67.3 0.0 collective-permute-done.5
  67.3 0.9 add_convert_fusion
  68.3 0.6 all-to-all-done.5
  68.9 3.6 %all_to_all.38 = f32[2,1,4]{2,1,0:T(1,128)S(1)} all-to-all(f32[2,1,4]{2,1,0:T(1,128)S(1)} %broadcast_in_dim.2), channel_id=1, replica_groups=mesh['ctx'=16,'tp'=2] {'tp'}, dimensions={0} | all-to-all | bytes 64 | tf_op jit(solution)/shard_map/all_to_all | solution.py:354
  72.5 7.2 %all-to-all-start.4 = ((bf16[16,16,1024]{2,1,0:T(8,128)(2,1)}), bf16[16,16,1024]{2,1,0:T(8,128)(2,1)S(1)}, u32[]{:S(2)}, u32[]{:S(2)}) async-start(bf16[16,16,1024]{2,1,0:T(8,128)(2,1)} %add_convert_fusion), calls=%async_computation.4 | async-start | bytes 1048576 | tf_op jit(solution)/shard_map/all_to_all | solution.py:370
  79.7 0.1 dynamic-slice_bitcast_fusion.1
  79.8 0.1 copy.16
  79.9 0.2 fusion
  80.1 0.3 reshape.34.weight
  80.4 0.6 broadcast.9
  81.0 0.7 reduce.3
  81.7 0.1 reshape.33.skip
  81.8 13.4 %all-to-all-done.4 = bf16[16,16,1024]{2,1,0:T(8,128)(2,1)S(1)} async-done(((bf16[16,16,1024]{2,1,0:T(8,128)(2,1)}), bf16[16,16,1024]{2,1,0:T(8,128)(2,1)S(1)}, u32[]{:S(2)}, u32[]{:S(2)}) %all-to-all-start.4) | async-done | bytes 524320 | tf_op jit(solution)/shard_map/all_to_all | solution.py:370
  95.2 0.9 shard_map.140
  96.1 0.1 collective-permute-start.6
  96.1 1.5 %collective-permute-done.6 = bf16[8,16384]{1,0:T(8,128)(2,1)S(1)} collective-permute-done((bf16[8,16384]{1,0:T(8,128)(2,1)S(1)}, bf16[8,16384]{1,0:T(8,128)(2,1)S(1)}, u32[]{:S(2)}, u32[]{:S(2)}) %collective-permute-start.6) | collective-permute-done | bytes 262176 | tf_op jit(solution)/shard_map/ppermute | solution.py:353
  97.7 0.8 pad_maximum_fusion
  (16 shorter events, 0.1 us)
Async XLA Ops:
  0.0 0.9 copy-start.3
  1.0 0.9 copy-start.4
  1.9 0.8 copy-start.6
  3.6 10.3 %all-to-all-start = ((bf16[2,4,16,1024]{3,2,1,0:T(8,128)(2,1)}), bf16[2,4,16,1024]{3,2,1,0:T(8,128)(2,1)S(1)}, u32[]{:S(2)}, u32[]{:S(2)}) async-start(bf16[2,4,16,1024]{3,2,1,0:T(8,128)(2,1)} %shard_map.136), calls=%async_computation | async-start | bytes 524288 | tf_op jit(solution)/shard_map/all_to_all | solution.py:354
  7.1 1.6 %copy-start = (bf16[1024,1024]{1,0:T(8,128)(2,1)S(1)}, bf16[1024,1024]{1,0:T(8,128)(2,1)}, u32[]{:S(2)}) copy-start(bf16[1024,1024]{1,0:T(8,128)(2,1)} %constant.50.clone.order_ref) | copy-start | bytes 6291460
  8.7 1.2 %copy-start.2 = (bf16[2,4,64,1024]{3,2,1,0:T(8,128)(2,1)S(1)}, bf16[2,4,64,1024]{3,2,1,0:T(8,128)(2,1)}, u32[]{:S(2)}) copy-start(bf16[2,4,64,1024]{3,2,1,0:T(8,128)(2,1)} %in_ref.1) | copy-start | bytes 3145732
  32.2 21.9 %all-to-all-start.3 = ((bf16[8,2,32,1024]{3,2,1,0:T(8,128)(2,1)}), bf16[8,2,32,1024]{3,2,1,0:T(8,128)(2,1)S(1)}, u32[]{:S(2)}, u32[]{:S(2)}) async-start(bf16[8,2,32,1024]{3,2,1,0:T(8,128)(2,1)} %bitcast.2), calls=%async_computation.3 | async-start | bytes 2097152 | tf_op jit(solution)/shard_map/all_to_all | solution.py:349
  35.8 14.6 %collective-permute-start.1 = (bf16[4,16,1024]{2,1,0:T(8,128)(2,1)S(1)}, bf16[4,16,1024]{2,1,0:T(8,128)(2,1)S(1)}, u32[]{:S(2)}, u32[]{:S(2)}) collective-permute-start(bf16[4,16,1024]{2,1,0:T(8,128)(2,1)S(1)} %get-tuple-element.16), channel_id=1, source_target_pairs={{0,16},{2,18},{4,20},{6,22},{8,24},{10,26},{12,28},{14,30},{16,0},... | collective-permute-start | bytes 393224 | tf_op jit(solution)/shard_map/ppermute | solution.py:350
  38.5 13.3 %collective-permute-start.2 = (bf16[4,16,1024]{2,1,0:T(8,128)(2,1)S(1)}, bf16[4,16,1024]{2,1,0:T(8,128)(2,1)S(1)}, u32[]{:S(2)}, u32[]{:S(2)}) collective-permute-start(bf16[4,16,1024]{2,1,0:T(8,128)(2,1)S(1)} %get-tuple-element.15), channel_id=1, source_target_pairs={{0,16},{2,18},{4,20},{6,22},{8,24},{10,26},{12,28},{14,30},{16,0},... | collective-permute-start | bytes 393224 | tf_op jit(solution)/shard_map/ppermute | solution.py:350
  38.8 14.3 %collective-permute-start = (bf16[8,16,1024]{2,1,0:T(8,128)(2,1)S(1)}, bf16[8,16,1024]{2,1,0:T(8,128)(2,1)S(1)}, u32[]{:S(2)}, u32[]{:S(2)}) collective-permute-start(bf16[8,16,1024]{2,1,0:T(8,128)(2,1)S(1)} %all_to_all.37.xa), channel_id=1, source_target_pairs={{0,1},{1,0},{2,3},{3,2},{4,5},{5,4},{6,7},{7,6},{8,9},{9,8},{10,11... | collective-permute-start | bytes 786440 | tf_op jit(solution)/shard_map/ppermute | solution.py:353
  50.4 1.4 %collective-permute-start.3 = (bf16[4,16,1024]{2,1,0:T(8,128)(2,1)S(1)}, bf16[4,16,1024]{2,1,0:T(8,128)(2,1)S(1)}, u32[]{:S(2)}, u32[]{:S(2)}) collective-permute-start(bf16[4,16,1024]{2,1,0:T(8,128)(2,1)S(1)} %collective-permute-done.1.za1), channel_id=1, source_target_pairs={{0,1},{1,0},{2,3},{3,2},{4,5},{5,4},{6,7},{7,6},{8,9},{9,8},{10,11... | collective-permute-start | bytes 393224 | tf_op jit(solution)/shard_map/ppermute | solution.py:353
  51.8 1.3 %collective-permute-start.4 = (bf16[4,16,1024]{2,1,0:T(8,128)(2,1)S(1)}, bf16[4,16,1024]{2,1,0:T(8,128)(2,1)S(1)}, u32[]{:S(2)}, u32[]{:S(2)}) collective-permute-start(bf16[4,16,1024]{2,1,0:T(8,128)(2,1)S(1)} %collective-permute-done.2.za2), channel_id=1, source_target_pairs={{0,1},{1,0},{2,3},{3,2},{4,5},{5,4},{6,7},{7,6},{8,9},{9,8},{10,11... | collective-permute-start | bytes 393224 | tf_op jit(solution)/shard_map/ppermute | solution.py:353
  54.2 1.6 %copy-start.1 = (bf16[4,512,512]{2,1,0:T(8,128)(2,1)S(1)}, bf16[4,512,512]{2,1,0:T(8,128)(2,1)}, u32[]{:S(2)}) copy-start(bf16[4,512,512]{2,1,0:T(8,128)(2,1)} %constant.45.clone.first) | copy-start | bytes 6291460
  55.8 7.1 %copy-start.5 = (bf16[4,32768]{1,0:T(4,128)(2,1)S(1)}, bf16[4,32768]{1,0:T(4,128)(2,1)}, u32[]{:S(2)}) copy-start(bf16[4,32768]{1,0:T(4,128)(2,1)} %refs_0_.3) | copy-start | bytes 786436
  55.8 7.2 %copy-start.7 = (bf16[128,128]{1,0:T(8,128)(2,1)S(1)}, bf16[128,128]{1,0:T(8,128)(2,1)}, u32[]{:S(2)}) copy-start(bf16[128,128]{1,0:T(8,128)(2,1)} %constant.51.clone.refs_2_.refs_1_) | copy-start | bytes 98308
  62.9 5.9 %copy-start.9 = (f32[4]{0:T(128)S(1)}, f32[4]{0:T(128)}, u32[]{:S(2)}) copy-start(f32[4]{0:T(128)} %param.18) | copy-start | bytes 52
  62.9 16.8 %copy-start.8 = (bf16[8,16]{1,0:T(8,128)(2,1)S(1)}, bf16[8,16]{1,0:T(8,128)(2,1)}, u32[]{:S(2)}) copy-start(bf16[8,16]{1,0:T(8,128)(2,1)} %param.19) | copy-start | bytes 772
  62.9 4.4 %collective-permute-start.5 = (bf16[16,16,1024]{2,1,0:T(8,128)(2,1)}, bf16[16,16,1024]{2,1,0:T(8,128)(2,1)S(1)}, u32[]{:S(2)}, u32[]{:S(2)}) collective-permute-start(bf16[16,16,1024]{2,1,0:T(8,128)(2,1)} %get-tuple-element.10), channel_id=1, source_target_pairs={{0,1},{1,0},{2,3},{3,2},{4,5},{5,4},{6,7},{7,6},{8,9},{9,8},{10,11... | collective-permute-start | bytes 1572872 | tf_op jit(solution)/shard_map/ppermute | solution.py:353
  63.9 5.0 %all-to-all-start.5 = ((bf16[2,4,16,1024]{3,2,1,0:T(8,128)(2,1)}), bf16[2,4,16,1024]{3,2,1,0:T(8,128)(2,1)S(1)}, u32[]{:S(2)}, u32[]{:S(2)}) async-start(bf16[2,4,16,1024]{3,2,1,0:T(8,128)(2,1)} %shard_map.139), calls=%async_computation.5 | async-start | bytes 524288 | tf_op jit(solution)/shard_map/all_to_all | solution.py:354
  72.5 22.7 %all-to-all-start.4 = ((bf16[16,16,1024]{2,1,0:T(8,128)(2,1)}), bf16[16,16,1024]{2,1,0:T(8,128)(2,1)S(1)}, u32[]{:S(2)}, u32[]{:S(2)}) async-start(bf16[16,16,1024]{2,1,0:T(8,128)(2,1)} %add_convert_fusion), calls=%async_computation.4 | async-start | bytes 1048576 | tf_op jit(solution)/shard_map/all_to_all | solution.py:370
  96.1 1.6 %collective-permute-start.6 = (bf16[8,16384]{1,0:T(8,128)(2,1)S(1)}, bf16[8,16384]{1,0:T(8,128)(2,1)S(1)}, u32[]{:S(2)}, u32[]{:S(2)}) collective-permute-start(bf16[8,16384]{1,0:T(8,128)(2,1)S(1)} %get-tuple-element.12), channel_id=1, source_target_pairs={{0,1},{1,0},{2,3},{3,2},{4,5},{5,4},{6,7},{7,6},{8,9},{9,8},{10,11... | collective-permute-start | bytes 786440 | tf_op jit(solution)/shard_map/ppermute | solution.py:353
where the time goes:
time: 99.3 us; the launch traced here: 98.5 us
  waiting for transfers between devices  30.8 us (31%)
  blocking collectives  21.9 us (22%)
  starting transfers between devices  20.7 us (21%)
  Pallas kernels  14 us (14%)
  local copies, waits for them, and re-layouts  8.24 us (8%)
  other arithmetic  2.7 us (3%)
    all_to_all x1, waiting for transfers between devices, local_channels(): lax.all_to_all(total, 'ctx', 0, 0, tiled=True)  13.4 us
    ppermute x2, waiting for transfers between devices, local_channels(): lax.ppermute(x, 'ctx', [(d, (d + members) % ctx_count) for d in range(ctx...  13 us
    all_to_all x1, blocking collectives, local_channels(): lax.all_to_all(x, 'ctx', 0, 0, axis_index_groups=halves, tiled=True)  12.9 us
    all_to_all x2, blocking collectives, local_channels(): regroup = lambda x: lax.all_to_all(x, 'tp', 0, 0, tiled=True)  9.03 us
    all_to_all x1, starting transfers between devices, local_channels(): lax.all_to_all(total, 'ctx', 0, 0, tiled=True)  7.2 us
    pallas_call x1, Pallas kernels, transform(): pl.pallas_call(transform_kernel, grid_spec=pltpu.PrefetchScalarGridSpec(n...  7.13 us
    unnamed x20, local copies, waits for them, and re-layouts  7.07 us
    all_to_all x2, starting transfers between devices, local_channels(): regroup = lambda x: lax.all_to_all(x, 'tp', 0, 0, tiled=True)  6.88 us
  transfers between devices with their start and end apart: 11, of which 7 were waited for; matrix products, arithmetic and copies ran while one was open for 3% of the time, Pallas kernels for 5%

commit v1 on v0

v1 whole, which is shorter than its diff:
```python
import functools
import math

import numpy as np
import ml_dtypes
import jax
import jax.numpy as jnp
from jax import lax
from jax.experimental import pallas as pl
from jax.experimental.pallas import tpu as pltpu
from jax.sharding import PartitionSpec as P

F32 = jnp.float32
BF16 = jnp.bfloat16
VMEM = pl.BlockSpec(memory_space=pltpu.VMEM)
SMEM = pl.BlockSpec(memory_space=pltpu.SMEM)
ANY = pl.BlockSpec(memory_space=pltpu.HBM)
MIB = 1 << 20
SMALL = pl.CostEstimate(flops=1, bytes_accessed=1, transcendentals=0)


def fourier_tables(length_all):
    positions = jnp.arange(length_all, dtype=jnp.int32)
    phase_index = positions[:, None] * positions[None, :] % length_all
    angles = phase_index.astype(jnp.float32) * (2.0 * math.pi / length_all)
    return (jnp.cos(angles).astype(jnp.bfloat16), jnp.sin(angles).astype(jnp.bfloat16))


def twist_tables(left_index, right_index, length_all):
    phase_index = left_index[:, None] * right_index[None, :] % length_all
    angles = phase_index.astype(jnp.float32) * (2.0 * math.pi / length_all)
    return (jnp.cos(angles), jnp.sin(angles))


def contract(form, left, right):
    return jnp.einsum(form, left, right, preferred_element_type=jnp.float32)


def local_general(k_feature, v_feature, q_feature, spectrum, skip_gain, out_weight):
    channels, tokens = k_feature.shape
    block_order = spectrum.shape[3]
    length_all = block_order * block_order
    ctx_count = lax.axis_size("ctx")
    slab_width = block_order // ctx_count
    rows_here = tokens // block_order
    ctx_index = lax.axis_index("ctx")
    product = (k_feature.astype(jnp.float32) * v_feature.astype(jnp.float32)).astype(jnp.bfloat16)
    cosine_full, sine_full = fourier_tables(block_order)
    cosine_half = cosine_full[: block_order // 2]
    sine_half = sine_full[: block_order // 2]
    positions = jnp.arange(block_order, dtype=jnp.int32)
    local_ticks = ctx_index * slab_width + jnp.arange(slab_width, dtype=jnp.int32)
    grid_rows = lax.all_to_all(
        product.reshape(channels, rows_here, block_order),
        "ctx",
        split_axis=2,
        concat_axis=1,
        tiled=True,
    )
    first_real = contract("cij,ia->caj", grid_rows, cosine_half)
    first_imag = -contract("cij,ia->caj", grid_rows, sine_half)
    twist_cosine, twist_sine = twist_tables(positions, local_ticks, length_all)
    spread_real = (first_real * twist_cosine + first_imag * twist_sine).astype(jnp.bfloat16)
    spread_imag = (first_imag * twist_cosine - first_real * twist_sine).astype(jnp.bfloat16)
    block_real, block_imag = (
        lax.all_to_all(spread_real, "ctx", split_axis=1, concat_axis=2, tiled=True),
        lax.all_to_all(spread_imag, "ctx", split_axis=1, concat_axis=2, tiled=True),
    )
    freq_real = contract("caj,jb->cab", block_real, cosine_full) + contract(
        "caj,jb->cab", block_imag, sine_full
    )
    freq_imag = contract("caj,jb->cab", block_imag, cosine_full) - contract(
        "caj,jb->cab", block_real, sine_full
    )
    resp_real = spectrum[0].astype(jnp.float32)
    resp_imag = spectrum[1].astype(jnp.float32)
    shaped_real = (freq_real * resp_real - freq_imag * resp_imag).astype(jnp.bfloat16)
    shaped_imag = (freq_real * resp_imag + freq_imag * resp_real).astype(jnp.bfloat16)
    inner_real = contract("cab,bj->caj", shaped_real, cosine_full) - contract(
        "cab,bj->caj", shaped_imag, sine_full
    )
    inner_imag = contract("cab,bj->caj", shaped_imag, cosine_full) + contract(
        "cab,bj->caj", shaped_real, sine_full
    )
    twist_cosine, twist_sine = twist_tables(local_ticks, positions, length_all)
    back_real = (inner_real * twist_cosine - inner_imag * twist_sine).astype(jnp.bfloat16)
    back_imag = (inner_imag * twist_cosine + inner_real * twist_sine).astype(jnp.bfloat16)
    summed = contract(
        "ia,caj->cij",
        cosine_half,
        lax.all_to_all(back_real, "ctx", split_axis=2, concat_axis=1, tiled=True),
    ) - contract(
        "ia,caj->cij",
        sine_half,
        lax.all_to_all(back_imag, "ctx", split_axis=2, concat_axis=1, tiled=True),
    )
    spatial = (summed * (1.0 / length_all)).astype(jnp.bfloat16)
    convolved = lax.all_to_all(spatial, "ctx", split_axis=1, concat_axis=2, tiled=True).reshape(
        channels, tokens
    )
    gated_rows = (
        q_feature.astype(jnp.float32)
        * (convolved.astype(jnp.float32) + skip_gain[:, None] * product.astype(jnp.float32))
    ).astype(jnp.bfloat16)
    tp_index = lax.axis_index("tp")
    my_weight = lax.dynamic_slice_in_dim(out_weight, tp_index * channels, channels, 0)
    return lax.psum_scatter(
        jnp.dot(my_weight.T, gated_rows, preferred_element_type=jnp.float32).astype(jnp.bfloat16),
        "tp",
        scatter_dimension=0,
        tiled=True,
    )


def cosine_sine(product, length):
    angles = (product % length).astype(np.float64) * (2.0 * np.pi / length)
    return np.cos(angles), np.sin(angles)


@functools.lru_cache(maxsize=None)
def constant_tables(block, members, rows_half, a_half):
    quarter = block // 4
    firsts, lasts, coarses, fines = [], [], [], []
    part = np.arange(members)
    for g in range(2):
        for s in range(2):
            a = (
                (g * members + part)[:, None] * 2 * a_half
                + s * a_half
                + np.arange(a_half)[None, :]
            ).reshape(-1)

            def rows(group, core):
                device = group * members + part
                i = device[:, None] * 2 * rows_half + core * rows_half
                return (i + np.arange(rows_half)[None, :]).reshape(-1)

            i_in = np.concatenate([rows(g, s), rows(g, 1 - s), rows(1 - g, s), rows(1 - g, 1 - s)])
            cosine, sine = cosine_sine(a[:, None] * i_in[None, :], block)
            firsts.append(np.concatenate([cosine, -sine], 0))
            i_out = np.concatenate([rows(0, 1 - s), rows(1, 1 - s), rows(0, s), rows(1, s)])
            cosine, sine = cosine_sine(i_out[:, None] * a[None, :], block)
            lasts.append(np.concatenate([cosine, -sine], 1))
            coarse = 128 * (np.arange(128) % (block // 128))
            coarses.append(np.stack(cosine_sine(a[:, None] * coarse[None, :], block * block)))
            fines.append(np.stack(cosine_sine(a[:, None] * np.arange(128)[None, :], block * block)))
    inner = []
    for rho in range(4):
        cosine, sine = cosine_sine(
            np.arange(quarter)[:, None] * (4 * np.arange(quarter) + rho)[None, :], block
        )
        inner.append(np.stack([cosine, sine, cosine.T, sine.T]))
    order = np.zeros((quarter, quarter), np.float32)
    b = np.arange(quarter)
    order[b, (b % 4) * (quarter // 4) + b // 4] = 1.0
    narrow = lambda x: np.asarray(x, np.float32).astype(ml_dtypes.bfloat16)
    return dict(
        first=narrow(np.stack(firsts)),
        last=narrow(np.stack(lasts)),
        turns=np.stack([coarses, fines], 1).astype(np.float32),
        inner=narrow(np.stack(inner)),
        order=narrow(order),
    )


def product_kernel(block, count, core_ref, *refs):
    ins, outs, scratch, sem = refs[:count], refs[count:-1 - count], refs[-1 - count : -1], refs[-1]
    copies = [pltpu.make_async_copy(ins[n], scratch[n], sem.at[n]) for n in range(count)]
    for copy in copies:
        copy.start()
    rows_copy = None
    if len(outs) == 4:
        spectrum, own, send, other_rows = outs
        a_half = other_rows.shape[2]
        at = pl.ds(pl.multiple_of((1 - core_ref[0]) * a_half, a_half), a_half)
        rows_copy = pltpu.make_async_copy(spectrum.at[:, :, at, :], other_rows, sem.at[count])
        rows_copy.start()
    else:
        own, send = outs
    core = core_ref[0]
    channels, tokens = ins[0].shape
    place = 0 if own.shape[0] == channels else channels * core
    rows = tokens // block
    half = rows // 2
    to = lax.broadcasted_iota(jnp.int32, (channels * rows, channels * rows), 0)
    at = lax.broadcasted_iota(jnp.int32, (channels * rows, channels * rows), 1)
    side = jnp.bitwise_xor(to // (channels * half), core)
    source = (side * half + to % half) * channels + (to // half) % channels
    order = jnp.where(at == source, 1.0, 0.0).astype(BF16)
    for copy in copies:
        copy.wait()
    pieces = []
    for i in range(rows):
        cut = slice(i * block, (i + 1) * block)
        piece = scratch[0][:, cut].astype(F32)
        for other in scratch[1:]:
            piece = piece * other[:, cut].astype(F32)
        pieces.append(piece)
    stacked = jnp.concatenate(pieces, axis=0).astype(BF16)
    ordered = jnp.dot(order, stacked, preferred_element_type=F32).astype(BF16)
    ordered = ordered.reshape(2, channels, half, block)
    own[pl.ds(place, channels)] = ordered[0]
    send[...] = ordered[1]
    if rows_copy is not None:
        rows_copy.wait()


def as_rows(core, block, *arrays, spectrum=None):
    channels, tokens = arrays[0].shape
    half = tokens // block // 2
    room, extra, shapes = 1, [], []
    if spectrum is not None:
        two, _, a_here, _ = spectrum.shape
        room, extra = 2, [spectrum]
        shapes = [jax.ShapeDtypeStruct((two, channels, a_here // 2, block), BF16)]
    return pl.pallas_call(
        functools.partial(product_kernel, block, len(arrays)),
        out_shape=[
            jax.ShapeDtypeStruct((room * channels, half, block), BF16),
            jax.ShapeDtypeStruct((channels, half, block), BF16),
        ]
        + shapes,
        in_specs=[SMEM] + [ANY] * len(arrays + tuple(extra)),
        out_specs=[VMEM] * (2 + len(shapes)),
        scratch_shapes=[pltpu.VMEM((channels, tokens), BF16)] * len(arrays)
        + [pltpu.SemaphoreType.DMA((len(arrays) + 1,))],
        cost_estimate=SMALL,
    )(core, *arrays, *extra)


def spectrum_kernel(core_ref, in_ref, came_ref, order_ref, *refs):
    moved, rows, came, order, sem = refs
    core = core_ref[0]
    two, channels, a_half, block = rows.shape
    at = pl.ds(pl.multiple_of(core * a_half, a_half), a_half)
    copies = [
        pltpu.make_async_copy(order_ref, order, sem.at[0]),
        pltpu.make_async_copy(in_ref.at[:, :, at, :], rows, sem.at[1]),
        pltpu.make_async_copy(came_ref, came, sem.at[2]),
    ]
    for copy in copies:
        copy.start()
    copies[0].wait()
    quarter = block // 4
    step = quarter // 4
    for side, ref in ((core, rows), (1 - core, came)):
        copies[1 if ref is rows else 2].wait()
        flat = jnp.concatenate([ref[n, c] for c in range(channels) for n in range(two)], 0)
        parts = [
            jnp.dot(flat[:, q * quarter : (q + 1) * quarter], order[...], preferred_element_type=F32)
            for q in range(4)
        ]
        for rho in range(4):
            columns = [part[:, rho * step : (rho + 1) * step] for part in parts]
            columns = jnp.concatenate(columns, axis=1).astype(BF16)
            moved[pl.ds(channels * side, channels), :, :, rho * quarter : (rho + 1) * quarter] = (
                columns.reshape(channels, two, a_half, quarter)
            )


def arrange_spectrum(core, spectrum, came, order):
    two, channels, a_half, block = came.shape
    return pl.pallas_call(
        spectrum_kernel,
        out_shape=jax.ShapeDtypeStruct((2 * channels, two, a_half, block), BF16),
        in_specs=[SMEM, ANY, ANY, ANY],
        out_specs=VMEM,
        scratch_shapes=[
            pltpu.VMEM(came.shape, BF16),
            pltpu.VMEM(came.shape, BF16),
            pltpu.VMEM(order.shape, BF16),
            pltpu.SemaphoreType.DMA((3,)),
        ],
        cost_estimate=SMALL,
    )(core, spectrum, came, order)


def weight_kernel(rows, core_ref, weight, out):
    channels, outs = weight.shape
    half = outs // 2
    core = core_ref[0]
    shape = out.shape
    to = lax.broadcasted_iota(jnp.int32, (shape[0], outs), 0)
    at = lax.broadcasted_iota(jnp.int32, (shape[0], outs), 1)
    column = jnp.bitwise_xor(to // (rows * half), core) * half + to % half
    pick = jnp.where(at == column, 1.0, 0.0).astype(BF16)
    turned = lax.dot_general(
        pick, weight[...], (((1,), (1,)), ((), ())), preferred_element_type=F32
    ).astype(BF16)
    to = lax.broadcasted_iota(jnp.int32, (channels, shape[1]), 0)
    at = lax.broadcasted_iota(jnp.int32, (channels, shape[1]), 1)
    channel = (at // rows + core * (channels // 2)) % channels
    widen = jnp.where(channel == to, 1.0, 0.0).astype(BF16)
    wide = jnp.dot(turned, widen, preferred_element_type=F32)
    to = lax.broadcasted_iota(jnp.int32, shape, 0)
    at = lax.broadcasted_iota(jnp.int32, shape, 1)
    out[...] = jnp.where(at % rows == (to // half) % rows, wide, 0.0).astype(BF16)


def projection(core, weight, rows):
    channels, outs = weight.shape
    return pl.pallas_call(
        functools.partial(weight_kernel, rows),
        out_shape=jax.ShapeDtypeStruct((rows * outs, rows * channels), BF16),
        in_specs=[SMEM, VMEM],
        out_specs=VMEM,
        compiler_params=pltpu.CompilerParams(vmem_limit_bytes=4 * MIB),
    )(core, weight)


def butterflies(values, sign):
    (r0, i0), (r1, i1), (r2, i2), (r3, i3) = values
    er, ei, dr, di = r0 + r2, i0 + i2, r0 - r2, i0 - i2
    fr, fi, hr, hi = r1 + r3, i1 + i3, r1 - r3, i1 - i3
    plus, minus = (dr - hi, di + hr), (dr + hi, di - hr)
    if sign < 0:
        plus, minus = minus, plus
    return [(er + fr, ei + fi), plus, (er - fr, ei - fi), minus]


def turn(values, cosine, sine):
    real, imag = values
    rows = real.shape[0]
    both = jnp.concatenate([real.astype(BF16), imag.astype(BF16)], axis=0)
    with_cosine = jnp.dot(both, cosine, preferred_element_type=F32)
    with_sine = jnp.dot(both, sine, preferred_element_type=F32)
    return with_cosine[:rows], with_cosine[rows:], with_sine[:rows], with_sine[rows:]


def transform_kernel(place_ref, *refs):
    ins, (send, keep, signal, spec, *tables, twist, sem) = refs[:9], refs[-10:]
    first, turns, inner, last = tables
    pieces, spec_in, (first_in, turns_in, inner_in, last_in) = ins[:4], ins[4], ins[5:9]
    place = place_ref[0]
    count = pieces[0].shape[0]
    moves = [(first_in.at[place], first)]
    moves += [(ref, signal.at[pl.ds(n * count, count)]) for n, ref in enumerate(pieces)]
    moves += [(turns_in.at[place], turns), (inner_in, inner), (spec_in, spec)]
    moves += [(last_in.at[place], last)]
    copies = [pltpu.make_async_copy(*move, sem.at[n]) for n, move in enumerate(moves)]
    for copy in copies:
        copy.start()
    for copy in copies[:6]:
        copy.wait()
    block = signal.shape[-1]
    quarter = block // 4
    lines = signal[...].reshape(-1, block)
    a_rows = first.shape[0] // 2
    turned = []
    for q in range(4):
        cut = slice(q * quarter, (q + 1) * quarter)
        both = jnp.dot(first[...], lines[:, cut], preferred_element_type=F32)
        for h in range(q * quarter // 128, (q + 1) * quarter // 128):
            lanes = slice(128 * h, 128 * (h + 1))
            uc, us = turns[0, 0, :, h : h + 1], turns[0, 1, :, h : h + 1]
            vc, vs = turns[1, 0], turns[1, 1]
            twist[0, :, lanes] = uc * vc - us * vs
            twist[1, :, lanes] = us * vc + uc * vs
        real, imag = both[:a_rows], both[a_rows:]
        cosine, sine = twist[0, :, cut], twist[1, :, cut]
        turned.append((real * cosine + imag * sine, imag * cosine - real * sine))
    mixes = butterflies(turned, -1)
    for copy in copies[6:-1]:
        copy.wait()
    backs = []
    for rho in range(4):
        rc, ic, rs, si = turn(mixes[rho], inner[rho, 0], inner[rho, 1])
        zr, zi = rc + si, ic - rs
        cut = slice(rho * quarter, (rho + 1) * quarter)
        gr = spec[:, 0, :, cut].reshape(-1, quarter).astype(F32)
        gi = spec[:, 1, :, cut].reshape(-1, quarter).astype(F32)
        shaped = (zr * gr - zi * gi, zr * gi + zi * gr)
        rc, ic, rs, si = turn(shaped, inner[rho, 2], inner[rho, 3])
        backs.append((rc - si, ic + rs))
    mixes = butterflies(backs, 1)
    scale = 1.0 / (block * block)
    half = last.shape[0] // 2
    copies[-1].wait()
    for q, (real, imag) in enumerate(mixes):
        cut = slice(q * quarter, (q + 1) * quarter)
        cosine, sine = twist[0, :, cut], twist[1, :, cut]
        pair = jnp.concatenate(
            [
                (real * cosine - imag * sine).astype(BF16),
                (imag * cosine + real * sine).astype(BF16),
            ],
            axis=0,
        )
        out = jnp.dot(last[...], pair, preferred_element_type=F32) * scale
        send[:, :, cut] = out[:half].astype(BF16).reshape(send.shape[0], send.shape[1], quarter)
        keep[:, :, cut] = out[half:].reshape(keep.shape[0], keep.shape[1], quarter)


def transform(place, pieces, spec, tables):
    members, rows_half, block = pieces[0].shape
    held = [tables[n] for n in ("first", "turns", "inner", "last")]
    first, turns, inner, last = held
    out = (2 * members, rows_half, block)
    operands = [*pieces, spec, *held]
    return pl.pallas_call(
        transform_kernel,
        in_specs=[SMEM] + [ANY] * len(operands),
        out_specs=[VMEM, VMEM],
        out_shape=[jax.ShapeDtypeStruct(out, BF16), jax.ShapeDtypeStruct(out, F32)],
        scratch_shapes=[
            pltpu.VMEM((4 * members, rows_half, block), BF16),
            pltpu.VMEM(spec.shape, BF16),
            pltpu.VMEM(first.shape[1:], BF16),
            pltpu.VMEM(turns.shape[1:], F32),
            pltpu.VMEM(inner.shape, BF16),
            pltpu.VMEM(last.shape[1:], BF16),
            pltpu.VMEM((2, turns.shape[3], block), F32),
            pltpu.SemaphoreType.DMA((9,)),
        ],
        compiler_params=pltpu.CompilerParams(vmem_limit_bytes=60 * MIB),
        cost_estimate=SMALL,
    )(place, *operands)


def gate_kernel(core_ref, conv, prod, gate, gate_other, skip, skip_other, weight, keep, send):
    _, channels, rows, block = conv.shape
    core = core_ref[0]
    here = channels // 2
    pieces = []
    for side, (values, gains) in enumerate(((gate, skip), (gate_other, skip_other))):
        for n in range(here):
            c = jnp.bitwise_xor(core, side) * here + n
            total = conv[0, c].astype(F32) + conv[1, c].astype(F32)
            total = total + gains[n] * prod[c].astype(F32)
            pieces.append((values[n].astype(F32) * total).astype(BF16))
    gated = jnp.concatenate(pieces, axis=0)
    mixed = jnp.dot(weight[...], gated, preferred_element_type=F32)
    outs = keep.shape[0]
    for r in range(rows):
        cut = slice(r * block, (r + 1) * block)
        keep[:, cut] = mixed[r * outs : (r + 1) * outs].astype(BF16)
        send[:, cut] = mixed[(rows + r) * outs : (rows + r + 1) * outs].astype(BF16)


def gate_and_project(core, conv, prod, gate, gate_other, skip, skip_other, weight):
    _, channels, rows, block = conv.shape
    outs = weight.shape[0] // (2 * rows)
    return pl.pallas_call(
        gate_kernel,
        out_shape=[jax.ShapeDtypeStruct((outs, rows * block), BF16)] * 2,
        in_specs=[SMEM, VMEM, VMEM, VMEM, VMEM, SMEM, SMEM, VMEM],
        out_specs=[VMEM, VMEM],
        compiler_params=pltpu.CompilerParams(vmem_limit_bytes=16 * MIB),
        cost_estimate=SMALL,
    )(core, conv, prod, gate, gate_other, skip, skip_other, weight)


def local_channels(k_feature, v_feature, q_feature, spectrum, skip_gain, out_weight):
    channels, tokens = k_feature.shape
    block = spectrum.shape[3]
    ctx_count = lax.axis_size("ctx")
    members = ctx_count // 2
    rows_half = tokens // block // 2
    a_half = spectrum.shape[2] // 2
    ctx, tp = lax.axis_index("ctx"), lax.axis_index("tp")
    core = tp.astype(jnp.int32).reshape(1)
    member = (ctx % members).astype(jnp.int32).reshape(1)
    place = (ctx // members * 2 + tp).astype(jnp.int32).reshape(1)
    tables = {
        name: jnp.asarray(table)
        for name, table in constant_tables(block, members, rows_half, a_half).items()
    }
    halves = [list(range(members)), list(range(members, 2 * members))]
    spread = lambda x: lax.all_to_all(x, "ctx", 0, 0, axis_index_groups=halves, tiled=True)
    across = lambda x: lax.ppermute(
        x, "ctx", [(d, (d + members) % ctx_count) for d in range(ctx_count)]
    )
    swap = lambda x: lax.ppermute(x, "tp", [(0, 1), (1, 0)])

    def joined(own, sent):
        start = ((1 - tp) * channels,) + (0,) * (own.ndim - 1)
        return lax.dynamic_update_slice(own, swap(sent), start)

    own, sent, other_rows = as_rows(core, block, k_feature, v_feature, spectrum=spectrum)
    sent, q_feature = lax.optimization_barrier((sent, q_feature))
    product = joined(own, sent)
    gate, gate_sent = as_rows(core, block, q_feature)
    product, spectrum, other_rows, gate, gate_sent, skip_gain, out_weight = (
        lax.optimization_barrier(
            (product, spectrum, other_rows, gate, gate_sent, skip_gain, out_weight)
        )
    )
    came_rows = swap(other_rows)
    gate_other = swap(gate_sent)
    skip_other = swap(skip_gain)
    xa = spread(product)
    spec = arrange_spectrum(core, spectrum, came_rows, tables["order"])
    weight = projection(core, out_weight, rows_half)
    xa, spec, gate_other, skip_other, weight = lax.optimization_barrier(
        (xa, spec, gate_other, skip_other, weight)
    )
    xb = swap(xa)
    za = across(xa)
    spec = spread(spec)
    zb = swap(za)


    send, keep = transform(place, (xa, xb, za, zb), spec, tables)
    total = (keep + swap(send).astype(F32)).astype(BF16)
    conv = lax.all_to_all(total, "ctx", 0, 0, tiled=True).reshape(2, members, rows_half, block)
    kept, sent = gate_and_project(
        core, conv, product, gate, gate_other, skip_gain, skip_other, weight
    )
    came = swap(sent)
    low = jnp.where(tp == 0, kept, came)
    high = jnp.where(tp == 0, came, kept)
    return jnp.concatenate([low, high], axis=1)


def local(k_feature, v_feature, q_feature, spectrum, skip_gain, out_weight):
    channels, tokens = k_feature.shape
    block = spectrum.shape[3]
    ctx_count, tp_count = lax.axis_size("ctx"), lax.axis_size("tp")
    by_channels = (
        tp_count == 2
        and ctx_count == 2 * channels * tp_count
        and tokens * ctx_count * 2 == block * block
        and tokens % (32 * block) == 0
        and spectrum.shape[2] % 32 == 0
        and block % 512 == 0
        and out_weight.shape[1] % 16 == 0
    )
    plan = local_channels if by_channels else local_general
    return plan(k_feature, v_feature, q_feature, spectrum, skip_gain, out_weight)


def solution(mesh):
    placed = (
        P("tp", "ctx"),
        P("tp", "ctx"),
        P("tp", "ctx"),
        P(None, "tp", "ctx", None),
        P("tp"),
        P(),
    )
    return jax.shard_map(
        local, mesh=mesh, in_specs=placed, out_specs=P("tp", "ctx"), check_vma=False
    )
```

time: 99.3 us -> 78.3 us (0.79)
  waiting for transfers between devices: 30.8 us -> 22 us
  starting transfers between devices: 20.7 us -> 13.7 us
  local copies, waits for them, and re-layouts: 8.24 us -> 2.49 us
    all_to_all x3 -> x0, starting transfers between devices: 14.1 us -> none  [the longest x1 7.2 us: local_channels(): lax.all_to_all(total, 'ctx', 0, 0, tiled=True)]
    all_to_all x3 -> x0, waiting for transfers between devices: 14 us -> none  [the longest x1 13.4 us: local_channels(): lax.all_to_all(total, 'ctx', 0, 0, tiled=True)]
    all_to_all x1 -> x2, starting transfers between devices: 3.56 us -> 9.74 us  [local_channels(): lax.all_to_all(x, 'ctx', 0, 0, axis_index_groups=halves, tiled=True)]
    unnamed x20, local copies, waits for them, and re-layouts: 7.07 us -> 1.81 us
    ppermute x5 -> x8, waiting for transfers between devices: 2.87 us -> 5.16 us  [local_channels(): swap = lambda x: lax.ppermute(x, 'tp', [(0, 1), (1, 0)])]
    all_to_all x1 -> x2, waiting for transfers between devices: 1.02 us -> 2.97 us  [local_channels(): lax.all_to_all(x, 'ctx', 0, 0, axis_index_groups=halves, tiled=True)]
    ppermute x5 -> x8, starting transfers between devices: 0.08 us -> 1.27 us  [local_channels(): swap = lambda x: lax.ppermute(x, 'tp', [(0, 1), (1, 0)])]
    ppermute x2 -> x1, waiting for transfers between devices: 13 us -> 13.9 us  [local_channels(): lax.ppermute(x, 'ctx', [(d, (d + members) % ctx_count) for d in range(ctx...]
  transfers between devices with their start and end apart: 11 -> 11, of which waited for: 7 -> 6; matrix products, arithmetic and copies ran while one was open for 3% -> 0% of each run, Pallas kernels for 5% -> 7%
where the time goes in v1:
time: 78.3 us; the launch traced here: 77.8 us
  blocking collectives  22.5 us (29%)
  waiting for transfers between devices  22 us (28%)
  Pallas kernels  14.7 us (19%)
  starting transfers between devices  13.7 us (17%)
  local copies, waits for them, and re-layouts  2.49 us (3%)
  other arithmetic  2.25 us (3%)
    all_to_all x1, blocking collectives, local_channels(): lax.all_to_all(total, 'ctx', 0, 0, tiled=True)  22.5 us
    ppermute x1, waiting for transfers between devices, local_channels(): lax.ppermute(x, 'ctx', [(d, (d + members) % ctx_count) for d in range(ctx...  13.9 us
    all_to_all x2, starting transfers between devices, local_channels(): lax.all_to_all(x, 'ctx', 0, 0, axis_index_groups=halves, tiled=True)  9.74 us
    pallas_call x1, Pallas kernels, transform(): pl.pallas_call(transform_kernel, in_specs=[SMEM] + [ANY] * len(operands),...  6.44 us
    ppermute x8, waiting for transfers between devices, local_channels(): swap = lambda x: lax.ppermute(x, 'tp', [(0, 1), (1, 0)])  5.16 us
    pallas_call x2, Pallas kernels, as_rows(): pl.pallas_call(functools.partial(product_kernel, block, len(arrays)), out...  4.16 us
    all_to_all x2, waiting for transfers between devices, local_channels(): lax.all_to_all(x, 'ctx', 0, 0, axis_index_groups=halves, tiled=True)  2.97 us
    pallas_call x1, Pallas kernels, arrange_spectrum(): pl.pallas_call(spectrum_kernel, out_shape=jax.ShapeDtypeStruct((2 * chann...  2.91 us
  transfers between devices with their start and end apart: 11, of which 6 were waited for; matrix products, arithmetic and copies ran while one was open for 0% of the time, Pallas kernels for 7%

profile of v1, /device:TPU:0, one launch (start us, length us, event | category | flops | bytes accessed | tf_op | source)
XLA Modules:
  0.0 77.8 jit_solution(5261241299387898171)
XLA Ops:
  0.0 0.0 copy-start.3
  0.0 0.0 copy-start.2
  0.0 2.3 %shard_map.109 = (bf16[8,16,1024]{2,1,0:T(8,128)(2,1)}, bf16[4,16,1024]{2,1,0:T(8,128)(2,1)}, bf16[2,4,32,1024]{3,2,1,0:T(8,128)(2,1)}) custom-call(s32[1]{0:T(128)} %bitcast.core_ref, bf16[4,32768]{1,0:T(4,128)(2,1)} %refs_0_.1, bf16[4,32768]{1,0:T(4,128)(2,1)} %refs_1_.1, bf16[2,4,64,1024]{3,2,1,0:T(8,128)(2,1)} %in_ref), custom_call_target="tpu_custom_call" | custom-call | flops 1 | bytes 1 | tf_op jit(solution)/shard_map/pallas_call | solution.py:216
  2.3 0.5 collective-permute-start
  2.8 1.9 %shard_map.110 = (bf16[4,16,1024]{2,1,0:T(8,128)(2,1)}, bf16[4,16,1024]{2,1,0:T(8,128)(2,1)}) custom-call(s32[1]{0:T(128)} %bitcast.core_ref, bf16[4,32768]{1,0:T(4,128)(2,1)} %refs_0_.2), custom_call_target="tpu_custom_call" | custom-call | flops 1 | bytes 1 | tf_op jit(solution)/shard_map/pallas_call | solution.py:216
  4.7 0.0 collective-permute-done
  4.7 0.7 constant_dynamic-update-slice_fusion.prod
  5.4 0.1 collective-permute-start.1
  5.4 6.2 %all-to-all-start = ((bf16[8,16,1024]{2,1,0:T(8,128)(2,1)}), bf16[8,16,1024]{2,1,0:T(8,128)(2,1)S(1)}, u32[]{:S(2)}, u32[]{:S(2)}) async-start(bf16[8,16,1024]{2,1,0:T(8,128)(2,1)} %constant_dynamic-update-slice_fusion.prod), calls=%async_computation | async-start | bytes 524288 | tf_op jit(solution)/shard_map/all_to_all | solution.py:469
  11.6 0.0 collective-permute-start.2
  11.6 0.0 copy-done.2
  11.6 0.3 shard_map.112.weight
  11.9 0.0 copy-done.3
  11.9 0.6 collective-permute-start.3
  12.5 0.0 collective-permute-done.1.came_ref
  12.5 0.0 copy-start.6
  12.5 0.8 %copy-done.6 = bf16[2,4,32,1024]{3,2,1,0:T(8,128)(2,1)} copy-done((bf16[2,4,32,1024]{3,2,1,0:T(8,128)(2,1)}, bf16[2,4,32,1024]{3,2,1,0:T(8,128)(2,1)S(1)}, u32[]{:S(2)}) %copy-start.6) | copy-done | bytes 524312
  13.3 2.9 %shard_map.111 = bf16[8,2,32,1024]{3,2,1,0:T(8,128)(2,1)} custom-call(s32[1]{0:T(128)} %bitcast.core_ref, bf16[2,4,64,1024]{3,2,1,0:T(8,128)(2,1)} %in_ref, bf16[2,4,32,1024]{3,2,1,0:T(8,128)(2,1)} %copy-done.6, bf16[256,256]{1,0:T(8,128)(2,1)} %constant.45.clone.order_ref), custom_call_target="tpu_custom_call" | custom-call | flops 1 | bytes 1 | tf_op jit(solution)/shard_map/pallas_call | solution.py:263
  16.2 0.0 collective-permute-done.3.skip_other
  16.2 0.0 collective-permute-done.2.gate_other
  16.2 2.2 %all-to-all-done.refs_0_ = bf16[8,16,1024]{2,1,0:T(8,128)(2,1)S(1)} async-done(((bf16[8,16,1024]{2,1,0:T(8,128)(2,1)}), bf16[8,16,1024]{2,1,0:T(8,128)(2,1)S(1)}, u32[]{:S(2)}, u32[]{:S(2)}) %all-to-all-start) | async-done | bytes 262176 | tf_op jit(solution)/shard_map/all_to_all | solution.py:469
  18.4 0.0 copy-start.5
  18.4 3.6 %all-to-all-start.1 = ((bf16[8,2,32,1024]{3,2,1,0:T(8,128)(2,1)}), bf16[8,2,32,1024]{3,2,1,0:T(8,128)(2,1)S(1)}, u32[]{:S(2)}, u32[]{:S(2)}) async-start(bf16[8,2,32,1024]{3,2,1,0:T(8,128)(2,1)} %shard_map.111), calls=%async_computation.1 | async-start | bytes 2097152 | tf_op jit(solution)/shard_map/all_to_all | solution.py:469
  22.0 2.7 %collective-permute-start.5 = (bf16[8,16,1024]{2,1,0:T(8,128)(2,1)S(1)}, bf16[8,16,1024]{2,1,0:T(8,128)(2,1)S(1)}, u32[]{:S(2)}, u32[]{:S(2)}) collective-permute-start(bf16[8,16,1024]{2,1,0:T(8,128)(2,1)S(1)} %all-to-all-done.refs_0_), channel_id=1, source_target_pairs={{0,16},{2,18},{4,20},{6,22},{8,24},{10,26},{12,28},{14,30},{16,0},... | collective-permute-start | bytes 786440 | tf_op jit(solution)/shard_map/ppermute | solution.py:470
  24.6 0.0 collective-permute-start.4
  24.6 13.9 %collective-permute-done.5.refs_2_ = bf16[8,16,1024]{2,1,0:T(8,128)(2,1)S(1)} collective-permute-done((bf16[8,16,1024]{2,1,0:T(8,128)(2,1)S(1)}, bf16[8,16,1024]{2,1,0:T(8,128)(2,1)S(1)}, u32[]{:S(2)}, u32[]{:S(2)}) %collective-permute-start.5) | collective-permute-done | bytes 262176 | tf_op jit(solution)/shard_map/ppermute | solution.py:470
  38.6 0.0 collective-permute-start.6
  38.6 0.0 collective-permute-done.4.refs_1_
  38.6 1.5 %collective-permute-done.6.refs_3_ = bf16[8,16,1024]{2,1,0:T(8,128)(2,1)S(1)} collective-permute-done((bf16[8,16,1024]{2,1,0:T(8,128)(2,1)S(1)}, bf16[8,16,1024]{2,1,0:T(8,128)(2,1)S(1)}, u32[]{:S(2)}, u32[]{:S(2)}) %collective-permute-start.6) | collective-permute-done | bytes 262176 | tf_op jit(solution)/shard_map/ppermute | solution.py:473
  40.1 0.8 %all-to-all-done.1.refs_4_ = bf16[8,2,32,1024]{3,2,1,0:T(8,128)(2,1)S(1)} async-done(((bf16[8,2,32,1024]{3,2,1,0:T(8,128)(2,1)}), bf16[8,2,32,1024]{3,2,1,0:T(8,128)(2,1)S(1)}, u32[]{:S(2)}, u32[]{:S(2)}) %all-to-all-start.1) | async-done | bytes 1048608 | tf_op jit(solution)/shard_map/all_to_all | solution.py:469
  40.9 0.0 copy-done.5
  40.9 0.0 copy-done.7
  40.9 0.0 copy-done.8
  40.9 0.0 copy-done.9
  40.9 1.0 %copy-done.4 = bf16[8,2,32,1024]{3,2,1,0:T(8,128)(2,1)} copy-done((bf16[8,2,32,1024]{3,2,1,0:T(8,128)(2,1)}, bf16[8,2,32,1024]{3,2,1,0:T(8,128)(2,1)S(1)}, u32[]{:S(2)}) %copy-start.4) | copy-done | bytes 1048600
  41.9 6.4 %shard_map.113 = (bf16[16,16,1024]{2,1,0:T(8,128)(2,1)}, f32[16,16,1024]{2,1,0:T(8,128)}) custom-call(s32[1]{0:T(128)} %bitcast.1.place_ref, bf16[8,16,1024]{2,1,0:T(8,128)(2,1)} %copy-done.5, bf16[8,16,1024]{2,1,0:T(8,128)(2,1)} %copy-done.8, bf16[8,16,1024]{2,1,0:T(8,128)(2,1)} %copy-done.7, bf16[8,16,1024]{2,1,0:T(8,128)(2,1)} %copy-done.9, ...), custom_call_target="tpu_custom_call" | custom-call | flops 1 | bytes 1 | tf_op jit(solution)/shard_map/pallas_call | solution.py:400
  48.3 0.0 copy-start
  48.3 0.0 copy-start.1
  48.4 0.1 collective-permute-start.7
  48.4 2.1 %collective-permute-done.7 = bf16[16,16,1024]{2,1,0:T(8,128)(2,1)S(1)} collective-permute-done((bf16[16,16,1024]{2,1,0:T(8,128)(2,1)}, bf16[16,16,1024]{2,1,0:T(8,128)(2,1)S(1)}, u32[]{:S(2)}, u32[]{:S(2)}) %collective-permute-start.7) | collective-permute-done | bytes 524320 | tf_op jit(solution)/shard_map/ppermute | solution.py:473
  50.5 1.4 %add_convert_fusion = bf16[16,16,1024]{2,1,0:T(8,128)(2,1)S(1)} fusion(f32[16,16,1024]{2,1,0:T(8,128)} %get-tuple-element.43, bf16[16,16,1024]{2,1,0:T(8,128)(2,1)S(1)} %collective-permute-done.7), kind=kLoop, calls=%fused_computation | loop fusion | flops 786432 | bytes 2097152 | tf_op jit(solution)/shard_map/convert_element_type | solution.py:504
  51.9 22.5 %all_to_all.15 = bf16[16,16,1024]{2,1,0:T(8,128)(2,1)S(1)} all-to-all(bf16[16,16,1024]{2,1,0:T(8,128)(2,1)S(1)} %add_convert_fusion), channel_id=1, replica_groups=mesh['ctx'=16,'tp'=2] {'ctx'}, dimensions={0} | all-to-all | bytes 1048576 | tf_op jit(solution)/shard_map/all_to_all | solution.py:505
  74.5 0.0 copy-done
  74.5 0.0 copy-done.1
  74.5 0.9 %shard_map.114 = (bf16[8,16384]{1,0:T(8,128)(2,1)S(1)}, bf16[8,16384]{1,0:T(8,128)(2,1)S(1)}) custom-call(s32[1]{0:T(128)} %bitcast.core_ref, bf16[2,8,16,1024]{3,2,1,0:T(8,128)(2,1)S(1)} %bitcast.3, bf16[8,16,1024]{2,1,0:T(8,128)(2,1)S(1)} %copy-done, bf16[4,16,1024]{2,1,0:T(8,128)(2,1)S(1)} %copy-done.1, ...), custom_call_target="tpu_custom_call" | custom-call | flops 1 | bytes 1 | tf_op jit(solution)/shard_map/pallas_call | solution.py:443
  75.4 0.1 collective-permute-start.8
  75.4 1.5 %collective-permute-done.8 = bf16[8,16384]{1,0:T(8,128)(2,1)S(1)} collective-permute-done((bf16[8,16384]{1,0:T(8,128)(2,1)S(1)}, bf16[8,16384]{1,0:T(8,128)(2,1)S(1)}, u32[]{:S(2)}, u32[]{:S(2)}) %collective-permute-start.8) | collective-permute-done | bytes 262176 | tf_op jit(solution)/shard_map/ppermute | solution.py:473
  77.0 0.8 %pad_maximum_fusion = bf16[8,32768]{1,0:T(8,128)(2,1)} fusion(bf16[8,16384]{1,0:T(8,128)(2,1)S(1)} %get-tuple-element.52, bf16[8,16384]{1,0:T(8,128)(2,1)S(1)} %get-tuple-element.51), kind=kLoop, calls=%fused_computation.1 | loop fusion | flops 1048576 | bytes 1048576 | tf_op jit(solution)/shard_map/concatenate | solution.py:512
  (5 shorter events, 0.0 us)
Async XLA Ops:
  0.0 11.9 %copy-start.3 = (f32[4]{0:T(128)S(1)}, f32[4]{0:T(128)}, u32[]{:S(2)}) copy-start(f32[4]{0:T(128)} %skip) | copy-start | bytes 52
  0.0 11.6 %copy-start.2 = (bf16[8,16]{1,0:T(8,128)(2,1)S(1)}, bf16[8,16]{1,0:T(8,128)(2,1)}, u32[]{:S(2)}) copy-start(bf16[8,16]{1,0:T(8,128)(2,1)} %weight) | copy-start | bytes 772
  2.3 2.4 %collective-permute-start = (bf16[4,16,1024]{2,1,0:T(8,128)(2,1)}, bf16[4,16,1024]{2,1,0:T(8,128)(2,1)S(1)}, u32[]{:S(2)}, u32[]{:S(2)}) collective-permute-start(bf16[4,16,1024]{2,1,0:T(8,128)(2,1)} %get-tuple-element.30), channel_id=1, source_target_pairs={{0,1},{1,0},{2,3},{3,2},{4,5},{5,4},{6,7},{7,6},{8,9},{9,8},{10,11... | collective-permute-start | bytes 393224 | tf_op jit(solution)/shard_map/ppermute | solution.py:473
  5.4 7.1 %collective-permute-start.1 = (bf16[2,4,32,1024]{3,2,1,0:T(8,128)(2,1)}, bf16[2,4,32,1024]{3,2,1,0:T(8,128)(2,1)S(1)}, u32[]{:S(2)}, u32[]{:S(2)}) collective-permute-start(bf16[2,4,32,1024]{3,2,1,0:T(8,128)(2,1)} %get-tuple-element.37), channel_id=1, source_target_pairs={{0,1},{1,0},{2,3},{3,2},{4,5},{5,4},{6,7},{7,6},{8,9},{9,8},{10,11... | collective-permute-start | bytes 1572872 | tf_op jit(solution)/shard_map/ppermute | solution.py:473
  5.4 13.0 %all-to-all-start = ((bf16[8,16,1024]{2,1,0:T(8,128)(2,1)}), bf16[8,16,1024]{2,1,0:T(8,128)(2,1)S(1)}, u32[]{:S(2)}, u32[]{:S(2)}) async-start(bf16[8,16,1024]{2,1,0:T(8,128)(2,1)} %constant_dynamic-update-slice_fusion.prod), calls=%async_computation | async-start | bytes 524288 | tf_op jit(solution)/shard_map/all_to_all | solution.py:469
  11.6 4.6 %collective-permute-start.2 = (bf16[4,16,1024]{2,1,0:T(8,128)(2,1)}, bf16[4,16,1024]{2,1,0:T(8,128)(2,1)S(1)}, u32[]{:S(2)}, u32[]{:S(2)}) collective-permute-start(bf16[4,16,1024]{2,1,0:T(8,128)(2,1)} %get-tuple-element.38), channel_id=1, source_target_pairs={{0,1},{1,0},{2,3},{3,2},{4,5},{5,4},{6,7},{7,6},{8,9},{9,8},{10,11... | collective-permute-start | bytes 393224 | tf_op jit(solution)/shard_map/ppermute | solution.py:473
  11.9 4.3 %collective-permute-start.3 = (f32[4]{0:T(128)S(1)}, f32[4]{0:T(128)S(1)}, u32[]{:S(2)}, u32[]{:S(2)}) collective-permute-start(f32[4]{0:T(128)S(1)} %copy-done.3), channel_id=1, source_target_pairs={{0,1},{1,0},{2,3},{3,2},{4,5},{5,4},{6,7},{7,6},{8,9},{9,8},{10,11... | collective-permute-start | bytes 56 | tf_op jit(solution)/shard_map/ppermute | solution.py:473
  12.5 0.8 %copy-start.6 = (bf16[2,4,32,1024]{3,2,1,0:T(8,128)(2,1)}, bf16[2,4,32,1024]{3,2,1,0:T(8,128)(2,1)S(1)}, u32[]{:S(2)}) copy-start(bf16[2,4,32,1024]{3,2,1,0:T(8,128)(2,1)S(1)} %collective-permute-done.1.came_ref) | copy-start | bytes 1572868
  18.4 22.5 %copy-start.5 = (bf16[8,16,1024]{2,1,0:T(8,128)(2,1)}, bf16[8,16,1024]{2,1,0:T(8,128)(2,1)S(1)}, u32[]{:S(2)}) copy-start(bf16[8,16,1024]{2,1,0:T(8,128)(2,1)S(1)} %all-to-all-done.refs_0_) | copy-start | bytes 786436
  18.4 22.5 %all-to-all-start.1 = ((bf16[8,2,32,1024]{3,2,1,0:T(8,128)(2,1)}), bf16[8,2,32,1024]{3,2,1,0:T(8,128)(2,1)S(1)}, u32[]{:S(2)}, u32[]{:S(2)}) async-start(bf16[8,2,32,1024]{3,2,1,0:T(8,128)(2,1)} %shard_map.111), calls=%async_computation.1 | async-start | bytes 2097152 | tf_op jit(solution)/shard_map/all_to_all | solution.py:469
  22.0 16.6 %collective-permute-start.5 = (bf16[8,16,1024]{2,1,0:T(8,128)(2,1)S(1)}, bf16[8,16,1024]{2,1,0:T(8,128)(2,1)S(1)}, u32[]{:S(2)}, u32[]{:S(2)}) collective-permute-start(bf16[8,16,1024]{2,1,0:T(8,128)(2,1)S(1)} %all-to-all-done.refs_0_), channel_id=1, source_target_pairs={{0,16},{2,18},{4,20},{6,22},{8,24},{10,26},{12,28},{14,30},{16,0},... | collective-permute-start | bytes 786440 | tf_op jit(solution)/shard_map/ppermute | solution.py:470
  24.6 13.9 %collective-permute-start.4 = (bf16[8,16,1024]{2,1,0:T(8,128)(2,1)S(1)}, bf16[8,16,1024]{2,1,0:T(8,128)(2,1)S(1)}, u32[]{:S(2)}, u32[]{:S(2)}) collective-permute-start(bf16[8,16,1024]{2,1,0:T(8,128)(2,1)S(1)} %all-to-all-done.refs_0_), channel_id=1, source_target_pairs={{0,1},{1,0},{2,3},{3,2},{4,5},{5,4},{6,7},{7,6},{8,9},{9,8},{10,11... | collective-permute-start | bytes 786440 | tf_op jit(solution)/shard_map/ppermute | solution.py:473
  38.6 2.3 %copy-start.7 = (bf16[8,16,1024]{2,1,0:T(8,128)(2,1)}, bf16[8,16,1024]{2,1,0:T(8,128)(2,1)S(1)}, u32[]{:S(2)}) copy-start(bf16[8,16,1024]{2,1,0:T(8,128)(2,1)S(1)} %collective-permute-done.5.refs_2_) | copy-start | bytes 786436
  38.6 1.5 %collective-permute-start.6 = (bf16[8,16,1024]{2,1,0:T(8,128)(2,1)S(1)}, bf16[8,16,1024]{2,1,0:T(8,128)(2,1)S(1)}, u32[]{:S(2)}, u32[]{:S(2)}) collective-permute-start(bf16[8,16,1024]{2,1,0:T(8,128)(2,1)S(1)} %collective-permute-done.5.refs_2_), channel_id=1, source_target_pairs={{0,1},{1,0},{2,3},{3,2},{4,5},{5,4},{6,7},{7,6},{8,9},{9,8},{10,11... | collective-permute-start | bytes 786440 | tf_op jit(solution)/shard_map/ppermute | solution.py:473
  38.6 2.3 %copy-start.8 = (bf16[8,16,1024]{2,1,0:T(8,128)(2,1)}, bf16[8,16,1024]{2,1,0:T(8,128)(2,1)S(1)}, u32[]{:S(2)}) copy-start(bf16[8,16,1024]{2,1,0:T(8,128)(2,1)S(1)} %collective-permute-done.4.refs_1_) | copy-start | bytes 786436
  40.1 0.8 %copy-start.9 = (bf16[8,16,1024]{2,1,0:T(8,128)(2,1)}, bf16[8,16,1024]{2,1,0:T(8,128)(2,1)S(1)}, u32[]{:S(2)}) copy-start(bf16[8,16,1024]{2,1,0:T(8,128)(2,1)S(1)} %collective-permute-done.6.refs_3_) | copy-start | bytes 786436
  40.9 1.0 %copy-start.4 = (bf16[8,2,32,1024]{3,2,1,0:T(8,128)(2,1)}, bf16[8,2,32,1024]{3,2,1,0:T(8,128)(2,1)S(1)}, u32[]{:S(2)}) copy-start(bf16[8,2,32,1024]{3,2,1,0:T(8,128)(2,1)S(1)} %all-to-all-done.1.refs_4_) | copy-start | bytes 3145732
  48.3 26.1 %copy-start = (bf16[8,16,1024]{2,1,0:T(8,128)(2,1)S(1)}, bf16[8,16,1024]{2,1,0:T(8,128)(2,1)}, u32[]{:S(2)}) copy-start(bf16[8,16,1024]{2,1,0:T(8,128)(2,1)} %constant_dynamic-update-slice_fusion.prod) | copy-start | bytes 786436
  48.3 26.1 %copy-start.1 = (bf16[4,16,1024]{2,1,0:T(8,128)(2,1)S(1)}, bf16[4,16,1024]{2,1,0:T(8,128)(2,1)}, u32[]{:S(2)}) copy-start(bf16[4,16,1024]{2,1,0:T(8,128)(2,1)} %get-tuple-element.45.gate) | copy-start | bytes 393220
  48.4 2.2 %collective-permute-start.7 = (bf16[16,16,1024]{2,1,0:T(8,128)(2,1)}, bf16[16,16,1024]{2,1,0:T(8,128)(2,1)S(1)}, u32[]{:S(2)}, u32[]{:S(2)}) collective-permute-start(bf16[16,16,1024]{2,1,0:T(8,128)(2,1)} %get-tuple-element.44), channel_id=1, source_target_pairs={{0,1},{1,0},{2,3},{3,2},{4,5},{5,4},{6,7},{7,6},{8,9},{9,8},{10,11... | collective-permute-start | bytes 1572872 | tf_op jit(solution)/shard_map/ppermute | solution.py:473
  75.4 1.6 %collective-permute-start.8 = (bf16[8,16384]{1,0:T(8,128)(2,1)S(1)}, bf16[8,16384]{1,0:T(8,128)(2,1)S(1)}, u32[]{:S(2)}, u32[]{:S(2)}) collective-permute-start(bf16[8,16384]{1,0:T(8,128)(2,1)S(1)} %get-tuple-element.50), channel_id=1, source_target_pairs={{0,1},{1,0},{2,3},{3,2},{4,5},{5,4},{6,7},{7,6},{8,9},{9,8},{10,11... | collective-permute-start | bytes 786440 | tf_op jit(solution)/shard_map/ppermute | solution.py:473

commit v2 on v1

--- a/solution.py
+++ b/solution.py
@@ -15,6 +15,7 @@
 VMEM = pl.BlockSpec(memory_space=pltpu.VMEM)
 SMEM = pl.BlockSpec(memory_space=pltpu.SMEM)
 ANY = pl.BlockSpec(memory_space=pltpu.HBM)
+ANYWHERE = pl.BlockSpec(memory_space=pl.ANY)
 MIB = 1 << 20
 SMALL = pl.CostEstimate(flops=1, bytes_accessed=1, transcendentals=0)
 
@@ -154,11 +155,17 @@
     b = np.arange(quarter)
     order[b, (b % 4) * (quarter // 4) + b // 4] = 1.0
     narrow = lambda x: np.asarray(x, np.float32).astype(ml_dtypes.bfloat16)
+    rest = np.stack([coarses, fines], 1).astype(np.float32)
+    turns = []
+    for _ in range(3):
+        turns.append(narrow(rest))
+        rest = rest - turns[-1].astype(np.float32)
+    turns = np.stack(turns + [np.zeros_like(turns[0])], 1).transpose(0, 2, 4, 1, 3, 5)
+    turns = turns.reshape(4, 2 * turns.shape[2], 2, 2 * quarter).transpose(0, 2, 1, 3)
+    square = (-1, 2 * quarter, 2 * quarter)
+    entries = [np.stack(firsts), np.stack(lasts), np.stack(inner).reshape(square)]
     return dict(
-        first=narrow(np.stack(firsts)),
-        last=narrow(np.stack(lasts)),
-        turns=np.stack([coarses, fines], 1).astype(np.float32),
-        inner=narrow(np.stack(inner)),
+        transform=np.concatenate([narrow(x) for x in entries] + [turns.reshape(square)]),
         order=narrow(order),
     )
 
@@ -327,16 +334,31 @@
     return with_cosine[:rows], with_cosine[rows:], with_sine[:rows], with_sine[rows:]
 
 
+def full_turns(turns, rows):
+    def whole(kind, which):
+        cut = slice(kind * rows, (kind + 1) * rows)
+        part = lambda n: turns[n // 2, cut, pl.ds((2 * (n % 2) + which) * 128, 128)].astype(F32)
+        return part(0) + part(1) + part(2)
+
+    return (whole(0, 0), whole(0, 1)), (whole(1, 0), whole(1, 1))
+
+
+def pair_of(inner, rho, way):
+    quarter = inner.shape[-1] // 2
+    four = inner[rho].reshape(4, quarter, quarter)
+    return four[2 * way], four[2 * way + 1]
+
+
 def transform_kernel(place_ref, *refs):
-    ins, (send, keep, signal, spec, *tables, twist, sem) = refs[:9], refs[-10:]
-    first, turns, inner, last = tables
-    pieces, spec_in, (first_in, turns_in, inner_in, last_in) = ins[:4], ins[4], ins[5:9]
+    ins, (send, keep, signal, spec, first, last, inner, turns, twist, sem) = refs[:-10], refs[-10:]
+    *pieces, spec_in, table = ins
     place = place_ref[0]
     count = pieces[0].shape[0]
-    moves = [(first_in.at[place], first)]
+    size = turns.shape[0]
+    moves = [(table.at[place], first)]
     moves += [(ref, signal.at[pl.ds(n * count, count)]) for n, ref in enumerate(pieces)]
-    moves += [(turns_in.at[place], turns), (inner_in, inner), (spec_in, spec)]
-    moves += [(last_in.at[place], last)]
+    moves += [(table.at[pl.ds(12 + size * place, size)], turns)]
+    moves += [(table.at[pl.ds(8, 4)], inner), (spec_in, spec), (table.at[4 + place], last)]
     copies = [pltpu.make_async_copy(*move, sem.at[n]) for n, move in enumerate(moves)]
     for copy in copies:
         copy.start()
@@ -346,16 +368,16 @@
     quarter = block // 4
     lines = signal[...].reshape(-1, block)
     a_rows = first.shape[0] // 2
+    coarse, fine = full_turns(turns, a_rows)
     turned = []
     for q in range(4):
         cut = slice(q * quarter, (q + 1) * quarter)
         both = jnp.dot(first[...], lines[:, cut], preferred_element_type=F32)
         for h in range(q * quarter // 128, (q + 1) * quarter // 128):
             lanes = slice(128 * h, 128 * (h + 1))
-            uc, us = turns[0, 0, :, h : h + 1], turns[0, 1, :, h : h + 1]
-            vc, vs = turns[1, 0], turns[1, 1]
-            twist[0, :, lanes] = uc * vc - us * vs
-            twist[1, :, lanes] = us * vc + uc * vs
+            uc, us = coarse[0][:, h : h + 1], coarse[1][:, h : h + 1]
+            twist[0, :, lanes] = uc * fine[0] - us * fine[1]
+            twist[1, :, lanes] = us * fine[0] + uc * fine[1]
         real, imag = both[:a_rows], both[a_rows:]
         cosine, sine = twist[0, :, cut], twist[1, :, cut]
         turned.append((real * cosine + imag * sine, imag * cosine - real * sine))
@@ -364,13 +386,13 @@
         copy.wait()
     backs = []
     for rho in range(4):
-        rc, ic, rs, si = turn(mixes[rho], inner[rho, 0], inner[rho, 1])
+        rc, ic, rs, si = turn(mixes[rho], *pair_of(inner, rho, 0))
         zr, zi = rc + si, ic - rs
         cut = slice(rho * quarter, (rho + 1) * quarter)
         gr = spec[:, 0, :, cut].reshape(-1, quarter).astype(F32)
         gi = spec[:, 1, :, cut].reshape(-1, quarter).astype(F32)
         shaped = (zr * gr - zi * gi, zr * gi + zi * gr)
-        rc, ic, rs, si = turn(shaped, inner[rho, 2], inner[rho, 3])
+        rc, ic, rs, si = turn(shaped, *pair_of(inner, rho, 1))
         backs.append((rc - si, ic + rs))
     mixes = butterflies(backs, 1)
     scale = 1.0 / (block * block)
@@ -388,33 +410,32 @@
         )
         out = jnp.dot(last[...], pair, preferred_element_type=F32) * scale
         send[:, :, cut] = out[:half].astype(BF16).reshape(send.shape[0], send.shape[1], quarter)
-        keep[:, :, cut] = out[half:].reshape(keep.shape[0], keep.shape[1], quarter)
-
-
-def transform(place, pieces, spec, tables):
+        keep[:, :, cut] = out[half:].astype(BF16).reshape(keep.shape[0], keep.shape[1], quarter)
+
+
+def transform(place, pieces, spec, table):
     members, rows_half, block = pieces[0].shape
-    held = [tables[n] for n in ("first", "turns", "inner", "last")]
-    first, turns, inner, last = held
+    a_rows = spec.shape[0] * spec.shape[2]
     out = (2 * members, rows_half, block)
-    operands = [*pieces, spec, *held]
+    square = table.shape[1:]
     return pl.pallas_call(
         transform_kernel,
-        in_specs=[SMEM] + [ANY] * len(operands),
+        in_specs=[SMEM] + [ANYWHERE] * (len(pieces) + 1) + [ANY],
         out_specs=[VMEM, VMEM],
-        out_shape=[jax.ShapeDtypeStruct(out, BF16), jax.ShapeDtypeStruct(out, F32)],
+        out_shape=[jax.ShapeDtypeStruct(out, BF16)] * 2,
         scratch_shapes=[
             pltpu.VMEM((4 * members, rows_half, block), BF16),
             pltpu.VMEM(spec.shape, BF16),
-            pltpu.VMEM(first.shape[1:], BF16),
-            pltpu.VMEM(turns.shape[1:], F32),
-            pltpu.VMEM(inner.shape, BF16),
-            pltpu.VMEM(last.shape[1:], BF16),
-            pltpu.VMEM((2, turns.shape[3], block), F32),
-            pltpu.SemaphoreType.DMA((9,)),
+            pltpu.VMEM(square, BF16),
+            pltpu.VMEM(square, BF16),
+            pltpu.VMEM((4,) + square, BF16),
+            pltpu.VMEM(((table.shape[0] - 12) // 4,) + square, BF16),
+            pltpu.VMEM((2, a_rows, block), F32),
+            pltpu.SemaphoreType.DMA((len(pieces) + 5,)),
         ],
-        compiler_params=pltpu.CompilerParams(vmem_limit_bytes=60 * MIB),
+        compiler_params=pltpu.CompilerParams(vmem_limit_bytes=48 * MIB),
         cost_estimate=SMALL,
-    )(place, *operands)
+    )(place, *pieces, spec, table)
 
 
 def gate_kernel(core_ref, conv, prod, gate, gate_other, skip, skip_other, weight, keep, send):
@@ -500,8 +521,8 @@
     zb = swap(za)
 
 
-    send, keep = transform(place, (xa, xb, za, zb), spec, tables)
-    total = (keep + swap(send).astype(F32)).astype(BF16)
+    send, keep = transform(place, (xa, xb, za, zb), spec, tables["transform"])
+    total = (keep.astype(F32) + swap(send).astype(F32)).astype(BF16)
     conv = lax.all_to_all(total, "ctx", 0, 0, tiled=True).reshape(2, members, rows_half, block)
     kept, sent = gate_and_project(
         core, conv, product, gate, gate_other, skip_gain, skip_other, weight

time: 78.3 us -> 75.2 us (0.960)
  Pallas kernels: 14.7 us -> 13.5 us
  other arithmetic: 2.25 us -> 1.06 us
    convert_element_type x1, other arithmetic: 1.38 us -> 0.19 us  [local_channels(): total = (keep.astype(F32) + swap(send).astype(F32)).astype(BF16)]
    pallas_call x1, Pallas kernels: 6.44 us -> 5.35 us  [transform(): pl.pallas_call(transform_kernel, in_specs=[SMEM] + [ANYWHERE] * (len(piec...]
    unnamed x20 -> x10, local copies, waits for them, and re-layouts: 1.81 us -> 1.48 us
where the time goes in v2:
time: 75.2 us; the launch traced here: 74.8 us
  blocking collectives  22.5 us (30%)
  waiting for transfers between devices  21.8 us (29%)
  starting transfers between devices  13.6 us (18%)
  Pallas kernels  13.5 us (18%)
  local copies, waits for them, and re-layouts  2.15 us (3%)
  other arithmetic  1.06 us (1%)
    all_to_all x1, blocking collectives, local_channels(): lax.all_to_all(total, 'ctx', 0, 0, tiled=True)  22.5 us
    ppermute x1, waiting for transfers between devices, local_channels(): lax.ppermute(x, 'ctx', [(d, (d + members) % ctx_count) for d in range(ctx...  14.4 us
    all_to_all x2, starting transfers between devices, local_channels(): lax.all_to_all(x, 'ctx', 0, 0, axis_index_groups=halves, tiled=True)  9.74 us
    pallas_call x1, Pallas kernels, transform(): pl.pallas_call(transform_kernel, in_specs=[SMEM] + [ANYWHERE] * (len(piec...  5.35 us
    ppermute x8, waiting for transfers between devices, local_channels(): swap = lambda x: lax.ppermute(x, 'tp', [(0, 1), (1, 0)])  4.96 us
    pallas_call x2, Pallas kernels, as_rows(): pl.pallas_call(functools.partial(product_kernel, block, len(arrays)), out...  4.12 us
    pallas_call x1, Pallas kernels, arrange_spectrum(): pl.pallas_call(spectrum_kernel, out_shape=jax.ShapeDtypeStruct((2 * chann...  2.9 us
    ppermute x1, starting transfers between devices, local_channels(): lax.ppermute(x, 'ctx', [(d, (d + members) % ctx_count) for d in range(ctx...  2.65 us
  transfers between devices with their start and end apart: 11, of which 6 were waited for; matrix products, arithmetic and copies ran while one was open for 0% of the time, Pallas kernels for 7%

profile of v2, /device:TPU:0, one launch (start us, length us, event | category | flops | bytes accessed | tf_op | source)
XLA Modules:
  0.0 74.8 jit_solution(11715653831488694405)
XLA Ops:
  0.0 2.3 %shard_map.82 = (bf16[8,16,1024]{2,1,0:T(8,128)(2,1)}, bf16[4,16,1024]{2,1,0:T(8,128)(2,1)}, bf16[2,4,32,1024]{3,2,1,0:T(8,128)(2,1)}) custom-call(s32[1]{0:T(128)} %bitcast.core_ref, bf16[4,32768]{1,0:T(4,128)(2,1)} %refs_0_.1, bf16[4,32768]{1,0:T(4,128)(2,1)} %refs_1_.1, bf16[2,4,64,1024]{3,2,1,0:T(8,128)(2,1)} %in_ref), custom_call_target="tpu_custom_call" | custom-call | flops 1 | bytes 1 | tf_op jit(solution)/shard_map/pallas_call | solution.py:223
  2.3 0.5 collective-permute-start
  2.8 1.9 %shard_map.83 = (bf16[4,16,1024]{2,1,0:T(8,128)(2,1)}, bf16[4,16,1024]{2,1,0:T(8,128)(2,1)}) custom-call(s32[1]{0:T(128)} %bitcast.core_ref, bf16[4,32768]{1,0:T(4,128)(2,1)} %refs_0_.2), custom_call_target="tpu_custom_call" | custom-call | flops 1 | bytes 1 | tf_op jit(solution)/shard_map/pallas_call | solution.py:223
  4.7 0.0 copy-start.1
  4.7 0.0 copy-start.3
  4.7 0.0 collective-permute-done
  4.7 0.7 constant_dynamic-update-slice_fusion.prod
  5.4 0.0 copy-start
  5.4 0.1 collective-permute-start.1
  5.4 6.2 %all-to-all-start = ((bf16[8,16,1024]{2,1,0:T(8,128)(2,1)}), bf16[8,16,1024]{2,1,0:T(8,128)(2,1)S(1)}, u32[]{:S(2)}, u32[]{:S(2)}) async-start(bf16[8,16,1024]{2,1,0:T(8,128)(2,1)} %constant_dynamic-update-slice_fusion.prod), calls=%async_computation | async-start | bytes 524288 | tf_op jit(solution)/shard_map/all_to_all | solution.py:490
  11.6 0.0 collective-permute-start.2
  11.6 0.5 collective-permute-start.3
  12.1 0.0 copy-start.2
  12.1 0.7 copy-done.2
  12.8 0.3 shard_map.85.weight
  13.1 0.0 collective-permute-done.1.came_ref
  13.1 0.0 copy-start.4
  13.1 0.8 %copy-done.4 = bf16[2,4,32,1024]{3,2,1,0:T(8,128)(2,1)} copy-done((bf16[2,4,32,1024]{3,2,1,0:T(8,128)(2,1)}, bf16[2,4,32,1024]{3,2,1,0:T(8,128)(2,1)S(1)}, u32[]{:S(2)}) %copy-start.4) | copy-done | bytes 524312
  13.9 2.9 %shard_map.84 = bf16[8,2,32,1024]{3,2,1,0:T(8,128)(2,1)} custom-call(s32[1]{0:T(128)} %bitcast.core_ref, bf16[2,4,64,1024]{3,2,1,0:T(8,128)(2,1)} %in_ref, bf16[2,4,32,1024]{3,2,1,0:T(8,128)(2,1)} %copy-done.4, bf16[256,256]{1,0:T(8,128)(2,1)} %constant.36.clone.order_ref), custom_call_target="tpu_custom_call" | custom-call | flops 1 | bytes 1 | tf_op jit(solution)/shard_map/pallas_call | solution.py:270
  16.8 0.0 collective-permute-done.3.skip_other
  16.8 0.0 collective-permute-done.2.gate_other
  16.8 1.7 %all-to-all-done.refs_0_ = bf16[8,16,1024]{2,1,0:T(8,128)(2,1)S(1)} async-done(((bf16[8,16,1024]{2,1,0:T(8,128)(2,1)}), bf16[8,16,1024]{2,1,0:T(8,128)(2,1)S(1)}, u32[]{:S(2)}, u32[]{:S(2)}) %all-to-all-start) | async-done | bytes 262176 | tf_op jit(solution)/shard_map/all_to_all | solution.py:490
  18.5 3.6 %all-to-all-start.1 = ((bf16[8,2,32,1024]{3,2,1,0:T(8,128)(2,1)}), bf16[8,2,32,1024]{3,2,1,0:T(8,128)(2,1)S(1)}, u32[]{:S(2)}, u32[]{:S(2)}) async-start(bf16[8,2,32,1024]{3,2,1,0:T(8,128)(2,1)} %shard_map.84), calls=%async_computation.1 | async-start | bytes 2097152 | tf_op jit(solution)/shard_map/all_to_all | solution.py:490
  22.1 2.7 %collective-permute-start.5 = (bf16[8,16,1024]{2,1,0:T(8,128)(2,1)S(1)}, bf16[8,16,1024]{2,1,0:T(8,128)(2,1)S(1)}, u32[]{:S(2)}, u32[]{:S(2)}) collective-permute-start(bf16[8,16,1024]{2,1,0:T(8,128)(2,1)S(1)} %all-to-all-done.refs_0_), channel_id=1, source_target_pairs={{0,16},{2,18},{4,20},{6,22},{8,24},{10,26},{12,28},{14,30},{16,0},... | collective-permute-start | bytes 786440 | tf_op jit(solution)/shard_map/ppermute | solution.py:491
  24.7 0.0 collective-permute-start.4
  24.7 14.4 %collective-permute-done.5.refs_2_ = bf16[8,16,1024]{2,1,0:T(8,128)(2,1)S(1)} collective-permute-done((bf16[8,16,1024]{2,1,0:T(8,128)(2,1)S(1)}, bf16[8,16,1024]{2,1,0:T(8,128)(2,1)S(1)}, u32[]{:S(2)}, u32[]{:S(2)}) %collective-permute-start.5) | collective-permute-done | bytes 262176 | tf_op jit(solution)/shard_map/ppermute | solution.py:491
  39.1 0.0 collective-permute-start.6
  39.1 0.0 collective-permute-done.4.refs_1_
  39.1 1.5 %collective-permute-done.6.refs_3_ = bf16[8,16,1024]{2,1,0:T(8,128)(2,1)S(1)} collective-permute-done((bf16[8,16,1024]{2,1,0:T(8,128)(2,1)S(1)}, bf16[8,16,1024]{2,1,0:T(8,128)(2,1)S(1)}, u32[]{:S(2)}, u32[]{:S(2)}) %collective-permute-start.6) | collective-permute-done | bytes 262176 | tf_op jit(solution)/shard_map/ppermute | solution.py:494
  40.7 0.8 %all-to-all-done.1.refs_4_ = bf16[8,2,32,1024]{3,2,1,0:T(8,128)(2,1)S(1)} async-done(((bf16[8,2,32,1024]{3,2,1,0:T(8,128)(2,1)}), bf16[8,2,32,1024]{3,2,1,0:T(8,128)(2,1)S(1)}, u32[]{:S(2)}, u32[]{:S(2)}) %all-to-all-start.1) | async-done | bytes 1048608 | tf_op jit(solution)/shard_map/all_to_all | solution.py:490
  41.4 5.3 %shard_map.86 = (bf16[16,16,1024]{2,1,0:T(8,128)(2,1)S(1)}, bf16[16,16,1024]{2,1,0:T(8,128)(2,1)S(1)}) custom-call(s32[1]{0:T(128)} %bitcast.1.place_ref, bf16[8,16,1024]{2,1,0:T(8,128)(2,1)S(1)} %all-to-all-done.refs_0_, bf16[8,16,1024]{2,1,0:T(8,128)(2,1)S(1)} %collective-permute-done.4.refs_1_, bf16[8,16,1024]{2,1,0:T(8,128)(2,1)S(1)} %collective-permute-done.5.refs_2_, ...), custom_call_target="tpu_custom_call" | custom-call | flops 1 | bytes 1 | tf_op jit(solution)/shard_map/pallas_call | solution.py:421
  46.8 0.1 collective-permute-start.7
  46.9 1.9 %collective-permute-done.7 = bf16[16,16,1024]{2,1,0:T(8,128)(2,1)S(1)} collective-permute-done((bf16[16,16,1024]{2,1,0:T(8,128)(2,1)S(1)}, bf16[16,16,1024]{2,1,0:T(8,128)(2,1)S(1)}, u32[]{:S(2)}, u32[]{:S(2)}) %collective-permute-start.7) | collective-permute-done | bytes 524320 | tf_op jit(solution)/shard_map/ppermute | solution.py:494
  48.8 0.2 add_convert_fusion
  49.0 22.5 %all_to_all.15 = bf16[16,16,1024]{2,1,0:T(8,128)(2,1)S(1)} all-to-all(bf16[16,16,1024]{2,1,0:T(8,128)(2,1)S(1)} %add_convert_fusion), channel_id=1, replica_groups=mesh['ctx'=16,'tp'=2] {'ctx'}, dimensions={0} | all-to-all | bytes 1048576 | tf_op jit(solution)/shard_map/all_to_all | solution.py:526
  71.4 0.0 copy-done.1
  71.4 0.0 copy-done.3
  71.4 0.0 copy-done
  71.4 0.9 %shard_map.87 = (bf16[8,16384]{1,0:T(8,128)(2,1)S(1)}, bf16[8,16384]{1,0:T(8,128)(2,1)S(1)}) custom-call(s32[1]{0:T(128)} %bitcast.core_ref, bf16[2,8,16,1024]{3,2,1,0:T(8,128)(2,1)S(1)} %bitcast.3, bf16[8,16,1024]{2,1,0:T(8,128)(2,1)S(1)} %copy-done, bf16[4,16,1024]{2,1,0:T(8,128)(2,1)S(1)} %copy-done.1, ...), custom_call_target="tpu_custom_call" | custom-call | flops 1 | bytes 1 | tf_op jit(solution)/shard_map/pallas_call | solution.py:464
  72.3 0.1 collective-permute-start.8
  72.4 1.5 %collective-permute-done.8 = bf16[8,16384]{1,0:T(8,128)(2,1)S(1)} collective-permute-done((bf16[8,16384]{1,0:T(8,128)(2,1)S(1)}, bf16[8,16384]{1,0:T(8,128)(2,1)S(1)}, u32[]{:S(2)}, u32[]{:S(2)}) %collective-permute-start.8) | collective-permute-done | bytes 262176 | tf_op jit(solution)/shard_map/ppermute | solution.py:494
  74.0 0.8 %pad_maximum_fusion = bf16[8,32768]{1,0:T(8,128)(2,1)} fusion(bf16[8,16384]{1,0:T(8,128)(2,1)S(1)} %get-tuple-element.52, bf16[8,16384]{1,0:T(8,128)(2,1)S(1)} %get-tuple-element.51), kind=kLoop, calls=%fused_computation.1 | loop fusion | flops 1048576 | bytes 1048576 | tf_op jit(solution)/shard_map/concatenate | solution.py:533
  (1 shorter events, 0.0 us)
Async XLA Ops:
  2.3 2.4 %collective-permute-start = (bf16[4,16,1024]{2,1,0:T(8,128)(2,1)}, bf16[4,16,1024]{2,1,0:T(8,128)(2,1)S(1)}, u32[]{:S(2)}, u32[]{:S(2)}) collective-permute-start(bf16[4,16,1024]{2,1,0:T(8,128)(2,1)} %get-tuple-element.30), channel_id=1, source_target_pairs={{0,1},{1,0},{2,3},{3,2},{4,5},{5,4},{6,7},{7,6},{8,9},{9,8},{10,11... | collective-permute-start | bytes 393224 | tf_op jit(solution)/shard_map/ppermute | solution.py:494
  4.7 66.8 %copy-start.1 = (bf16[4,16,1024]{2,1,0:T(8,128)(2,1)S(1)}, bf16[4,16,1024]{2,1,0:T(8,128)(2,1)}, u32[]{:S(2)}) copy-start(bf16[4,16,1024]{2,1,0:T(8,128)(2,1)} %get-tuple-element.45.gate) | copy-start | bytes 393220
  4.7 66.7 %copy-start.3 = (f32[4]{0:T(128)S(1)}, f32[4]{0:T(128)}, u32[]{:S(2)}) copy-start(f32[4]{0:T(128)} %skip) | copy-start | bytes 52
  5.4 66.1 %copy-start = (bf16[8,16,1024]{2,1,0:T(8,128)(2,1)S(1)}, bf16[8,16,1024]{2,1,0:T(8,128)(2,1)}, u32[]{:S(2)}) copy-start(bf16[8,16,1024]{2,1,0:T(8,128)(2,1)} %constant_dynamic-update-slice_fusion.prod) | copy-start | bytes 786436
  5.4 7.7 %collective-permute-start.1 = (bf16[2,4,32,1024]{3,2,1,0:T(8,128)(2,1)}, bf16[2,4,32,1024]{3,2,1,0:T(8,128)(2,1)S(1)}, u32[]{:S(2)}, u32[]{:S(2)}) collective-permute-start(bf16[2,4,32,1024]{3,2,1,0:T(8,128)(2,1)} %get-tuple-element.37), channel_id=1, source_target_pairs={{0,1},{1,0},{2,3},{3,2},{4,5},{5,4},{6,7},{7,6},{8,9},{9,8},{10,11... | collective-permute-start | bytes 1572872 | tf_op jit(solution)/shard_map/ppermute | solution.py:494
  5.4 13.1 %all-to-all-start = ((bf16[8,16,1024]{2,1,0:T(8,128)(2,1)}), bf16[8,16,1024]{2,1,0:T(8,128)(2,1)S(1)}, u32[]{:S(2)}, u32[]{:S(2)}) async-start(bf16[8,16,1024]{2,1,0:T(8,128)(2,1)} %constant_dynamic-update-slice_fusion.prod), calls=%async_computation | async-start | bytes 524288 | tf_op jit(solution)/shard_map/all_to_all | solution.py:490
  11.6 5.2 %collective-permute-start.2 = (bf16[4,16,1024]{2,1,0:T(8,128)(2,1)}, bf16[4,16,1024]{2,1,0:T(8,128)(2,1)S(1)}, u32[]{:S(2)}, u32[]{:S(2)}) collective-permute-start(bf16[4,16,1024]{2,1,0:T(8,128)(2,1)} %get-tuple-element.38), channel_id=1, source_target_pairs={{0,1},{1,0},{2,3},{3,2},{4,5},{5,4},{6,7},{7,6},{8,9},{9,8},{10,11... | collective-permute-start | bytes 393224 | tf_op jit(solution)/shard_map/ppermute | solution.py:494
  11.6 5.2 %collective-permute-start.3 = (f32[4]{0:T(128)}, f32[4]{0:T(128)S(1)}, u32[]{:S(2)}, u32[]{:S(2)}) collective-permute-start(f32[4]{0:T(128)} %skip), channel_id=1, source_target_pairs={{0,1},{1,0},{2,3},{3,2},{4,5},{5,4},{6,7},{7,6},{8,9},{9,8},{10,11... | collective-permute-start | bytes 56 | tf_op jit(solution)/shard_map/ppermute | solution.py:494
  12.1 0.7 copy-start.2
  13.1 0.8 %copy-start.4 = (bf16[2,4,32,1024]{3,2,1,0:T(8,128)(2,1)}, bf16[2,4,32,1024]{3,2,1,0:T(8,128)(2,1)S(1)}, u32[]{:S(2)}) copy-start(bf16[2,4,32,1024]{3,2,1,0:T(8,128)(2,1)S(1)} %collective-permute-done.1.came_ref) | copy-start | bytes 1572868
  18.5 22.9 %all-to-all-start.1 = ((bf16[8,2,32,1024]{3,2,1,0:T(8,128)(2,1)}), bf16[8,2,32,1024]{3,2,1,0:T(8,128)(2,1)S(1)}, u32[]{:S(2)}, u32[]{:S(2)}) async-start(bf16[8,2,32,1024]{3,2,1,0:T(8,128)(2,1)} %shard_map.84), calls=%async_computation.1 | async-start | bytes 2097152 | tf_op jit(solution)/shard_map/all_to_all | solution.py:490
  22.1 17.0 %collective-permute-start.5 = (bf16[8,16,1024]{2,1,0:T(8,128)(2,1)S(1)}, bf16[8,16,1024]{2,1,0:T(8,128)(2,1)S(1)}, u32[]{:S(2)}, u32[]{:S(2)}) collective-permute-start(bf16[8,16,1024]{2,1,0:T(8,128)(2,1)S(1)} %all-to-all-done.refs_0_), channel_id=1, source_target_pairs={{0,16},{2,18},{4,20},{6,22},{8,24},{10,26},{12,28},{14,30},{16,0},... | collective-permute-start | bytes 786440 | tf_op jit(solution)/shard_map/ppermute | solution.py:491
  24.7 14.4 %collective-permute-start.4 = (bf16[8,16,1024]{2,1,0:T(8,128)(2,1)S(1)}, bf16[8,16,1024]{2,1,0:T(8,128)(2,1)S(1)}, u32[]{:S(2)}, u32[]{:S(2)}) collective-permute-start(bf16[8,16,1024]{2,1,0:T(8,128)(2,1)S(1)} %all-to-all-done.refs_0_), channel_id=1, source_target_pairs={{0,1},{1,0},{2,3},{3,2},{4,5},{5,4},{6,7},{7,6},{8,9},{9,8},{10,11... | collective-permute-start | bytes 786440 | tf_op jit(solution)/shard_map/ppermute | solution.py:494
  39.1 1.5 %collective-permute-start.6 = (bf16[8,16,1024]{2,1,0:T(8,128)(2,1)S(1)}, bf16[8,16,1024]{2,1,0:T(8,128)(2,1)S(1)}, u32[]{:S(2)}, u32[]{:S(2)}) collective-permute-start(bf16[8,16,1024]{2,1,0:T(8,128)(2,1)S(1)} %collective-permute-done.5.refs_2_), channel_id=1, source_target_pairs={{0,1},{1,0},{2,3},{3,2},{4,5},{5,4},{6,7},{7,6},{8,9},{9,8},{10,11... | collective-permute-start | bytes 786440 | tf_op jit(solution)/shard_map/ppermute | solution.py:494
  46.8 2.0 %collective-permute-start.7 = (bf16[16,16,1024]{2,1,0:T(8,128)(2,1)S(1)}, bf16[16,16,1024]{2,1,0:T(8,128)(2,1)S(1)}, u32[]{:S(2)}, u32[]{:S(2)}) collective-permute-start(bf16[16,16,1024]{2,1,0:T(8,128)(2,1)S(1)} %get-tuple-element.44), channel_id=1, source_target_pairs={{0,1},{1,0},{2,3},{3,2},{4,5},{5,4},{6,7},{7,6},{8,9},{9,8},{10,11... | collective-permute-start | bytes 1572872 | tf_op jit(solution)/shard_map/ppermute | solution.py:494
  72.3 1.6 %collective-permute-start.8 = (bf16[8,16384]{1,0:T(8,128)(2,1)S(1)}, bf16[8,16384]{1,0:T(8,128)(2,1)S(1)}, u32[]{:S(2)}, u32[]{:S(2)}) collective-permute-start(bf16[8,16384]{1,0:T(8,128)(2,1)S(1)} %get-tuple-element.50), channel_id=1, source_target_pairs={{0,1},{1,0},{2,3},{3,2},{4,5},{5,4},{6,7},{7,6},{8,9},{9,8},{10,11... | collective-permute-start | bytes 786440 | tf_op jit(solution)/shard_map/ppermute | solution.py:494

commit v3 on v2

--- a/solution.py
+++ b/solution.py
@@ -498,28 +498,24 @@
         return lax.dynamic_update_slice(own, swap(sent), start)
 
     own, sent, other_rows = as_rows(core, block, k_feature, v_feature, spectrum=spectrum)
-    sent, q_feature = lax.optimization_barrier((sent, q_feature))
     product = joined(own, sent)
-    gate, gate_sent = as_rows(core, block, q_feature)
-    product, spectrum, other_rows, gate, gate_sent, skip_gain, out_weight = (
-        lax.optimization_barrier(
-            (product, spectrum, other_rows, gate, gate_sent, skip_gain, out_weight)
-        )
-    )
-    came_rows = swap(other_rows)
-    gate_other = swap(gate_sent)
-    skip_other = swap(skip_gain)
+    product, spectrum, other_rows = lax.optimization_barrier((product, spectrum, other_rows))
     xa = spread(product)
-    spec = arrange_spectrum(core, spectrum, came_rows, tables["order"])
-    weight = projection(core, out_weight, rows_half)
-    xa, spec, gate_other, skip_other, weight = lax.optimization_barrier(
-        (xa, spec, gate_other, skip_other, weight)
+    spec = arrange_spectrum(core, spectrum, swap(other_rows), tables["order"])
+    xa, spec, q_feature, skip_gain, out_weight = lax.optimization_barrier(
+        (xa, spec, q_feature, skip_gain, out_weight)
     )
     xb = swap(xa)
     za = across(xa)
     spec = spread(spec)
+    gate, gate_sent = as_rows(core, block, q_feature)
+    gate_other = swap(gate_sent)
+    skip_other = swap(skip_gain)
+    weight = projection(core, out_weight, rows_half)
+    za, gate, gate_other, skip_other, weight = lax.optimization_barrier(
+        (za, gate, gate_other, skip_other, weight)
+    )
     zb = swap(za)
-
 
     send, keep = transform(place, (xa, xb, za, zb), spec, tables["transform"])
     total = (keep.astype(F32) + swap(send).astype(F32)).astype(BF16)

time: 75.2 us -> 73.9 us (0.983)
  waiting for transfers between devices: 21.8 us -> 20.3 us
    ppermute x1, waiting for transfers between devices: 14.4 us -> 9.73 us  [local_channels(): lax.ppermute(x, 'ctx', [(d, (d + members) % ctx_count) for d in range(ctx...]
    all_to_all x2, waiting for transfers between devices: 2.46 us -> 4.16 us  [local_channels(): lax.all_to_all(x, 'ctx', 0, 0, axis_index_groups=halves, tiled=True)]
    ppermute x8, waiting for transfers between devices: 4.96 us -> 6.41 us  [local_channels(): swap = lambda x: lax.ppermute(x, 'tp', [(0, 1), (1, 0)])]
  transfers between devices with their start and end apart: 11 -> 11, of which waited for: 6 -> 8; matrix products, arithmetic and copies ran while one was open for 0% -> 0% of each run, Pallas kernels for 7% -> 7%
where the time goes in v3:
time: 73.9 us; the launch traced here: 73.5 us
  blocking collectives  22.5 us (30%)
  waiting for transfers between devices  20.3 us (27%)
  starting transfers between devices  13.8 us (19%)
  Pallas kernels  13.6 us (18%)
  local copies, waits for them, and re-layouts  2.14 us (3%)
  other arithmetic  1.06 us (1%)
    all_to_all x1, blocking collectives, local_channels(): lax.all_to_all(total, 'ctx', 0, 0, tiled=True)  22.5 us
    ppermute x1, waiting for transfers between devices, local_channels(): lax.ppermute(x, 'ctx', [(d, (d + members) % ctx_count) for d in range(ctx...  9.73 us
    all_to_all x2, starting transfers between devices, local_channels(): lax.all_to_all(x, 'ctx', 0, 0, axis_index_groups=halves, tiled=True)  9.44 us
    ppermute x8, waiting for transfers between devices, local_channels(): swap = lambda x: lax.ppermute(x, 'tp', [(0, 1), (1, 0)])  6.41 us
    pallas_call x1, Pallas kernels, transform(): pl.pallas_call(transform_kernel, in_specs=[SMEM] + [ANYWHERE] * (len(piec...  5.35 us
    all_to_all x2, waiting for transfers between devices, local_channels(): lax.all_to_all(x, 'ctx', 0, 0, axis_index_groups=halves, tiled=True)  4.16 us
    pallas_call x2, Pallas kernels, as_rows(): pl.pallas_call(functools.partial(product_kernel, block, len(arrays)), out...  4.13 us
    pallas_call x1, Pallas kernels, arrange_spectrum(): pl.pallas_call(spectrum_kernel, out_shape=jax.ShapeDtypeStruct((2 * chann...  2.9 us
  transfers between devices with their start and end apart: 11, of which 8 were waited for; matrix products, arithmetic and copies ran while one was open for 0% of the time, Pallas kernels for 7%

profile of v3, /device:TPU:0, one launch (start us, length us, event | category | flops | bytes accessed | tf_op | source)
XLA Modules:
  0.0 73.5 jit_solution(15409799359258541653)
XLA Ops:
  0.0 2.3 %shard_map.82 = (bf16[8,16,1024]{2,1,0:T(8,128)(2,1)}, bf16[4,16,1024]{2,1,0:T(8,128)(2,1)}, bf16[2,4,32,1024]{3,2,1,0:T(8,128)(2,1)}) custom-call(s32[1]{0:T(128)} %bitcast.core_ref, bf16[4,32768]{1,0:T(4,128)(2,1)} %refs_0_.1, bf16[4,32768]{1,0:T(4,128)(2,1)} %refs_1_.1, bf16[2,4,64,1024]{3,2,1,0:T(8,128)(2,1)} %in_ref), custom_call_target="tpu_custom_call" | custom-call | flops 1 | bytes 1 | tf_op jit(solution)/shard_map/pallas_call | solution.py:223
  2.3 0.5 collective-permute-start
  2.8 1.2 %collective-permute-done = bf16[4,16,1024]{2,1,0:T(8,128)(2,1)S(1)} collective-permute-done((bf16[4,16,1024]{2,1,0:T(8,128)(2,1)}, bf16[4,16,1024]{2,1,0:T(8,128)(2,1)S(1)}, u32[]{:S(2)}, u32[]{:S(2)}) %collective-permute-start) | collective-permute-done | bytes 131104 | tf_op jit(solution)/shard_map/ppermute | solution.py:494
  4.0 0.7 constant_dynamic-update-slice_fusion.prod
  4.6 0.0 copy-start
  4.6 0.0 copy-start.3
  4.6 0.4 collective-permute-start.1
  5.0 5.9 %all-to-all-start = ((bf16[8,16,1024]{2,1,0:T(8,128)(2,1)}), bf16[8,16,1024]{2,1,0:T(8,128)(2,1)S(1)}, u32[]{:S(2)}, u32[]{:S(2)}) async-start(bf16[8,16,1024]{2,1,0:T(8,128)(2,1)} %constant_dynamic-update-slice_fusion.prod), calls=%async_computation | async-start | bytes 524288 | tf_op jit(solution)/shard_map/all_to_all | solution.py:490
  10.9 0.0 collective-permute-done.1.came_ref
  10.9 0.0 copy-start.4
  10.9 0.8 %copy-done.4 = bf16[2,4,32,1024]{3,2,1,0:T(8,128)(2,1)} copy-done((bf16[2,4,32,1024]{3,2,1,0:T(8,128)(2,1)}, bf16[2,4,32,1024]{3,2,1,0:T(8,128)(2,1)S(1)}, u32[]{:S(2)}) %copy-start.4) | copy-done | bytes 524312
  11.7 2.9 %shard_map.83 = bf16[8,2,32,1024]{3,2,1,0:T(8,128)(2,1)} custom-call(s32[1]{0:T(128)} %bitcast.core_ref, bf16[2,4,64,1024]{3,2,1,0:T(8,128)(2,1)} %in_ref, bf16[2,4,32,1024]{3,2,1,0:T(8,128)(2,1)} %copy-done.4, bf16[256,256]{1,0:T(8,128)(2,1)} %constant.36.clone.order_ref), custom_call_target="tpu_custom_call" | custom-call | flops 1 | bytes 1 | tf_op jit(solution)/shard_map/pallas_call | solution.py:270
  14.6 3.4 %all-to-all-done.refs_0_ = bf16[8,16,1024]{2,1,0:T(8,128)(2,1)S(1)} async-done(((bf16[8,16,1024]{2,1,0:T(8,128)(2,1)}), bf16[8,16,1024]{2,1,0:T(8,128)(2,1)S(1)}, u32[]{:S(2)}, u32[]{:S(2)}) %all-to-all-start) | async-done | bytes 262176 | tf_op jit(solution)/shard_map/all_to_all | solution.py:490
  18.0 3.6 %all-to-all-start.1 = ((bf16[8,2,32,1024]{3,2,1,0:T(8,128)(2,1)}), bf16[8,2,32,1024]{3,2,1,0:T(8,128)(2,1)S(1)}, u32[]{:S(2)}, u32[]{:S(2)}) async-start(bf16[8,2,32,1024]{3,2,1,0:T(8,128)(2,1)} %shard_map.83), calls=%async_computation.1 | async-start | bytes 2097152 | tf_op jit(solution)/shard_map/all_to_all | solution.py:490
  21.6 2.7 %collective-permute-start.3 = (bf16[8,16,1024]{2,1,0:T(8,128)(2,1)S(1)}, bf16[8,16,1024]{2,1,0:T(8,128)(2,1)S(1)}, u32[]{:S(2)}, u32[]{:S(2)}) collective-permute-start(bf16[8,16,1024]{2,1,0:T(8,128)(2,1)S(1)} %all-to-all-done.refs_0_), channel_id=1, source_target_pairs={{0,16},{2,18},{4,20},{6,22},{8,24},{10,26},{12,28},{14,30},{16,0},... | collective-permute-start | bytes 786440 | tf_op jit(solution)/shard_map/ppermute | solution.py:491
  24.2 1.9 %shard_map.84 = (bf16[4,16,1024]{2,1,0:T(8,128)(2,1)}, bf16[4,16,1024]{2,1,0:T(8,128)(2,1)}) custom-call(s32[1]{0:T(128)} %bitcast.core_ref, bf16[4,32768]{1,0:T(4,128)(2,1)} %refs_0_.2), custom_call_target="tpu_custom_call" | custom-call | flops 1 | bytes 1 | tf_op jit(solution)/shard_map/pallas_call | solution.py:223
  26.1 0.0 copy-start.1
  26.1 0.1 collective-permute-start.4
  26.2 0.5 collective-permute-start.2
  26.7 0.1 collective-permute-start.5
  26.8 0.0 copy-start.2
  26.8 0.7 copy-done.2
  27.5 0.3 shard_map.85.weight
  27.8 0.3 collective-permute-done.5.skip_other
  28.0 0.0 collective-permute-done.4.gate_other
  28.0 9.7 %collective-permute-done.3.refs_2_ = bf16[8,16,1024]{2,1,0:T(8,128)(2,1)S(1)} collective-permute-done((bf16[8,16,1024]{2,1,0:T(8,128)(2,1)S(1)}, bf16[8,16,1024]{2,1,0:T(8,128)(2,1)S(1)}, u32[]{:S(2)}, u32[]{:S(2)}) %collective-permute-start.3) | collective-permute-done | bytes 262176 | tf_op jit(solution)/shard_map/ppermute | solution.py:491
  37.7 0.0 collective-permute-start.6
  37.8 0.0 collective-permute-done.2.refs_1_
  37.8 1.5 %collective-permute-done.6.refs_3_ = bf16[8,16,1024]{2,1,0:T(8,128)(2,1)S(1)} collective-permute-done((bf16[8,16,1024]{2,1,0:T(8,128)(2,1)S(1)}, bf16[8,16,1024]{2,1,0:T(8,128)(2,1)S(1)}, u32[]{:S(2)}, u32[]{:S(2)}) %collective-permute-start.6) | collective-permute-done | bytes 262176 | tf_op jit(solution)/shard_map/ppermute | solution.py:494
  39.3 0.7 %all-to-all-done.1.refs_4_ = bf16[8,2,32,1024]{3,2,1,0:T(8,128)(2,1)S(1)} async-done(((bf16[8,2,32,1024]{3,2,1,0:T(8,128)(2,1)}), bf16[8,2,32,1024]{3,2,1,0:T(8,128)(2,1)S(1)}, u32[]{:S(2)}, u32[]{:S(2)}) %all-to-all-start.1) | async-done | bytes 1048608 | tf_op jit(solution)/shard_map/all_to_all | solution.py:490
  40.0 5.3 %shard_map.86 = (bf16[16,16,1024]{2,1,0:T(8,128)(2,1)S(1)}, bf16[16,16,1024]{2,1,0:T(8,128)(2,1)S(1)}) custom-call(s32[1]{0:T(128)} %bitcast.1.place_ref, bf16[8,16,1024]{2,1,0:T(8,128)(2,1)S(1)} %all-to-all-done.refs_0_, bf16[8,16,1024]{2,1,0:T(8,128)(2,1)S(1)} %collective-permute-done.2.refs_1_, bf16[8,16,1024]{2,1,0:T(8,128)(2,1)S(1)} %collective-permute-done.3.refs_2_, ...), custom_call_target="tpu_custom_call" | custom-call | flops 1 | bytes 1 | tf_op jit(solution)/shard_map/pallas_call | solution.py:421
  45.4 0.1 collective-permute-start.7
  45.5 1.9 %collective-permute-done.7 = bf16[16,16,1024]{2,1,0:T(8,128)(2,1)S(1)} collective-permute-done((bf16[16,16,1024]{2,1,0:T(8,128)(2,1)S(1)}, bf16[16,16,1024]{2,1,0:T(8,128)(2,1)S(1)}, u32[]{:S(2)}, u32[]{:S(2)}) %collective-permute-start.7) | collective-permute-done | bytes 524320 | tf_op jit(solution)/shard_map/ppermute | solution.py:494
  47.4 0.2 add_convert_fusion
  47.6 22.5 %all_to_all.15 = bf16[16,16,1024]{2,1,0:T(8,128)(2,1)S(1)} all-to-all(bf16[16,16,1024]{2,1,0:T(8,128)(2,1)S(1)} %add_convert_fusion), channel_id=1, replica_groups=mesh['ctx'=16,'tp'=2] {'ctx'}, dimensions={0} | all-to-all | bytes 1048576 | tf_op jit(solution)/shard_map/all_to_all | solution.py:522
  70.1 0.0 copy-done
  70.1 0.0 copy-done.3
  70.1 0.0 copy-done.1
  70.1 0.9 %shard_map.87 = (bf16[8,16384]{1,0:T(8,128)(2,1)S(1)}, bf16[8,16384]{1,0:T(8,128)(2,1)S(1)}) custom-call(s32[1]{0:T(128)} %bitcast.core_ref, bf16[2,8,16,1024]{3,2,1,0:T(8,128)(2,1)S(1)} %bitcast.3, bf16[8,16,1024]{2,1,0:T(8,128)(2,1)S(1)} %copy-done, bf16[4,16,1024]{2,1,0:T(8,128)(2,1)S(1)} %copy-done.1, ...), custom_call_target="tpu_custom_call" | custom-call | flops 1 | bytes 1 | tf_op jit(solution)/shard_map/pallas_call | solution.py:464
  71.0 0.1 collective-permute-start.8
  71.1 1.5 %collective-permute-done.8 = bf16[8,16384]{1,0:T(8,128)(2,1)S(1)} collective-permute-done((bf16[8,16384]{1,0:T(8,128)(2,1)S(1)}, bf16[8,16384]{1,0:T(8,128)(2,1)S(1)}, u32[]{:S(2)}, u32[]{:S(2)}) %collective-permute-start.8) | collective-permute-done | bytes 262176 | tf_op jit(solution)/shard_map/ppermute | solution.py:494
  72.6 0.8 %pad_maximum_fusion = bf16[8,32768]{1,0:T(8,128)(2,1)} fusion(bf16[8,16384]{1,0:T(8,128)(2,1)S(1)} %get-tuple-element.50, bf16[8,16384]{1,0:T(8,128)(2,1)S(1)} %get-tuple-element.49), kind=kLoop, calls=%fused_computation.1 | loop fusion | flops 1048576 | bytes 1048576 | tf_op jit(solution)/shard_map/concatenate | solution.py:529
  (1 shorter events, 0.0 us)
Async XLA Ops:
  2.3 1.7 %collective-permute-start = (bf16[4,16,1024]{2,1,0:T(8,128)(2,1)}, bf16[4,16,1024]{2,1,0:T(8,128)(2,1)S(1)}, u32[]{:S(2)}, u32[]{:S(2)}) collective-permute-start(bf16[4,16,1024]{2,1,0:T(8,128)(2,1)} %get-tuple-element.28), channel_id=1, source_target_pairs={{0,1},{1,0},{2,3},{3,2},{4,5},{5,4},{6,7},{7,6},{8,9},{9,8},{10,11... | collective-permute-start | bytes 393224 | tf_op jit(solution)/shard_map/ppermute | solution.py:494
  4.6 65.4 %copy-start = (bf16[8,16,1024]{2,1,0:T(8,128)(2,1)S(1)}, bf16[8,16,1024]{2,1,0:T(8,128)(2,1)}, u32[]{:S(2)}) copy-start(bf16[8,16,1024]{2,1,0:T(8,128)(2,1)} %constant_dynamic-update-slice_fusion.prod) | copy-start | bytes 786436
  4.6 65.4 %copy-start.3 = (f32[4]{0:T(128)S(1)}, f32[4]{0:T(128)}, u32[]{:S(2)}) copy-start(f32[4]{0:T(128)} %skip) | copy-start | bytes 52
  4.6 6.3 %collective-permute-start.1 = (bf16[2,4,32,1024]{3,2,1,0:T(8,128)(2,1)}, bf16[2,4,32,1024]{3,2,1,0:T(8,128)(2,1)S(1)}, u32[]{:S(2)}, u32[]{:S(2)}) collective-permute-start(bf16[2,4,32,1024]{3,2,1,0:T(8,128)(2,1)} %get-tuple-element.32), channel_id=1, source_target_pairs={{0,1},{1,0},{2,3},{3,2},{4,5},{5,4},{6,7},{7,6},{8,9},{9,8},{10,11... | collective-permute-start | bytes 1572872 | tf_op jit(solution)/shard_map/ppermute | solution.py:494
  5.0 13.0 %all-to-all-start = ((bf16[8,16,1024]{2,1,0:T(8,128)(2,1)}), bf16[8,16,1024]{2,1,0:T(8,128)(2,1)S(1)}, u32[]{:S(2)}, u32[]{:S(2)}) async-start(bf16[8,16,1024]{2,1,0:T(8,128)(2,1)} %constant_dynamic-update-slice_fusion.prod), calls=%async_computation | async-start | bytes 524288 | tf_op jit(solution)/shard_map/all_to_all | solution.py:490
  10.9 0.8 %copy-start.4 = (bf16[2,4,32,1024]{3,2,1,0:T(8,128)(2,1)}, bf16[2,4,32,1024]{3,2,1,0:T(8,128)(2,1)S(1)}, u32[]{:S(2)}) copy-start(bf16[2,4,32,1024]{3,2,1,0:T(8,128)(2,1)S(1)} %collective-permute-done.1.came_ref) | copy-start | bytes 1572868
  18.0 22.0 %all-to-all-start.1 = ((bf16[8,2,32,1024]{3,2,1,0:T(8,128)(2,1)}), bf16[8,2,32,1024]{3,2,1,0:T(8,128)(2,1)S(1)}, u32[]{:S(2)}, u32[]{:S(2)}) async-start(bf16[8,2,32,1024]{3,2,1,0:T(8,128)(2,1)} %shard_map.83), calls=%async_computation.1 | async-start | bytes 2097152 | tf_op jit(solution)/shard_map/all_to_all | solution.py:490
  21.6 16.2 %collective-permute-start.3 = (bf16[8,16,1024]{2,1,0:T(8,128)(2,1)S(1)}, bf16[8,16,1024]{2,1,0:T(8,128)(2,1)S(1)}, u32[]{:S(2)}, u32[]{:S(2)}) collective-permute-start(bf16[8,16,1024]{2,1,0:T(8,128)(2,1)S(1)} %all-to-all-done.refs_0_), channel_id=1, source_target_pairs={{0,16},{2,18},{4,20},{6,22},{8,24},{10,26},{12,28},{14,30},{16,0},... | collective-permute-start | bytes 786440 | tf_op jit(solution)/shard_map/ppermute | solution.py:491
  26.1 44.0 %copy-start.1 = (bf16[4,16,1024]{2,1,0:T(8,128)(2,1)S(1)}, bf16[4,16,1024]{2,1,0:T(8,128)(2,1)}, u32[]{:S(2)}) copy-start(bf16[4,16,1024]{2,1,0:T(8,128)(2,1)} %get-tuple-element.43.gate) | copy-start | bytes 393220
  26.1 1.9 %collective-permute-start.4 = (bf16[4,16,1024]{2,1,0:T(8,128)(2,1)}, bf16[4,16,1024]{2,1,0:T(8,128)(2,1)S(1)}, u32[]{:S(2)}, u32[]{:S(2)}) collective-permute-start(bf16[4,16,1024]{2,1,0:T(8,128)(2,1)} %get-tuple-element.36), channel_id=1, source_target_pairs={{0,1},{1,0},{2,3},{3,2},{4,5},{5,4},{6,7},{7,6},{8,9},{9,8},{10,11... | collective-permute-start | bytes 393224 | tf_op jit(solution)/shard_map/ppermute | solution.py:494
  26.2 11.5 %collective-permute-start.2 = (bf16[8,16,1024]{2,1,0:T(8,128)(2,1)S(1)}, bf16[8,16,1024]{2,1,0:T(8,128)(2,1)S(1)}, u32[]{:S(2)}, u32[]{:S(2)}) collective-permute-start(bf16[8,16,1024]{2,1,0:T(8,128)(2,1)S(1)} %all-to-all-done.refs_0_), channel_id=1, source_target_pairs={{0,1},{1,0},{2,3},{3,2},{4,5},{5,4},{6,7},{7,6},{8,9},{9,8},{10,11... | collective-permute-start | bytes 786440 | tf_op jit(solution)/shard_map/ppermute | solution.py:494
  26.7 1.3 %collective-permute-start.5 = (f32[4]{0:T(128)}, f32[4]{0:T(128)S(1)}, u32[]{:S(2)}, u32[]{:S(2)}) collective-permute-start(f32[4]{0:T(128)} %skip), channel_id=1, source_target_pairs={{0,1},{1,0},{2,3},{3,2},{4,5},{5,4},{6,7},{7,6},{8,9},{9,8},{10,11... | collective-permute-start | bytes 56 | tf_op jit(solution)/shard_map/ppermute | solution.py:494
  26.8 0.7 copy-start.2
  37.7 1.5 %collective-permute-start.6 = (bf16[8,16,1024]{2,1,0:T(8,128)(2,1)S(1)}, bf16[8,16,1024]{2,1,0:T(8,128)(2,1)S(1)}, u32[]{:S(2)}, u32[]{:S(2)}) collective-permute-start(bf16[8,16,1024]{2,1,0:T(8,128)(2,1)S(1)} %collective-permute-done.3.refs_2_), channel_id=1, source_target_pairs={{0,1},{1,0},{2,3},{3,2},{4,5},{5,4},{6,7},{7,6},{8,9},{9,8},{10,11... | collective-permute-start | bytes 786440 | tf_op jit(solution)/shard_map/ppermute | solution.py:494
  45.4 2.0 %collective-permute-start.7 = (bf16[16,16,1024]{2,1,0:T(8,128)(2,1)S(1)}, bf16[16,16,1024]{2,1,0:T(8,128)(2,1)S(1)}, u32[]{:S(2)}, u32[]{:S(2)}) collective-permute-start(bf16[16,16,1024]{2,1,0:T(8,128)(2,1)S(1)} %get-tuple-element.42), channel_id=1, source_target_pairs={{0,1},{1,0},{2,3},{3,2},{4,5},{5,4},{6,7},{7,6},{8,9},{9,8},{10,11... | collective-permute-start | bytes 1572872 | tf_op jit(solution)/shard_map/ppermute | solution.py:494
  71.0 1.6 %collective-permute-start.8 = (bf16[8,16384]{1,0:T(8,128)(2,1)S(1)}, bf16[8,16384]{1,0:T(8,128)(2,1)S(1)}, u32[]{:S(2)}, u32[]{:S(2)}) collective-permute-start(bf16[8,16384]{1,0:T(8,128)(2,1)S(1)} %get-tuple-element.48), channel_id=1, source_target_pairs={{0,1},{1,0},{2,3},{3,2},{4,5},{5,4},{6,7},{7,6},{8,9},{9,8},{10,11... | collective-permute-start | bytes 786440 | tf_op jit(solution)/shard_map/ppermute | solution.py:494

commit v4 on v3

--- a/solution.py
+++ b/solution.py
@@ -118,6 +118,11 @@
     return np.cos(angles), np.sin(angles)
 
 
+def last_order(members):
+    size = members // 2
+    return [quarter * size + n for n in range(size) for quarter in (2, 0, 3, 1)]
+
+
 @functools.lru_cache(maxsize=None)
 def constant_tables(block, members, rows_half, a_half):
     quarter = block // 4
@@ -139,7 +144,13 @@
             i_in = np.concatenate([rows(g, s), rows(g, 1 - s), rows(1 - g, s), rows(1 - g, 1 - s)])
             cosine, sine = cosine_sine(a[:, None] * i_in[None, :], block)
             firsts.append(np.concatenate([cosine, -sine], 0))
-            i_out = np.concatenate([rows(0, 1 - s), rows(1, 1 - s), rows(0, s), rows(1, s)])
+            place = last_order(members)
+
+            def by_place(core):
+                i = np.concatenate([rows(0, core), rows(1, core)])
+                return i.reshape(2 * members, -1)[place].reshape(-1)
+
+            i_out = np.concatenate([by_place(1 - s), by_place(s)])
             cosine, sine = cosine_sine(i_out[:, None] * a[None, :], block)
             lasts.append(np.concatenate([cosine, -sine], 1))
             coarse = 128 * (np.arange(128) % (block // 128))
@@ -439,15 +450,14 @@
 
 
 def gate_kernel(core_ref, conv, prod, gate, gate_other, skip, skip_other, weight, keep, send):
-    _, channels, rows, block = conv.shape
+    here, _, rows, block = conv.shape
     core = core_ref[0]
-    here = channels // 2
     pieces = []
     for side, (values, gains) in enumerate(((gate, skip), (gate_other, skip_other))):
         for n in range(here):
-            c = jnp.bitwise_xor(core, side) * here + n
-            total = conv[0, c].astype(F32) + conv[1, c].astype(F32)
-            total = total + gains[n] * prod[c].astype(F32)
+            high = jnp.bitwise_xor(core, side)
+            total = conv[n, 2 * high].astype(F32) + conv[n, 2 * high + 1].astype(F32)
+            total = total + gains[n] * prod[high * here + n].astype(F32)
             pieces.append((values[n].astype(F32) * total).astype(BF16))
     gated = jnp.concatenate(pieces, axis=0)
     mixed = jnp.dot(weight[...], gated, preferred_element_type=F32)
@@ -459,7 +469,7 @@
 
 
 def gate_and_project(core, conv, prod, gate, gate_other, skip, skip_other, weight):
-    _, channels, rows, block = conv.shape
+    _, _, rows, block = conv.shape
     outs = weight.shape[0] // (2 * rows)
     return pl.pallas_call(
         gate_kernel,
@@ -519,7 +529,9 @@
 
     send, keep = transform(place, (xa, xb, za, zb), spec, tables["transform"])
     total = (keep.astype(F32) + swap(send).astype(F32)).astype(BF16)
-    conv = lax.all_to_all(total, "ctx", 0, 0, tiled=True).reshape(2, members, rows_half, block)
+    conv = lax.all_to_all(
+        total, "ctx", 0, 0, axis_index_groups=[last_order(members)], tiled=True
+    ).reshape(channels, 4, rows_half, block)
     kept, sent = gate_and_project(
         core, conv, product, gate, gate_other, skip_gain, skip_other, weight
     )

time: 73.9 us -> 72.8 us (0.985)
  blocking collectives: 22.5 us -> 21.4 us
    all_to_all x1, blocking collectives: 22.5 us -> 21.4 us  [local_channels(): lax.all_to_all(total, 'ctx', 0, 0, axis_index_groups=[last_order(members)...]
where the time goes in v4:
time: 72.8 us; the launch traced here: 72.4 us
  blocking collectives  21.4 us (29%)
  waiting for transfers between devices  20.3 us (28%)
  starting transfers between devices  13.8 us (19%)
  Pallas kernels  13.6 us (19%)
  local copies, waits for them, and re-layouts  2.14 us (3%)
  other arithmetic  1.06 us (1%)
    all_to_all x1, blocking collectives, local_channels(): lax.all_to_all(total, 'ctx', 0, 0, axis_index_groups=[last_order(members)...  21.4 us
    ppermute x1, waiting for transfers between devices, local_channels(): lax.ppermute(x, 'ctx', [(d, (d + members) % ctx_count) for d in range(ctx...  9.73 us
    all_to_all x2, starting transfers between devices, local_channels(): lax.all_to_all(x, 'ctx', 0, 0, axis_index_groups=halves, tiled=True)  9.44 us
    ppermute x8, waiting for transfers between devices, local_channels(): swap = lambda x: lax.ppermute(x, 'tp', [(0, 1), (1, 0)])  6.41 us
    pallas_call x1, Pallas kernels, transform(): pl.pallas_call(transform_kernel, in_specs=[SMEM] + [ANYWHERE] * (len(piec...  5.35 us
    all_to_all x2, waiting for transfers between devices, local_channels(): lax.all_to_all(x, 'ctx', 0, 0, axis_index_groups=halves, tiled=True)  4.16 us
    pallas_call x2, Pallas kernels, as_rows(): pl.pallas_call(functools.partial(product_kernel, block, len(arrays)), out...  4.13 us
    pallas_call x1, Pallas kernels, arrange_spectrum(): pl.pallas_call(spectrum_kernel, out_shape=jax.ShapeDtypeStruct((2 * chann...  2.9 us
  transfers between devices with their start and end apart: 11, of which 8 were waited for; matrix products, arithmetic and copies ran while one was open for 0% of the time, Pallas kernels for 7%

profile of v4, /device:TPU:0, one launch (start us, length us, event | category | flops | bytes accessed | tf_op | source)
XLA Modules:
  0.0 72.4 jit_solution(1962472047442565260)
XLA Ops:
  0.0 2.3 %shard_map.82 = (bf16[8,16,1024]{2,1,0:T(8,128)(2,1)}, bf16[4,16,1024]{2,1,0:T(8,128)(2,1)}, bf16[2,4,32,1024]{3,2,1,0:T(8,128)(2,1)}) custom-call(s32[1]{0:T(128)} %bitcast.core_ref, bf16[4,32768]{1,0:T(4,128)(2,1)} %refs_0_.1, bf16[4,32768]{1,0:T(4,128)(2,1)} %refs_1_.1, bf16[2,4,64,1024]{3,2,1,0:T(8,128)(2,1)} %in_ref), custom_call_target="tpu_custom_call" | custom-call | flops 1 | bytes 1 | tf_op jit(solution)/shard_map/pallas_call | solution.py:234
  2.3 0.5 collective-permute-start
  2.8 1.2 %collective-permute-done = bf16[4,16,1024]{2,1,0:T(8,128)(2,1)S(1)} collective-permute-done((bf16[4,16,1024]{2,1,0:T(8,128)(2,1)}, bf16[4,16,1024]{2,1,0:T(8,128)(2,1)S(1)}, u32[]{:S(2)}, u32[]{:S(2)}) %collective-permute-start) | collective-permute-done | bytes 131104 | tf_op jit(solution)/shard_map/ppermute | solution.py:504
  4.0 0.7 constant_dynamic-update-slice_fusion.prod
  4.6 0.0 copy-start
  4.6 0.0 copy-start.3
  4.6 0.4 collective-permute-start.1
  5.0 5.9 %all-to-all-start = ((bf16[8,16,1024]{2,1,0:T(8,128)(2,1)}), bf16[8,16,1024]{2,1,0:T(8,128)(2,1)S(1)}, u32[]{:S(2)}, u32[]{:S(2)}) async-start(bf16[8,16,1024]{2,1,0:T(8,128)(2,1)} %constant_dynamic-update-slice_fusion.prod), calls=%async_computation | async-start | bytes 524288 | tf_op jit(solution)/shard_map/all_to_all | solution.py:500
  10.9 0.0 collective-permute-done.1.came_ref
  10.9 0.0 copy-start.4
  10.9 0.8 %copy-done.4 = bf16[2,4,32,1024]{3,2,1,0:T(8,128)(2,1)} copy-done((bf16[2,4,32,1024]{3,2,1,0:T(8,128)(2,1)}, bf16[2,4,32,1024]{3,2,1,0:T(8,128)(2,1)S(1)}, u32[]{:S(2)}) %copy-start.4) | copy-done | bytes 524312
  11.7 2.9 %shard_map.83 = bf16[8,2,32,1024]{3,2,1,0:T(8,128)(2,1)} custom-call(s32[1]{0:T(128)} %bitcast.core_ref, bf16[2,4,64,1024]{3,2,1,0:T(8,128)(2,1)} %in_ref, bf16[2,4,32,1024]{3,2,1,0:T(8,128)(2,1)} %copy-done.4, bf16[256,256]{1,0:T(8,128)(2,1)} %constant.36.clone.order_ref), custom_call_target="tpu_custom_call" | custom-call | flops 1 | bytes 1 | tf_op jit(solution)/shard_map/pallas_call | solution.py:281
  14.6 3.4 %all-to-all-done.refs_0_ = bf16[8,16,1024]{2,1,0:T(8,128)(2,1)S(1)} async-done(((bf16[8,16,1024]{2,1,0:T(8,128)(2,1)}), bf16[8,16,1024]{2,1,0:T(8,128)(2,1)S(1)}, u32[]{:S(2)}, u32[]{:S(2)}) %all-to-all-start) | async-done | bytes 262176 | tf_op jit(solution)/shard_map/all_to_all | solution.py:500
  18.0 3.6 %all-to-all-start.1 = ((bf16[8,2,32,1024]{3,2,1,0:T(8,128)(2,1)}), bf16[8,2,32,1024]{3,2,1,0:T(8,128)(2,1)S(1)}, u32[]{:S(2)}, u32[]{:S(2)}) async-start(bf16[8,2,32,1024]{3,2,1,0:T(8,128)(2,1)} %shard_map.83), calls=%async_computation.1 | async-start | bytes 2097152 | tf_op jit(solution)/shard_map/all_to_all | solution.py:500
  21.6 2.7 %collective-permute-start.3 = (bf16[8,16,1024]{2,1,0:T(8,128)(2,1)S(1)}, bf16[8,16,1024]{2,1,0:T(8,128)(2,1)S(1)}, u32[]{:S(2)}, u32[]{:S(2)}) collective-permute-start(bf16[8,16,1024]{2,1,0:T(8,128)(2,1)S(1)} %all-to-all-done.refs_0_), channel_id=1, source_target_pairs={{0,16},{2,18},{4,20},{6,22},{8,24},{10,26},{12,28},{14,30},{16,0},... | collective-permute-start | bytes 786440 | tf_op jit(solution)/shard_map/ppermute | solution.py:501
  24.2 1.9 %shard_map.84 = (bf16[4,16,1024]{2,1,0:T(8,128)(2,1)}, bf16[4,16,1024]{2,1,0:T(8,128)(2,1)}) custom-call(s32[1]{0:T(128)} %bitcast.core_ref, bf16[4,32768]{1,0:T(4,128)(2,1)} %refs_0_.2), custom_call_target="tpu_custom_call" | custom-call | flops 1 | bytes 1 | tf_op jit(solution)/shard_map/pallas_call | solution.py:234
  26.1 0.0 copy-start.1
  26.1 0.1 collective-permute-start.4
  26.2 0.5 collective-permute-start.2
  26.7 0.1 collective-permute-start.5
  26.8 0.0 copy-start.2
  26.8 0.7 copy-done.2
  27.5 0.3 shard_map.85.weight
  27.8 0.3 collective-permute-done.5.skip_other
  28.0 0.0 collective-permute-done.4.gate_other
  28.0 9.7 %collective-permute-done.3.refs_2_ = bf16[8,16,1024]{2,1,0:T(8,128)(2,1)S(1)} collective-permute-done((bf16[8,16,1024]{2,1,0:T(8,128)(2,1)S(1)}, bf16[8,16,1024]{2,1,0:T(8,128)(2,1)S(1)}, u32[]{:S(2)}, u32[]{:S(2)}) %collective-permute-start.3) | collective-permute-done | bytes 262176 | tf_op jit(solution)/shard_map/ppermute | solution.py:501
  37.7 0.0 collective-permute-start.6
  37.8 0.0 collective-permute-done.2.refs_1_
  37.8 1.5 %collective-permute-done.6.refs_3_ = bf16[8,16,1024]{2,1,0:T(8,128)(2,1)S(1)} collective-permute-done((bf16[8,16,1024]{2,1,0:T(8,128)(2,1)S(1)}, bf16[8,16,1024]{2,1,0:T(8,128)(2,1)S(1)}, u32[]{:S(2)}, u32[]{:S(2)}) %collective-permute-start.6) | collective-permute-done | bytes 262176 | tf_op jit(solution)/shard_map/ppermute | solution.py:504
  39.3 0.7 %all-to-all-done.1.refs_4_ = bf16[8,2,32,1024]{3,2,1,0:T(8,128)(2,1)S(1)} async-done(((bf16[8,2,32,1024]{3,2,1,0:T(8,128)(2,1)}), bf16[8,2,32,1024]{3,2,1,0:T(8,128)(2,1)S(1)}, u32[]{:S(2)}, u32[]{:S(2)}) %all-to-all-start.1) | async-done | bytes 1048608 | tf_op jit(solution)/shard_map/all_to_all | solution.py:500
  40.0 5.3 %shard_map.86 = (bf16[16,16,1024]{2,1,0:T(8,128)(2,1)S(1)}, bf16[16,16,1024]{2,1,0:T(8,128)(2,1)S(1)}) custom-call(s32[1]{0:T(128)} %bitcast.1.place_ref, bf16[8,16,1024]{2,1,0:T(8,128)(2,1)S(1)} %all-to-all-done.refs_0_, bf16[8,16,1024]{2,1,0:T(8,128)(2,1)S(1)} %collective-permute-done.2.refs_1_, bf16[8,16,1024]{2,1,0:T(8,128)(2,1)S(1)} %collective-permute-done.3.refs_2_, ...), custom_call_target="tpu_custom_call" | custom-call | flops 1 | bytes 1 | tf_op jit(solution)/shard_map/pallas_call | solution.py:432
  45.4 0.1 collective-permute-start.7
  45.5 1.9 %collective-permute-done.7 = bf16[16,16,1024]{2,1,0:T(8,128)(2,1)S(1)} collective-permute-done((bf16[16,16,1024]{2,1,0:T(8,128)(2,1)S(1)}, bf16[16,16,1024]{2,1,0:T(8,128)(2,1)S(1)}, u32[]{:S(2)}, u32[]{:S(2)}) %collective-permute-start.7) | collective-permute-done | bytes 524320 | tf_op jit(solution)/shard_map/ppermute | solution.py:504
  47.4 0.2 add_convert_fusion
  47.6 21.4 %all_to_all.15 = bf16[16,16,1024]{2,1,0:T(8,128)(2,1)S(1)} all-to-all(bf16[16,16,1024]{2,1,0:T(8,128)(2,1)S(1)} %add_convert_fusion), channel_id=1, replica_groups={{16,0,24,8,18,2,26,10,20,4,28,12,22,6,30,14},{17,1,25,9,19,3,27,11,21,5..., dimensions={0} | all-to-all | bytes 1048576 | tf_op jit(solution)/shard_map/all_to_all | solution.py:532
  69.0 0.0 copy-done
  69.0 0.0 copy-done.3
  69.0 0.0 copy-done.1
  69.0 0.9 %shard_map.87 = (bf16[8,16384]{1,0:T(8,128)(2,1)S(1)}, bf16[8,16384]{1,0:T(8,128)(2,1)S(1)}) custom-call(s32[1]{0:T(128)} %bitcast.core_ref, bf16[4,4,16,1024]{3,2,1,0:T(8,128)(2,1)S(1)} %bitcast.3, bf16[8,16,1024]{2,1,0:T(8,128)(2,1)S(1)} %copy-done, bf16[4,16,1024]{2,1,0:T(8,128)(2,1)S(1)} %copy-done.1, ...), custom_call_target="tpu_custom_call" | custom-call | flops 1 | bytes 1 | tf_op jit(solution)/shard_map/pallas_call | solution.py:474
  69.9 0.1 collective-permute-start.8
  70.0 1.5 %collective-permute-done.8 = bf16[8,16384]{1,0:T(8,128)(2,1)S(1)} collective-permute-done((bf16[8,16384]{1,0:T(8,128)(2,1)S(1)}, bf16[8,16384]{1,0:T(8,128)(2,1)S(1)}, u32[]{:S(2)}, u32[]{:S(2)}) %collective-permute-start.8) | collective-permute-done | bytes 262176 | tf_op jit(solution)/shard_map/ppermute | solution.py:504
  71.6 0.8 %pad_maximum_fusion = bf16[8,32768]{1,0:T(8,128)(2,1)} fusion(bf16[8,16384]{1,0:T(8,128)(2,1)S(1)} %get-tuple-element.50, bf16[8,16384]{1,0:T(8,128)(2,1)S(1)} %get-tuple-element.49), kind=kLoop, calls=%fused_computation.1 | loop fusion | flops 1048576 | bytes 1048576 | tf_op jit(solution)/shard_map/concatenate | solution.py:541
  (1 shorter events, 0.0 us)
Async XLA Ops:
  2.3 1.7 %collective-permute-start = (bf16[4,16,1024]{2,1,0:T(8,128)(2,1)}, bf16[4,16,1024]{2,1,0:T(8,128)(2,1)S(1)}, u32[]{:S(2)}, u32[]{:S(2)}) collective-permute-start(bf16[4,16,1024]{2,1,0:T(8,128)(2,1)} %get-tuple-element.28), channel_id=1, source_target_pairs={{0,1},{1,0},{2,3},{3,2},{4,5},{5,4},{6,7},{7,6},{8,9},{9,8},{10,11... | collective-permute-start | bytes 393224 | tf_op jit(solution)/shard_map/ppermute | solution.py:504
  4.6 64.4 %copy-start = (bf16[8,16,1024]{2,1,0:T(8,128)(2,1)S(1)}, bf16[8,16,1024]{2,1,0:T(8,128)(2,1)}, u32[]{:S(2)}) copy-start(bf16[8,16,1024]{2,1,0:T(8,128)(2,1)} %constant_dynamic-update-slice_fusion.prod) | copy-start | bytes 786436
  4.6 64.4 %copy-start.3 = (f32[4]{0:T(128)S(1)}, f32[4]{0:T(128)}, u32[]{:S(2)}) copy-start(f32[4]{0:T(128)} %skip) | copy-start | bytes 52
  4.6 6.3 %collective-permute-start.1 = (bf16[2,4,32,1024]{3,2,1,0:T(8,128)(2,1)}, bf16[2,4,32,1024]{3,2,1,0:T(8,128)(2,1)S(1)}, u32[]{:S(2)}, u32[]{:S(2)}) collective-permute-start(bf16[2,4,32,1024]{3,2,1,0:T(8,128)(2,1)} %get-tuple-element.32), channel_id=1, source_target_pairs={{0,1},{1,0},{2,3},{3,2},{4,5},{5,4},{6,7},{7,6},{8,9},{9,8},{10,11... | collective-permute-start | bytes 1572872 | tf_op jit(solution)/shard_map/ppermute | solution.py:504
  5.0 13.0 %all-to-all-start = ((bf16[8,16,1024]{2,1,0:T(8,128)(2,1)}), bf16[8,16,1024]{2,1,0:T(8,128)(2,1)S(1)}, u32[]{:S(2)}, u32[]{:S(2)}) async-start(bf16[8,16,1024]{2,1,0:T(8,128)(2,1)} %constant_dynamic-update-slice_fusion.prod), calls=%async_computation | async-start | bytes 524288 | tf_op jit(solution)/shard_map/all_to_all | solution.py:500
  10.9 0.8 %copy-start.4 = (bf16[2,4,32,1024]{3,2,1,0:T(8,128)(2,1)}, bf16[2,4,32,1024]{3,2,1,0:T(8,128)(2,1)S(1)}, u32[]{:S(2)}) copy-start(bf16[2,4,32,1024]{3,2,1,0:T(8,128)(2,1)S(1)} %collective-permute-done.1.came_ref) | copy-start | bytes 1572868
  18.0 22.0 %all-to-all-start.1 = ((bf16[8,2,32,1024]{3,2,1,0:T(8,128)(2,1)}), bf16[8,2,32,1024]{3,2,1,0:T(8,128)(2,1)S(1)}, u32[]{:S(2)}, u32[]{:S(2)}) async-start(bf16[8,2,32,1024]{3,2,1,0:T(8,128)(2,1)} %shard_map.83), calls=%async_computation.1 | async-start | bytes 2097152 | tf_op jit(solution)/shard_map/all_to_all | solution.py:500
  21.6 16.2 %collective-permute-start.3 = (bf16[8,16,1024]{2,1,0:T(8,128)(2,1)S(1)}, bf16[8,16,1024]{2,1,0:T(8,128)(2,1)S(1)}, u32[]{:S(2)}, u32[]{:S(2)}) collective-permute-start(bf16[8,16,1024]{2,1,0:T(8,128)(2,1)S(1)} %all-to-all-done.refs_0_), channel_id=1, source_target_pairs={{0,16},{2,18},{4,20},{6,22},{8,24},{10,26},{12,28},{14,30},{16,0},... | collective-permute-start | bytes 786440 | tf_op jit(solution)/shard_map/ppermute | solution.py:501
  26.1 42.9 %copy-start.1 = (bf16[4,16,1024]{2,1,0:T(8,128)(2,1)S(1)}, bf16[4,16,1024]{2,1,0:T(8,128)(2,1)}, u32[]{:S(2)}) copy-start(bf16[4,16,1024]{2,1,0:T(8,128)(2,1)} %get-tuple-element.43.gate) | copy-start | bytes 393220
  26.1 1.9 %collective-permute-start.4 = (bf16[4,16,1024]{2,1,0:T(8,128)(2,1)}, bf16[4,16,1024]{2,1,0:T(8,128)(2,1)S(1)}, u32[]{:S(2)}, u32[]{:S(2)}) collective-permute-start(bf16[4,16,1024]{2,1,0:T(8,128)(2,1)} %get-tuple-element.36), channel_id=1, source_target_pairs={{0,1},{1,0},{2,3},{3,2},{4,5},{5,4},{6,7},{7,6},{8,9},{9,8},{10,11... | collective-permute-start | bytes 393224 | tf_op jit(solution)/shard_map/ppermute | solution.py:504
  26.2 11.5 %collective-permute-start.2 = (bf16[8,16,1024]{2,1,0:T(8,128)(2,1)S(1)}, bf16[8,16,1024]{2,1,0:T(8,128)(2,1)S(1)}, u32[]{:S(2)}, u32[]{:S(2)}) collective-permute-start(bf16[8,16,1024]{2,1,0:T(8,128)(2,1)S(1)} %all-to-all-done.refs_0_), channel_id=1, source_target_pairs={{0,1},{1,0},{2,3},{3,2},{4,5},{5,4},{6,7},{7,6},{8,9},{9,8},{10,11... | collective-permute-start | bytes 786440 | tf_op jit(solution)/shard_map/ppermute | solution.py:504
  26.7 1.3 %collective-permute-start.5 = (f32[4]{0:T(128)}, f32[4]{0:T(128)S(1)}, u32[]{:S(2)}, u32[]{:S(2)}) collective-permute-start(f32[4]{0:T(128)} %skip), channel_id=1, source_target_pairs={{0,1},{1,0},{2,3},{3,2},{4,5},{5,4},{6,7},{7,6},{8,9},{9,8},{10,11... | collective-permute-start | bytes 56 | tf_op jit(solution)/shard_map/ppermute | solution.py:504
  26.8 0.7 copy-start.2
  37.7 1.5 %collective-permute-start.6 = (bf16[8,16,1024]{2,1,0:T(8,128)(2,1)S(1)}, bf16[8,16,1024]{2,1,0:T(8,128)(2,1)S(1)}, u32[]{:S(2)}, u32[]{:S(2)}) collective-permute-start(bf16[8,16,1024]{2,1,0:T(8,128)(2,1)S(1)} %collective-permute-done.3.refs_2_), channel_id=1, source_target_pairs={{0,1},{1,0},{2,3},{3,2},{4,5},{5,4},{6,7},{7,6},{8,9},{9,8},{10,11... | collective-permute-start | bytes 786440 | tf_op jit(solution)/shard_map/ppermute | solution.py:504
  45.4 2.0 %collective-permute-start.7 = (bf16[16,16,1024]{2,1,0:T(8,128)(2,1)S(1)}, bf16[16,16,1024]{2,1,0:T(8,128)(2,1)S(1)}, u32[]{:S(2)}, u32[]{:S(2)}) collective-permute-start(bf16[16,16,1024]{2,1,0:T(8,128)(2,1)S(1)} %get-tuple-element.42), channel_id=1, source_target_pairs={{0,1},{1,0},{2,3},{3,2},{4,5},{5,4},{6,7},{7,6},{8,9},{9,8},{10,11... | collective-permute-start | bytes 1572872 | tf_op jit(solution)/shard_map/ppermute | solution.py:504
  69.9 1.6 %collective-permute-start.8 = (bf16[8,16384]{1,0:T(8,128)(2,1)S(1)}, bf16[8,16384]{1,0:T(8,128)(2,1)S(1)}, u32[]{:S(2)}, u32[]{:S(2)}) collective-permute-start(bf16[8,16384]{1,0:T(8,128)(2,1)S(1)} %get-tuple-element.48), channel_id=1, source_target_pairs={{0,1},{1,0},{2,3},{3,2},{4,5},{5,4},{6,7},{7,6},{8,9},{9,8},{10,11... | collective-permute-start | bytes 786440 | tf_op jit(solution)/shard_map/ppermute | solution.py:504

commit v5 on v4

--- a/solution.py
+++ b/solution.py
@@ -120,7 +120,8 @@
 
 def last_order(members):
     size = members // 2
-    return [quarter * size + n for n in range(size) for quarter in (2, 0, 3, 1)]
+    turns = lambda n: (2 * size + n, size - 1 - n, 3 * size + n, 2 * size - 1 - n)
+    return [device for n in range(size) for device in turns(n)]
 
 
 @functools.lru_cache(maxsize=None)
@@ -456,7 +457,7 @@
     for side, (values, gains) in enumerate(((gate, skip), (gate_other, skip_other))):
         for n in range(here):
             high = jnp.bitwise_xor(core, side)
-            total = conv[n, 2 * high].astype(F32) + conv[n, 2 * high + 1].astype(F32)
+            total = conv[n, 2 * high].astype(F32) + conv[here - 1 - n, 2 * high + 1].astype(F32)
             total = total + gains[n] * prod[high * here + n].astype(F32)
             pieces.append((values[n].astype(F32) * total).astype(BF16))
     gated = jnp.concatenate(pieces, axis=0)

time: 72.8 us -> 72.1 us (level)
  no operation moved by 1% of the time
where the time goes in v5:
time: 72.1 us; the launch traced here: 71.7 us
  blocking collectives  20.7 us (29%)
  waiting for transfers between devices  20.3 us (28%)
  starting transfers between devices  13.8 us (19%)
  Pallas kernels  13.6 us (19%)
  local copies, waits for them, and re-layouts  2.14 us (3%)
  other arithmetic  1.06 us (1%)
    all_to_all x1, blocking collectives, local_channels(): lax.all_to_all(total, 'ctx', 0, 0, axis_index_groups=[last_order(members)...  20.7 us
    ppermute x1, waiting for transfers between devices, local_channels(): lax.ppermute(x, 'ctx', [(d, (d + members) % ctx_count) for d in range(ctx...  9.73 us
    all_to_all x2, starting transfers between devices, local_channels(): lax.all_to_all(x, 'ctx', 0, 0, axis_index_groups=halves, tiled=True)  9.44 us
    ppermute x8, waiting for transfers between devices, local_channels(): swap = lambda x: lax.ppermute(x, 'tp', [(0, 1), (1, 0)])  6.41 us
    pallas_call x1, Pallas kernels, transform(): pl.pallas_call(transform_kernel, in_specs=[SMEM] + [ANYWHERE] * (len(piec...  5.35 us
    all_to_all x2, waiting for transfers between devices, local_channels(): lax.all_to_all(x, 'ctx', 0, 0, axis_index_groups=halves, tiled=True)  4.16 us
    pallas_call x2, Pallas kernels, as_rows(): pl.pallas_call(functools.partial(product_kernel, block, len(arrays)), out...  4.13 us
    pallas_call x1, Pallas kernels, arrange_spectrum(): pl.pallas_call(spectrum_kernel, out_shape=jax.ShapeDtypeStruct((2 * chann...  2.9 us
  transfers between devices with their start and end apart: 11, of which 8 were waited for; matrix products, arithmetic and copies ran while one was open for 0% of the time, Pallas kernels for 7%

profile of v5, /device:TPU:0, one launch (start us, length us, event | category | flops | bytes accessed | tf_op | source)
XLA Modules:
  0.0 71.7 jit_solution(6215665645084113956)
XLA Ops:
  0.0 2.3 %shard_map.82 = (bf16[8,16,1024]{2,1,0:T(8,128)(2,1)}, bf16[4,16,1024]{2,1,0:T(8,128)(2,1)}, bf16[2,4,32,1024]{3,2,1,0:T(8,128)(2,1)}) custom-call(s32[1]{0:T(128)} %bitcast.core_ref, bf16[4,32768]{1,0:T(4,128)(2,1)} %refs_0_.1, bf16[4,32768]{1,0:T(4,128)(2,1)} %refs_1_.1, bf16[2,4,64,1024]{3,2,1,0:T(8,128)(2,1)} %in_ref), custom_call_target="tpu_custom_call" | custom-call | flops 1 | bytes 1 | tf_op jit(solution)/shard_map/pallas_call | solution.py:235
  2.3 0.5 collective-permute-start
  2.8 1.2 %collective-permute-done = bf16[4,16,1024]{2,1,0:T(8,128)(2,1)S(1)} collective-permute-done((bf16[4,16,1024]{2,1,0:T(8,128)(2,1)}, bf16[4,16,1024]{2,1,0:T(8,128)(2,1)S(1)}, u32[]{:S(2)}, u32[]{:S(2)}) %collective-permute-start) | collective-permute-done | bytes 131104 | tf_op jit(solution)/shard_map/ppermute | solution.py:505
  4.0 0.7 constant_dynamic-update-slice_fusion.prod
  4.6 0.0 copy-start
  4.6 0.0 copy-start.3
  4.6 0.4 collective-permute-start.1
  5.0 5.9 %all-to-all-start = ((bf16[8,16,1024]{2,1,0:T(8,128)(2,1)}), bf16[8,16,1024]{2,1,0:T(8,128)(2,1)S(1)}, u32[]{:S(2)}, u32[]{:S(2)}) async-start(bf16[8,16,1024]{2,1,0:T(8,128)(2,1)} %constant_dynamic-update-slice_fusion.prod), calls=%async_computation | async-start | bytes 524288 | tf_op jit(solution)/shard_map/all_to_all | solution.py:501
  10.9 0.0 collective-permute-done.1.came_ref
  10.9 0.0 copy-start.4
  10.9 0.8 %copy-done.4 = bf16[2,4,32,1024]{3,2,1,0:T(8,128)(2,1)} copy-done((bf16[2,4,32,1024]{3,2,1,0:T(8,128)(2,1)}, bf16[2,4,32,1024]{3,2,1,0:T(8,128)(2,1)S(1)}, u32[]{:S(2)}) %copy-start.4) | copy-done | bytes 524312
  11.7 2.9 %shard_map.83 = bf16[8,2,32,1024]{3,2,1,0:T(8,128)(2,1)} custom-call(s32[1]{0:T(128)} %bitcast.core_ref, bf16[2,4,64,1024]{3,2,1,0:T(8,128)(2,1)} %in_ref, bf16[2,4,32,1024]{3,2,1,0:T(8,128)(2,1)} %copy-done.4, bf16[256,256]{1,0:T(8,128)(2,1)} %constant.36.clone.order_ref), custom_call_target="tpu_custom_call" | custom-call | flops 1 | bytes 1 | tf_op jit(solution)/shard_map/pallas_call | solution.py:282
  14.6 3.4 %all-to-all-done.refs_0_ = bf16[8,16,1024]{2,1,0:T(8,128)(2,1)S(1)} async-done(((bf16[8,16,1024]{2,1,0:T(8,128)(2,1)}), bf16[8,16,1024]{2,1,0:T(8,128)(2,1)S(1)}, u32[]{:S(2)}, u32[]{:S(2)}) %all-to-all-start) | async-done | bytes 262176 | tf_op jit(solution)/shard_map/all_to_all | solution.py:501
  18.0 3.6 %all-to-all-start.1 = ((bf16[8,2,32,1024]{3,2,1,0:T(8,128)(2,1)}), bf16[8,2,32,1024]{3,2,1,0:T(8,128)(2,1)S(1)}, u32[]{:S(2)}, u32[]{:S(2)}) async-start(bf16[8,2,32,1024]{3,2,1,0:T(8,128)(2,1)} %shard_map.83), calls=%async_computation.1 | async-start | bytes 2097152 | tf_op jit(solution)/shard_map/all_to_all | solution.py:501
  21.6 2.7 %collective-permute-start.3 = (bf16[8,16,1024]{2,1,0:T(8,128)(2,1)S(1)}, bf16[8,16,1024]{2,1,0:T(8,128)(2,1)S(1)}, u32[]{:S(2)}, u32[]{:S(2)}) collective-permute-start(bf16[8,16,1024]{2,1,0:T(8,128)(2,1)S(1)} %all-to-all-done.refs_0_), channel_id=1, source_target_pairs={{0,16},{2,18},{4,20},{6,22},{8,24},{10,26},{12,28},{14,30},{16,0},... | collective-permute-start | bytes 786440 | tf_op jit(solution)/shard_map/ppermute | solution.py:502
  24.2 1.9 %shard_map.84 = (bf16[4,16,1024]{2,1,0:T(8,128)(2,1)}, bf16[4,16,1024]{2,1,0:T(8,128)(2,1)}) custom-call(s32[1]{0:T(128)} %bitcast.core_ref, bf16[4,32768]{1,0:T(4,128)(2,1)} %refs_0_.2), custom_call_target="tpu_custom_call" | custom-call | flops 1 | bytes 1 | tf_op jit(solution)/shard_map/pallas_call | solution.py:235
  26.1 0.0 copy-start.1
  26.1 0.1 collective-permute-start.4
  26.2 0.5 collective-permute-start.2
  26.7 0.1 collective-permute-start.5
  26.8 0.0 copy-start.2
  26.8 0.7 copy-done.2
  27.5 0.3 shard_map.85.weight
  27.8 0.3 collective-permute-done.5.skip_other
  28.0 0.0 collective-permute-done.4.gate_other
  28.0 9.7 %collective-permute-done.3.refs_2_ = bf16[8,16,1024]{2,1,0:T(8,128)(2,1)S(1)} collective-permute-done((bf16[8,16,1024]{2,1,0:T(8,128)(2,1)S(1)}, bf16[8,16,1024]{2,1,0:T(8,128)(2,1)S(1)}, u32[]{:S(2)}, u32[]{:S(2)}) %collective-permute-start.3) | collective-permute-done | bytes 262176 | tf_op jit(solution)/shard_map/ppermute | solution.py:502
  37.7 0.0 collective-permute-start.6
  37.8 0.0 collective-permute-done.2.refs_1_
  37.8 1.5 %collective-permute-done.6.refs_3_ = bf16[8,16,1024]{2,1,0:T(8,128)(2,1)S(1)} collective-permute-done((bf16[8,16,1024]{2,1,0:T(8,128)(2,1)S(1)}, bf16[8,16,1024]{2,1,0:T(8,128)(2,1)S(1)}, u32[]{:S(2)}, u32[]{:S(2)}) %collective-permute-start.6) | collective-permute-done | bytes 262176 | tf_op jit(solution)/shard_map/ppermute | solution.py:505
  39.3 0.7 %all-to-all-done.1.refs_4_ = bf16[8,2,32,1024]{3,2,1,0:T(8,128)(2,1)S(1)} async-done(((bf16[8,2,32,1024]{3,2,1,0:T(8,128)(2,1)}), bf16[8,2,32,1024]{3,2,1,0:T(8,128)(2,1)S(1)}, u32[]{:S(2)}, u32[]{:S(2)}) %all-to-all-start.1) | async-done | bytes 1048608 | tf_op jit(solution)/shard_map/all_to_all | solution.py:501
  40.0 5.3 %shard_map.86 = (bf16[16,16,1024]{2,1,0:T(8,128)(2,1)S(1)}, bf16[16,16,1024]{2,1,0:T(8,128)(2,1)S(1)}) custom-call(s32[1]{0:T(128)} %bitcast.1.place_ref, bf16[8,16,1024]{2,1,0:T(8,128)(2,1)S(1)} %all-to-all-done.refs_0_, bf16[8,16,1024]{2,1,0:T(8,128)(2,1)S(1)} %collective-permute-done.2.refs_1_, bf16[8,16,1024]{2,1,0:T(8,128)(2,1)S(1)} %collective-permute-done.3.refs_2_, ...), custom_call_target="tpu_custom_call" | custom-call | flops 1 | bytes 1 | tf_op jit(solution)/shard_map/pallas_call | solution.py:433
  45.4 0.1 collective-permute-start.7
  45.5 1.9 %collective-permute-done.7 = bf16[16,16,1024]{2,1,0:T(8,128)(2,1)S(1)} collective-permute-done((bf16[16,16,1024]{2,1,0:T(8,128)(2,1)S(1)}, bf16[16,16,1024]{2,1,0:T(8,128)(2,1)S(1)}, u32[]{:S(2)}, u32[]{:S(2)}) %collective-permute-start.7) | collective-permute-done | bytes 524320 | tf_op jit(solution)/shard_map/ppermute | solution.py:505
  47.4 0.2 add_convert_fusion
  47.6 20.7 %all_to_all.15 = bf16[16,16,1024]{2,1,0:T(8,128)(2,1)S(1)} all-to-all(bf16[16,16,1024]{2,1,0:T(8,128)(2,1)S(1)} %add_convert_fusion), channel_id=1, replica_groups={{16,6,24,14,18,4,26,12,20,2,28,10,22,0,30,8},{17,7,25,15,19,5,27,13,21,..., dimensions={0} | all-to-all | bytes 1048576 | tf_op jit(solution)/shard_map/all_to_all | solution.py:533
  68.3 0.0 copy-done
  68.3 0.0 copy-done.3
  68.3 0.0 copy-done.1
  68.3 0.9 %shard_map.87 = (bf16[8,16384]{1,0:T(8,128)(2,1)S(1)}, bf16[8,16384]{1,0:T(8,128)(2,1)S(1)}) custom-call(s32[1]{0:T(128)} %bitcast.core_ref, bf16[4,4,16,1024]{3,2,1,0:T(8,128)(2,1)S(1)} %bitcast.3, bf16[8,16,1024]{2,1,0:T(8,128)(2,1)S(1)} %copy-done, bf16[4,16,1024]{2,1,0:T(8,128)(2,1)S(1)} %copy-done.1, ...), custom_call_target="tpu_custom_call" | custom-call | flops 1 | bytes 1 | tf_op jit(solution)/shard_map/pallas_call | solution.py:475
  69.2 0.1 collective-permute-start.8
  69.3 1.5 %collective-permute-done.8 = bf16[8,16384]{1,0:T(8,128)(2,1)S(1)} collective-permute-done((bf16[8,16384]{1,0:T(8,128)(2,1)S(1)}, bf16[8,16384]{1,0:T(8,128)(2,1)S(1)}, u32[]{:S(2)}, u32[]{:S(2)}) %collective-permute-start.8) | collective-permute-done | bytes 262176 | tf_op jit(solution)/shard_map/ppermute | solution.py:505
  70.9 0.8 %pad_maximum_fusion = bf16[8,32768]{1,0:T(8,128)(2,1)} fusion(bf16[8,16384]{1,0:T(8,128)(2,1)S(1)} %get-tuple-element.50, bf16[8,16384]{1,0:T(8,128)(2,1)S(1)} %get-tuple-element.49), kind=kLoop, calls=%fused_computation.1 | loop fusion | flops 1048576 | bytes 1048576 | tf_op jit(solution)/shard_map/concatenate | solution.py:542
  (1 shorter events, 0.0 us)
Async XLA Ops:
  2.3 1.7 %collective-permute-start = (bf16[4,16,1024]{2,1,0:T(8,128)(2,1)}, bf16[4,16,1024]{2,1,0:T(8,128)(2,1)S(1)}, u32[]{:S(2)}, u32[]{:S(2)}) collective-permute-start(bf16[4,16,1024]{2,1,0:T(8,128)(2,1)} %get-tuple-element.28), channel_id=1, source_target_pairs={{0,1},{1,0},{2,3},{3,2},{4,5},{5,4},{6,7},{7,6},{8,9},{9,8},{10,11... | collective-permute-start | bytes 393224 | tf_op jit(solution)/shard_map/ppermute | solution.py:505
  4.6 63.7 %copy-start = (bf16[8,16,1024]{2,1,0:T(8,128)(2,1)S(1)}, bf16[8,16,1024]{2,1,0:T(8,128)(2,1)}, u32[]{:S(2)}) copy-start(bf16[8,16,1024]{2,1,0:T(8,128)(2,1)} %constant_dynamic-update-slice_fusion.prod) | copy-start | bytes 786436
  4.6 63.7 %copy-start.3 = (f32[4]{0:T(128)S(1)}, f32[4]{0:T(128)}, u32[]{:S(2)}) copy-start(f32[4]{0:T(128)} %skip) | copy-start | bytes 52
  4.6 6.3 %collective-permute-start.1 = (bf16[2,4,32,1024]{3,2,1,0:T(8,128)(2,1)}, bf16[2,4,32,1024]{3,2,1,0:T(8,128)(2,1)S(1)}, u32[]{:S(2)}, u32[]{:S(2)}) collective-permute-start(bf16[2,4,32,1024]{3,2,1,0:T(8,128)(2,1)} %get-tuple-element.32), channel_id=1, source_target_pairs={{0,1},{1,0},{2,3},{3,2},{4,5},{5,4},{6,7},{7,6},{8,9},{9,8},{10,11... | collective-permute-start | bytes 1572872 | tf_op jit(solution)/shard_map/ppermute | solution.py:505
  5.0 13.0 %all-to-all-start = ((bf16[8,16,1024]{2,1,0:T(8,128)(2,1)}), bf16[8,16,1024]{2,1,0:T(8,128)(2,1)S(1)}, u32[]{:S(2)}, u32[]{:S(2)}) async-start(bf16[8,16,1024]{2,1,0:T(8,128)(2,1)} %constant_dynamic-update-slice_fusion.prod), calls=%async_computation | async-start | bytes 524288 | tf_op jit(solution)/shard_map/all_to_all | solution.py:501
  10.9 0.8 %copy-start.4 = (bf16[2,4,32,1024]{3,2,1,0:T(8,128)(2,1)}, bf16[2,4,32,1024]{3,2,1,0:T(8,128)(2,1)S(1)}, u32[]{:S(2)}) copy-start(bf16[2,4,32,1024]{3,2,1,0:T(8,128)(2,1)S(1)} %collective-permute-done.1.came_ref) | copy-start | bytes 1572868
  18.0 22.0 %all-to-all-start.1 = ((bf16[8,2,32,1024]{3,2,1,0:T(8,128)(2,1)}), bf16[8,2,32,1024]{3,2,1,0:T(8,128)(2,1)S(1)}, u32[]{:S(2)}, u32[]{:S(2)}) async-start(bf16[8,2,32,1024]{3,2,1,0:T(8,128)(2,1)} %shard_map.83), calls=%async_computation.1 | async-start | bytes 2097152 | tf_op jit(solution)/shard_map/all_to_all | solution.py:501
  21.6 16.2 %collective-permute-start.3 = (bf16[8,16,1024]{2,1,0:T(8,128)(2,1)S(1)}, bf16[8,16,1024]{2,1,0:T(8,128)(2,1)S(1)}, u32[]{:S(2)}, u32[]{:S(2)}) collective-permute-start(bf16[8,16,1024]{2,1,0:T(8,128)(2,1)S(1)} %all-to-all-done.refs_0_), channel_id=1, source_target_pairs={{0,16},{2,18},{4,20},{6,22},{8,24},{10,26},{12,28},{14,30},{16,0},... | collective-permute-start | bytes 786440 | tf_op jit(solution)/shard_map/ppermute | solution.py:502
  26.1 42.2 %copy-start.1 = (bf16[4,16,1024]{2,1,0:T(8,128)(2,1)S(1)}, bf16[4,16,1024]{2,1,0:T(8,128)(2,1)}, u32[]{:S(2)}) copy-start(bf16[4,16,1024]{2,1,0:T(8,128)(2,1)} %get-tuple-element.43.gate) | copy-start | bytes 393220
  26.1 1.9 %collective-permute-start.4 = (bf16[4,16,1024]{2,1,0:T(8,128)(2,1)}, bf16[4,16,1024]{2,1,0:T(8,128)(2,1)S(1)}, u32[]{:S(2)}, u32[]{:S(2)}) collective-permute-start(bf16[4,16,1024]{2,1,0:T(8,128)(2,1)} %get-tuple-element.36), channel_id=1, source_target_pairs={{0,1},{1,0},{2,3},{3,2},{4,5},{5,4},{6,7},{7,6},{8,9},{9,8},{10,11... | collective-permute-start | bytes 393224 | tf_op jit(solution)/shard_map/ppermute | solution.py:505
  26.2 11.5 %collective-permute-start.2 = (bf16[8,16,1024]{2,1,0:T(8,128)(2,1)S(1)}, bf16[8,16,1024]{2,1,0:T(8,128)(2,1)S(1)}, u32[]{:S(2)}, u32[]{:S(2)}) collective-permute-start(bf16[8,16,1024]{2,1,0:T(8,128)(2,1)S(1)} %all-to-all-done.refs_0_), channel_id=1, source_target_pairs={{0,1},{1,0},{2,3},{3,2},{4,5},{5,4},{6,7},{7,6},{8,9},{9,8},{10,11... | collective-permute-start | bytes 786440 | tf_op jit(solution)/shard_map/ppermute | solution.py:505
  26.7 1.3 %collective-permute-start.5 = (f32[4]{0:T(128)}, f32[4]{0:T(128)S(1)}, u32[]{:S(2)}, u32[]{:S(2)}) collective-permute-start(f32[4]{0:T(128)} %skip), channel_id=1, source_target_pairs={{0,1},{1,0},{2,3},{3,2},{4,5},{5,4},{6,7},{7,6},{8,9},{9,8},{10,11... | collective-permute-start | bytes 56 | tf_op jit(solution)/shard_map/ppermute | solution.py:505
  26.8 0.7 copy-start.2
  37.7 1.5 %collective-permute-start.6 = (bf16[8,16,1024]{2,1,0:T(8,128)(2,1)S(1)}, bf16[8,16,1024]{2,1,0:T(8,128)(2,1)S(1)}, u32[]{:S(2)}, u32[]{:S(2)}) collective-permute-start(bf16[8,16,1024]{2,1,0:T(8,128)(2,1)S(1)} %collective-permute-done.3.refs_2_), channel_id=1, source_target_pairs={{0,1},{1,0},{2,3},{3,2},{4,5},{5,4},{6,7},{7,6},{8,9},{9,8},{10,11... | collective-permute-start | bytes 786440 | tf_op jit(solution)/shard_map/ppermute | solution.py:505
  45.4 2.0 %collective-permute-start.7 = (bf16[16,16,1024]{2,1,0:T(8,128)(2,1)S(1)}, bf16[16,16,1024]{2,1,0:T(8,128)(2,1)S(1)}, u32[]{:S(2)}, u32[]{:S(2)}) collective-permute-start(bf16[16,16,1024]{2,1,0:T(8,128)(2,1)S(1)} %get-tuple-element.42), channel_id=1, source_target_pairs={{0,1},{1,0},{2,3},{3,2},{4,5},{5,4},{6,7},{7,6},{8,9},{9,8},{10,11... | collective-permute-start | bytes 1572872 | tf_op jit(solution)/shard_map/ppermute | solution.py:505
  69.2 1.6 %collective-permute-start.8 = (bf16[8,16384]{1,0:T(8,128)(2,1)S(1)}, bf16[8,16384]{1,0:T(8,128)(2,1)S(1)}, u32[]{:S(2)}, u32[]{:S(2)}) collective-permute-start(bf16[8,16384]{1,0:T(8,128)(2,1)S(1)} %get-tuple-element.48), channel_id=1, source_target_pairs={{0,1},{1,0},{2,3},{3,2},{4,5},{5,4},{6,7},{7,6},{8,9},{9,8},{10,11... | collective-permute-start | bytes 786440 | tf_op jit(solution)/shard_map/ppermute | solution.py:505

commit v6 on v5

--- a/solution.py
+++ b/solution.py
@@ -482,6 +482,31 @@
     )(core, conv, prod, gate, gate_other, skip, skip_other, weight)
 
 
+def halves_kernel(core_ref, kept, came, out, sem):
+    half = kept.shape[1]
+    copies = []
+    for n, (ref, side) in enumerate(((kept, core_ref[0]), (came, 1 - core_ref[0]))):
+        target = out.at[:, pl.ds(pl.multiple_of(side * half, half), half)]
+        copies.append(pltpu.make_async_copy(ref, target, sem.at[n]))
+    for copy in copies:
+        copy.start()
+    for copy in copies:
+        copy.wait()
+
+
+def place_halves(core, kept, came):
+    outs, half = kept.shape
+    return pl.pallas_call(
+        halves_kernel,
+        out_shape=jax.ShapeDtypeStruct((outs, 2 * half), BF16),
+        in_specs=[SMEM, VMEM, VMEM],
+        out_specs=ANY,
+        scratch_shapes=[pltpu.SemaphoreType.DMA((2,))],
+        compiler_params=pltpu.CompilerParams(vmem_limit_bytes=4 * MIB),
+        cost_estimate=SMALL,
+    )(core, kept, came)
+
+
 def local_channels(k_feature, v_feature, q_feature, spectrum, skip_gain, out_weight):
     channels, tokens = k_feature.shape
     block = spectrum.shape[3]
@@ -536,10 +561,7 @@
     kept, sent = gate_and_project(
         core, conv, product, gate, gate_other, skip_gain, skip_other, weight
     )
-    came = swap(sent)
-    low = jnp.where(tp == 0, kept, came)
-    high = jnp.where(tp == 0, came, kept)
-    return jnp.concatenate([low, high], axis=1)
+    return place_halves(core, kept, swap(sent))
 
 
 def local(k_feature, v_feature, q_feature, spectrum, skip_gain, out_weight):

time: 72.1 us -> 72 us (level)
  other arithmetic: 1.06 us -> 0.19 us
  Pallas kernels: 13.6 us -> 14.4 us
    concatenate x1 -> x0, other arithmetic: 0.83 us -> none  [local_channels(): return jnp.concatenate([low, high], axis=1)]
    pallas_call x0 -> x1, Pallas kernels: none -> 0.8 us  [place_halves(): pl.pallas_call(halves_kernel, out_shape=jax.ShapeDtypeStruct((outs, 2 * h...]
where the time goes in v6:
time: 72 us; the launch traced here: 71.6 us
  blocking collectives  20.7 us (29%)
  waiting for transfers between devices  20.3 us (28%)
  Pallas kernels  14.4 us (20%)
  starting transfers between devices  13.8 us (19%)
  local copies, waits for them, and re-layouts  2.13 us (3%)
    all_to_all x1, blocking collectives, local_channels(): lax.all_to_all(total, 'ctx', 0, 0, axis_index_groups=[last_order(members)...  20.7 us
    ppermute x1, waiting for transfers between devices, local_channels(): lax.ppermute(x, 'ctx', [(d, (d + members) % ctx_count) for d in range(ctx...  9.74 us
    all_to_all x2, starting transfers between devices, local_channels(): lax.all_to_all(x, 'ctx', 0, 0, axis_index_groups=halves, tiled=True)  9.44 us
    ppermute x8, waiting for transfers between devices, local_channels(): swap = lambda x: lax.ppermute(x, 'tp', [(0, 1), (1, 0)])  6.42 us
    pallas_call x1, Pallas kernels, transform(): pl.pallas_call(transform_kernel, in_specs=[SMEM] + [ANYWHERE] * (len(piec...  5.36 us
    all_to_all x2, waiting for transfers between devices, local_channels(): lax.all_to_all(x, 'ctx', 0, 0, axis_index_groups=halves, tiled=True)  4.18 us
    pallas_call x2, Pallas kernels, as_rows(): pl.pallas_call(functools.partial(product_kernel, block, len(arrays)), out...  4.12 us
    pallas_call x1, Pallas kernels, arrange_spectrum(): pl.pallas_call(spectrum_kernel, out_shape=jax.ShapeDtypeStruct((2 * chann...  2.89 us
  transfers between devices with their start and end apart: 11, of which 8 were waited for; matrix products, arithmetic and copies ran while one was open for 0% of the time, Pallas kernels for 7%

profile of v6, /device:TPU:0, one launch (start us, length us, event | category | flops | bytes accessed | tf_op | source)
XLA Modules:
  0.0 71.6 jit_solution(2274713515152635632)
XLA Ops:
  0.0 2.3 %shard_map.82 = (bf16[8,16,1024]{2,1,0:T(8,128)(2,1)}, bf16[4,16,1024]{2,1,0:T(8,128)(2,1)}, bf16[2,4,32,1024]{3,2,1,0:T(8,128)(2,1)}) custom-call(s32[1]{0:T(128)} %bitcast.core_ref, bf16[4,32768]{1,0:T(4,128)(2,1)} %refs_0_.1, bf16[4,32768]{1,0:T(4,128)(2,1)} %refs_1_.1, bf16[2,4,64,1024]{3,2,1,0:T(8,128)(2,1)} %in_ref), custom_call_target="tpu_custom_call" | custom-call | flops 1 | bytes 1 | tf_op jit(solution)/shard_map/pallas_call | solution.py:235
  2.3 0.5 collective-permute-start
  2.8 1.2 %collective-permute-done = bf16[4,16,1024]{2,1,0:T(8,128)(2,1)S(1)} collective-permute-done((bf16[4,16,1024]{2,1,0:T(8,128)(2,1)}, bf16[4,16,1024]{2,1,0:T(8,128)(2,1)S(1)}, u32[]{:S(2)}, u32[]{:S(2)}) %collective-permute-start) | collective-permute-done | bytes 131104 | tf_op jit(solution)/shard_map/ppermute | solution.py:530
  4.0 0.6 constant_dynamic-update-slice_fusion.prod
  4.6 0.0 copy-start
  4.6 0.0 copy-start.3
  4.6 0.4 collective-permute-start.1
  5.0 5.9 %all-to-all-start = ((bf16[8,16,1024]{2,1,0:T(8,128)(2,1)}), bf16[8,16,1024]{2,1,0:T(8,128)(2,1)S(1)}, u32[]{:S(2)}, u32[]{:S(2)}) async-start(bf16[8,16,1024]{2,1,0:T(8,128)(2,1)} %constant_dynamic-update-slice_fusion.prod), calls=%async_computation | async-start | bytes 524288 | tf_op jit(solution)/shard_map/all_to_all | solution.py:526
  10.9 0.0 collective-permute-done.1.came_ref
  10.9 0.0 copy-start.4
  10.9 0.8 %copy-done.4 = bf16[2,4,32,1024]{3,2,1,0:T(8,128)(2,1)} copy-done((bf16[2,4,32,1024]{3,2,1,0:T(8,128)(2,1)}, bf16[2,4,32,1024]{3,2,1,0:T(8,128)(2,1)S(1)}, u32[]{:S(2)}) %copy-start.4) | copy-done | bytes 524312
  11.7 2.9 %shard_map.83 = bf16[8,2,32,1024]{3,2,1,0:T(8,128)(2,1)} custom-call(s32[1]{0:T(128)} %bitcast.core_ref, bf16[2,4,64,1024]{3,2,1,0:T(8,128)(2,1)} %in_ref, bf16[2,4,32,1024]{3,2,1,0:T(8,128)(2,1)} %copy-done.4, bf16[256,256]{1,0:T(8,128)(2,1)} %constant.36.clone.order_ref), custom_call_target="tpu_custom_call" | custom-call | flops 1 | bytes 1 | tf_op jit(solution)/shard_map/pallas_call | solution.py:282
  14.6 3.4 %all-to-all-done.refs_0_ = bf16[8,16,1024]{2,1,0:T(8,128)(2,1)S(1)} async-done(((bf16[8,16,1024]{2,1,0:T(8,128)(2,1)}), bf16[8,16,1024]{2,1,0:T(8,128)(2,1)S(1)}, u32[]{:S(2)}, u32[]{:S(2)}) %all-to-all-start) | async-done | bytes 262176 | tf_op jit(solution)/shard_map/all_to_all | solution.py:526
  18.0 3.6 %all-to-all-start.1 = ((bf16[8,2,32,1024]{3,2,1,0:T(8,128)(2,1)}), bf16[8,2,32,1024]{3,2,1,0:T(8,128)(2,1)S(1)}, u32[]{:S(2)}, u32[]{:S(2)}) async-start(bf16[8,2,32,1024]{3,2,1,0:T(8,128)(2,1)} %shard_map.83), calls=%async_computation.1 | async-start | bytes 2097152 | tf_op jit(solution)/shard_map/all_to_all | solution.py:526
  21.6 2.7 %collective-permute-start.3 = (bf16[8,16,1024]{2,1,0:T(8,128)(2,1)S(1)}, bf16[8,16,1024]{2,1,0:T(8,128)(2,1)S(1)}, u32[]{:S(2)}, u32[]{:S(2)}) collective-permute-start(bf16[8,16,1024]{2,1,0:T(8,128)(2,1)S(1)} %all-to-all-done.refs_0_), channel_id=1, source_target_pairs={{0,16},{2,18},{4,20},{6,22},{8,24},{10,26},{12,28},{14,30},{16,0},... | collective-permute-start | bytes 786440 | tf_op jit(solution)/shard_map/ppermute | solution.py:527
  24.2 1.9 %shard_map.84 = (bf16[4,16,1024]{2,1,0:T(8,128)(2,1)}, bf16[4,16,1024]{2,1,0:T(8,128)(2,1)}) custom-call(s32[1]{0:T(128)} %bitcast.core_ref, bf16[4,32768]{1,0:T(4,128)(2,1)} %refs_0_.2), custom_call_target="tpu_custom_call" | custom-call | flops 1 | bytes 1 | tf_op jit(solution)/shard_map/pallas_call | solution.py:235
  26.1 0.0 copy-start.1
  26.1 0.1 collective-permute-start.4
  26.2 0.5 collective-permute-start.2
  26.7 0.1 collective-permute-start.5
  26.8 0.0 copy-start.2
  26.8 0.7 copy-done.2
  27.5 0.3 shard_map.85.weight
  27.7 0.3 collective-permute-done.5.skip_other
  28.0 0.0 collective-permute-done.4.gate_other
  28.0 9.7 %collective-permute-done.3.refs_2_ = bf16[8,16,1024]{2,1,0:T(8,128)(2,1)S(1)} collective-permute-done((bf16[8,16,1024]{2,1,0:T(8,128)(2,1)S(1)}, bf16[8,16,1024]{2,1,0:T(8,128)(2,1)S(1)}, u32[]{:S(2)}, u32[]{:S(2)}) %collective-permute-start.3) | collective-permute-done | bytes 262176 | tf_op jit(solution)/shard_map/ppermute | solution.py:527
  37.7 0.0 collective-permute-start.6
  37.7 0.0 collective-permute-done.2.refs_1_
  37.7 1.5 %collective-permute-done.6.refs_3_ = bf16[8,16,1024]{2,1,0:T(8,128)(2,1)S(1)} collective-permute-done((bf16[8,16,1024]{2,1,0:T(8,128)(2,1)S(1)}, bf16[8,16,1024]{2,1,0:T(8,128)(2,1)S(1)}, u32[]{:S(2)}, u32[]{:S(2)}) %collective-permute-start.6) | collective-permute-done | bytes 262176 | tf_op jit(solution)/shard_map/ppermute | solution.py:530
  39.3 0.7 %all-to-all-done.1.refs_4_ = bf16[8,2,32,1024]{3,2,1,0:T(8,128)(2,1)S(1)} async-done(((bf16[8,2,32,1024]{3,2,1,0:T(8,128)(2,1)}), bf16[8,2,32,1024]{3,2,1,0:T(8,128)(2,1)S(1)}, u32[]{:S(2)}, u32[]{:S(2)}) %all-to-all-start.1) | async-done | bytes 1048608 | tf_op jit(solution)/shard_map/all_to_all | solution.py:526
  40.0 5.4 %shard_map.86 = (bf16[16,16,1024]{2,1,0:T(8,128)(2,1)S(1)}, bf16[16,16,1024]{2,1,0:T(8,128)(2,1)S(1)}) custom-call(s32[1]{0:T(128)} %bitcast.1.place_ref, bf16[8,16,1024]{2,1,0:T(8,128)(2,1)S(1)} %all-to-all-done.refs_0_, bf16[8,16,1024]{2,1,0:T(8,128)(2,1)S(1)} %collective-permute-done.2.refs_1_, bf16[8,16,1024]{2,1,0:T(8,128)(2,1)S(1)} %collective-permute-done.3.refs_2_, ...), custom_call_target="tpu_custom_call" | custom-call | flops 1 | bytes 1 | tf_op jit(solution)/shard_map/pallas_call | solution.py:433
  45.4 0.1 collective-permute-start.7
  45.5 1.9 %collective-permute-done.7 = bf16[16,16,1024]{2,1,0:T(8,128)(2,1)S(1)} collective-permute-done((bf16[16,16,1024]{2,1,0:T(8,128)(2,1)S(1)}, bf16[16,16,1024]{2,1,0:T(8,128)(2,1)S(1)}, u32[]{:S(2)}, u32[]{:S(2)}) %collective-permute-start.7) | collective-permute-done | bytes 524320 | tf_op jit(solution)/shard_map/ppermute | solution.py:530
  47.4 0.2 add_convert_fusion
  47.6 20.7 %all_to_all.15 = bf16[16,16,1024]{2,1,0:T(8,128)(2,1)S(1)} all-to-all(bf16[16,16,1024]{2,1,0:T(8,128)(2,1)S(1)} %add_convert_fusion), channel_id=1, replica_groups={{16,6,24,14,18,4,26,12,20,2,28,10,22,0,30,8},{17,7,25,15,19,5,27,13,21,..., dimensions={0} | all-to-all | bytes 1048576 | tf_op jit(solution)/shard_map/all_to_all | solution.py:558
  68.3 0.0 copy-done
  68.3 0.0 copy-done.3
  68.3 0.0 copy-done.1
  68.3 0.9 %shard_map.87 = (bf16[8,16384]{1,0:T(8,128)(2,1)S(1)}, bf16[8,16384]{1,0:T(8,128)(2,1)S(1)}) custom-call(s32[1]{0:T(128)} %bitcast.core_ref, bf16[4,4,16,1024]{3,2,1,0:T(8,128)(2,1)S(1)} %bitcast.3, bf16[8,16,1024]{2,1,0:T(8,128)(2,1)S(1)} %copy-done, bf16[4,16,1024]{2,1,0:T(8,128)(2,1)S(1)} %copy-done.1, ...), custom_call_target="tpu_custom_call" | custom-call | flops 1 | bytes 1 | tf_op jit(solution)/shard_map/pallas_call | solution.py:475
  69.2 0.1 collective-permute-start.8
  69.3 1.5 %collective-permute-done.8.came = bf16[8,16384]{1,0:T(8,128)(2,1)S(1)} collective-permute-done((bf16[8,16384]{1,0:T(8,128)(2,1)S(1)}, bf16[8,16384]{1,0:T(8,128)(2,1)S(1)}, u32[]{:S(2)}, u32[]{:S(2)}) %collective-permute-start.8) | collective-permute-done | bytes 262176 | tf_op jit(solution)/shard_map/ppermute | solution.py:530
  70.8 0.8 %shard_map.88 = bf16[8,32768]{1,0:T(8,128)(2,1)} custom-call(s32[1]{0:T(128)} %bitcast.core_ref, bf16[8,16384]{1,0:T(8,128)(2,1)S(1)} %get-tuple-element.47.kept, bf16[8,16384]{1,0:T(8,128)(2,1)S(1)} %collective-permute-done.8.came), custom_call_target="tpu_custom_call" | custom-call | flops 1 | bytes 1 | tf_op jit(solution)/shard_map/pallas_call | solution.py:499
Async XLA Ops:
  2.3 1.7 %collective-permute-start = (bf16[4,16,1024]{2,1,0:T(8,128)(2,1)}, bf16[4,16,1024]{2,1,0:T(8,128)(2,1)S(1)}, u32[]{:S(2)}, u32[]{:S(2)}) collective-permute-start(bf16[4,16,1024]{2,1,0:T(8,128)(2,1)} %get-tuple-element.28), channel_id=1, source_target_pairs={{0,1},{1,0},{2,3},{3,2},{4,5},{5,4},{6,7},{7,6},{8,9},{9,8},{10,11... | collective-permute-start | bytes 393224 | tf_op jit(solution)/shard_map/ppermute | solution.py:530
  4.6 63.7 %copy-start = (bf16[8,16,1024]{2,1,0:T(8,128)(2,1)S(1)}, bf16[8,16,1024]{2,1,0:T(8,128)(2,1)}, u32[]{:S(2)}) copy-start(bf16[8,16,1024]{2,1,0:T(8,128)(2,1)} %constant_dynamic-update-slice_fusion.prod) | copy-start | bytes 786436
  4.6 63.7 %copy-start.3 = (f32[4]{0:T(128)S(1)}, f32[4]{0:T(128)}, u32[]{:S(2)}) copy-start(f32[4]{0:T(128)} %skip) | copy-start | bytes 52
  4.6 6.3 %collective-permute-start.1 = (bf16[2,4,32,1024]{3,2,1,0:T(8,128)(2,1)}, bf16[2,4,32,1024]{3,2,1,0:T(8,128)(2,1)S(1)}, u32[]{:S(2)}, u32[]{:S(2)}) collective-permute-start(bf16[2,4,32,1024]{3,2,1,0:T(8,128)(2,1)} %get-tuple-element.32), channel_id=1, source_target_pairs={{0,1},{1,0},{2,3},{3,2},{4,5},{5,4},{6,7},{7,6},{8,9},{9,8},{10,11... | collective-permute-start | bytes 1572872 | tf_op jit(solution)/shard_map/ppermute | solution.py:530
  5.0 13.0 %all-to-all-start = ((bf16[8,16,1024]{2,1,0:T(8,128)(2,1)}), bf16[8,16,1024]{2,1,0:T(8,128)(2,1)S(1)}, u32[]{:S(2)}, u32[]{:S(2)}) async-start(bf16[8,16,1024]{2,1,0:T(8,128)(2,1)} %constant_dynamic-update-slice_fusion.prod), calls=%async_computation | async-start | bytes 524288 | tf_op jit(solution)/shard_map/all_to_all | solution.py:526
  10.9 0.8 %copy-start.4 = (bf16[2,4,32,1024]{3,2,1,0:T(8,128)(2,1)}, bf16[2,4,32,1024]{3,2,1,0:T(8,128)(2,1)S(1)}, u32[]{:S(2)}) copy-start(bf16[2,4,32,1024]{3,2,1,0:T(8,128)(2,1)S(1)} %collective-permute-done.1.came_ref) | copy-start | bytes 1572868
  18.0 22.0 %all-to-all-start.1 = ((bf16[8,2,32,1024]{3,2,1,0:T(8,128)(2,1)}), bf16[8,2,32,1024]{3,2,1,0:T(8,128)(2,1)S(1)}, u32[]{:S(2)}, u32[]{:S(2)}) async-start(bf16[8,2,32,1024]{3,2,1,0:T(8,128)(2,1)} %shard_map.83), calls=%async_computation.1 | async-start | bytes 2097152 | tf_op jit(solution)/shard_map/all_to_all | solution.py:526
  21.6 16.2 %collective-permute-start.3 = (bf16[8,16,1024]{2,1,0:T(8,128)(2,1)S(1)}, bf16[8,16,1024]{2,1,0:T(8,128)(2,1)S(1)}, u32[]{:S(2)}, u32[]{:S(2)}) collective-permute-start(bf16[8,16,1024]{2,1,0:T(8,128)(2,1)S(1)} %all-to-all-done.refs_0_), channel_id=1, source_target_pairs={{0,16},{2,18},{4,20},{6,22},{8,24},{10,26},{12,28},{14,30},{16,0},... | collective-permute-start | bytes 786440 | tf_op jit(solution)/shard_map/ppermute | solution.py:527
  26.1 42.2 %copy-start.1 = (bf16[4,16,1024]{2,1,0:T(8,128)(2,1)S(1)}, bf16[4,16,1024]{2,1,0:T(8,128)(2,1)}, u32[]{:S(2)}) copy-start(bf16[4,16,1024]{2,1,0:T(8,128)(2,1)} %get-tuple-element.43.gate) | copy-start | bytes 393220
  26.1 1.9 %collective-permute-start.4 = (bf16[4,16,1024]{2,1,0:T(8,128)(2,1)}, bf16[4,16,1024]{2,1,0:T(8,128)(2,1)S(1)}, u32[]{:S(2)}, u32[]{:S(2)}) collective-permute-start(bf16[4,16,1024]{2,1,0:T(8,128)(2,1)} %get-tuple-element.36), channel_id=1, source_target_pairs={{0,1},{1,0},{2,3},{3,2},{4,5},{5,4},{6,7},{7,6},{8,9},{9,8},{10,11... | collective-permute-start | bytes 393224 | tf_op jit(solution)/shard_map/ppermute | solution.py:530
  26.2 11.6 %collective-permute-start.2 = (bf16[8,16,1024]{2,1,0:T(8,128)(2,1)S(1)}, bf16[8,16,1024]{2,1,0:T(8,128)(2,1)S(1)}, u32[]{:S(2)}, u32[]{:S(2)}) collective-permute-start(bf16[8,16,1024]{2,1,0:T(8,128)(2,1)S(1)} %all-to-all-done.refs_0_), channel_id=1, source_target_pairs={{0,1},{1,0},{2,3},{3,2},{4,5},{5,4},{6,7},{7,6},{8,9},{9,8},{10,11... | collective-permute-start | bytes 786440 | tf_op jit(solution)/shard_map/ppermute | solution.py:530
  26.7 1.3 %collective-permute-start.5 = (f32[4]{0:T(128)}, f32[4]{0:T(128)S(1)}, u32[]{:S(2)}, u32[]{:S(2)}) collective-permute-start(f32[4]{0:T(128)} %skip), channel_id=1, source_target_pairs={{0,1},{1,0},{2,3},{3,2},{4,5},{5,4},{6,7},{7,6},{8,9},{9,8},{10,11... | collective-permute-start | bytes 56 | tf_op jit(solution)/shard_map/ppermute | solution.py:530
  26.8 0.7 copy-start.2
  37.7 1.5 %collective-permute-start.6 = (bf16[8,16,1024]{2,1,0:T(8,128)(2,1)S(1)}, bf16[8,16,1024]{2,1,0:T(8,128)(2,1)S(1)}, u32[]{:S(2)}, u32[]{:S(2)}) collective-permute-start(bf16[8,16,1024]{2,1,0:T(8,128)(2,1)S(1)} %collective-permute-done.3.refs_2_), channel_id=1, source_target_pairs={{0,1},{1,0},{2,3},{3,2},{4,5},{5,4},{6,7},{7,6},{8,9},{9,8},{10,11... | collective-permute-start | bytes 786440 | tf_op jit(solution)/shard_map/ppermute | solution.py:530
  45.4 2.0 %collective-permute-start.7 = (bf16[16,16,1024]{2,1,0:T(8,128)(2,1)S(1)}, bf16[16,16,1024]{2,1,0:T(8,128)(2,1)S(1)}, u32[]{:S(2)}, u32[]{:S(2)}) collective-permute-start(bf16[16,16,1024]{2,1,0:T(8,128)(2,1)S(1)} %get-tuple-element.42), channel_id=1, source_target_pairs={{0,1},{1,0},{2,3},{3,2},{4,5},{5,4},{6,7},{7,6},{8,9},{9,8},{10,11... | collective-permute-start | bytes 1572872 | tf_op jit(solution)/shard_map/ppermute | solution.py:530
  69.2 1.6 %collective-permute-start.8 = (bf16[8,16384]{1,0:T(8,128)(2,1)S(1)}, bf16[8,16384]{1,0:T(8,128)(2,1)S(1)}, u32[]{:S(2)}, u32[]{:S(2)}) collective-permute-start(bf16[8,16384]{1,0:T(8,128)(2,1)S(1)} %get-tuple-element.48), channel_id=1, source_target_pairs={{0,1},{1,0},{2,3},{3,2},{4,5},{5,4},{6,7},{7,6},{8,9},{9,8},{10,11... | collective-permute-start | bytes 786440 | tf_op jit(solution)/shard_map/ppermute | solution.py:530

commit v7 on v6

--- a/solution.py
+++ b/solution.py
@@ -153,7 +153,7 @@
 
             i_out = np.concatenate([by_place(1 - s), by_place(s)])
             cosine, sine = cosine_sine(i_out[:, None] * a[None, :], block)
-            lasts.append(np.concatenate([cosine, -sine], 1))
+            lasts.append(np.concatenate([cosine, -sine], 1) / (block * block))
             coarse = 128 * (np.arange(128) % (block // 128))
             coarses.append(np.stack(cosine_sine(a[:, None] * coarse[None, :], block * block)))
             fines.append(np.stack(cosine_sine(a[:, None] * np.arange(128)[None, :], block * block)))
@@ -407,7 +407,6 @@
         rc, ic, rs, si = turn(shaped, *pair_of(inner, rho, 1))
         backs.append((rc - si, ic + rs))
     mixes = butterflies(backs, 1)
-    scale = 1.0 / (block * block)
     half = last.shape[0] // 2
     copies[-1].wait()
     for q, (real, imag) in enumerate(mixes):
@@ -420,7 +419,7 @@
             ],
             axis=0,
         )
-        out = jnp.dot(last[...], pair, preferred_element_type=F32) * scale
+        out = jnp.dot(last[...], pair, preferred_element_type=F32)
         send[:, :, cut] = out[:half].astype(BF16).reshape(send.shape[0], send.shape[1], quarter)
         keep[:, :, cut] = out[half:].astype(BF16).reshape(keep.shape[0], keep.shape[1], quarter)
 

time: 72 us -> 72 us (level)
  no operation moved by 1% of the time
where the time goes in v7:
time: 72 us; the launch traced here: 71.6 us
  blocking collectives  20.7 us (29%)
  waiting for transfers between devices  20.3 us (28%)
  Pallas kernels  14.4 us (20%)
  starting transfers between devices  13.8 us (19%)
  local copies, waits for them, and re-layouts  2.13 us (3%)
    all_to_all x1, blocking collectives, local_channels(): lax.all_to_all(total, 'ctx', 0, 0, axis_index_groups=[last_order(members)...  20.7 us
    ppermute x1, waiting for transfers between devices, local_channels(): lax.ppermute(x, 'ctx', [(d, (d + members) % ctx_count) for d in range(ctx...  9.74 us
    all_to_all x2, starting transfers between devices, local_channels(): lax.all_to_all(x, 'ctx', 0, 0, axis_index_groups=halves, tiled=True)  9.44 us
    ppermute x8, waiting for transfers between devices, local_channels(): swap = lambda x: lax.ppermute(x, 'tp', [(0, 1), (1, 0)])  6.42 us
    pallas_call x1, Pallas kernels, transform(): pl.pallas_call(transform_kernel, in_specs=[SMEM] + [ANYWHERE] * (len(piec...  5.36 us
    all_to_all x2, waiting for transfers between devices, local_channels(): lax.all_to_all(x, 'ctx', 0, 0, axis_index_groups=halves, tiled=True)  4.18 us
    pallas_call x2, Pallas kernels, as_rows(): pl.pallas_call(functools.partial(product_kernel, block, len(arrays)), out...  4.12 us
    pallas_call x1, Pallas kernels, arrange_spectrum(): pl.pallas_call(spectrum_kernel, out_shape=jax.ShapeDtypeStruct((2 * chann...  2.89 us
  transfers between devices with their start and end apart: 11, of which 8 were waited for; matrix products, arithmetic and copies ran while one was open for 0% of the time, Pallas kernels for 7%

profile of v7, /device:TPU:0, one launch (start us, length us, event | category | flops | bytes accessed | tf_op | source)
XLA Modules:
  0.0 71.6 jit_solution(3879743393293544583)
XLA Ops:
  0.0 2.3 %shard_map.82 = (bf16[8,16,1024]{2,1,0:T(8,128)(2,1)}, bf16[4,16,1024]{2,1,0:T(8,128)(2,1)}, bf16[2,4,32,1024]{3,2,1,0:T(8,128)(2,1)}) custom-call(s32[1]{0:T(128)} %bitcast.core_ref, bf16[4,32768]{1,0:T(4,128)(2,1)} %refs_0_.1, bf16[4,32768]{1,0:T(4,128)(2,1)} %refs_1_.1, bf16[2,4,64,1024]{3,2,1,0:T(8,128)(2,1)} %in_ref), custom_call_target="tpu_custom_call" | custom-call | flops 1 | bytes 1 | tf_op jit(solution)/shard_map/pallas_call | solution.py:235
  2.3 0.5 collective-permute-start
  2.8 1.2 %collective-permute-done = bf16[4,16,1024]{2,1,0:T(8,128)(2,1)S(1)} collective-permute-done((bf16[4,16,1024]{2,1,0:T(8,128)(2,1)}, bf16[4,16,1024]{2,1,0:T(8,128)(2,1)S(1)}, u32[]{:S(2)}, u32[]{:S(2)}) %collective-permute-start) | collective-permute-done | bytes 131104 | tf_op jit(solution)/shard_map/ppermute | solution.py:529
  4.0 0.6 constant_dynamic-update-slice_fusion.prod
  4.6 0.0 copy-start
  4.6 0.0 copy-start.3
  4.6 0.4 collective-permute-start.1
  5.0 5.9 %all-to-all-start = ((bf16[8,16,1024]{2,1,0:T(8,128)(2,1)}), bf16[8,16,1024]{2,1,0:T(8,128)(2,1)S(1)}, u32[]{:S(2)}, u32[]{:S(2)}) async-start(bf16[8,16,1024]{2,1,0:T(8,128)(2,1)} %constant_dynamic-update-slice_fusion.prod), calls=%async_computation | async-start | bytes 524288 | tf_op jit(solution)/shard_map/all_to_all | solution.py:525
  10.9 0.0 collective-permute-done.1.came_ref
  10.9 0.0 copy-start.4
  10.9 0.8 %copy-done.4 = bf16[2,4,32,1024]{3,2,1,0:T(8,128)(2,1)} copy-done((bf16[2,4,32,1024]{3,2,1,0:T(8,128)(2,1)}, bf16[2,4,32,1024]{3,2,1,0:T(8,128)(2,1)S(1)}, u32[]{:S(2)}) %copy-start.4) | copy-done | bytes 524312
  11.7 2.9 %shard_map.83 = bf16[8,2,32,1024]{3,2,1,0:T(8,128)(2,1)} custom-call(s32[1]{0:T(128)} %bitcast.core_ref, bf16[2,4,64,1024]{3,2,1,0:T(8,128)(2,1)} %in_ref, bf16[2,4,32,1024]{3,2,1,0:T(8,128)(2,1)} %copy-done.4, bf16[256,256]{1,0:T(8,128)(2,1)} %constant.36.clone.order_ref), custom_call_target="tpu_custom_call" | custom-call | flops 1 | bytes 1 | tf_op jit(solution)/shard_map/pallas_call | solution.py:282
  14.6 3.4 %all-to-all-done.refs_0_ = bf16[8,16,1024]{2,1,0:T(8,128)(2,1)S(1)} async-done(((bf16[8,16,1024]{2,1,0:T(8,128)(2,1)}), bf16[8,16,1024]{2,1,0:T(8,128)(2,1)S(1)}, u32[]{:S(2)}, u32[]{:S(2)}) %all-to-all-start) | async-done | bytes 262176 | tf_op jit(solution)/shard_map/all_to_all | solution.py:525
  18.0 3.6 %all-to-all-start.1 = ((bf16[8,2,32,1024]{3,2,1,0:T(8,128)(2,1)}), bf16[8,2,32,1024]{3,2,1,0:T(8,128)(2,1)S(1)}, u32[]{:S(2)}, u32[]{:S(2)}) async-start(bf16[8,2,32,1024]{3,2,1,0:T(8,128)(2,1)} %shard_map.83), calls=%async_computation.1 | async-start | bytes 2097152 | tf_op jit(solution)/shard_map/all_to_all | solution.py:525
  21.6 2.7 %collective-permute-start.3 = (bf16[8,16,1024]{2,1,0:T(8,128)(2,1)S(1)}, bf16[8,16,1024]{2,1,0:T(8,128)(2,1)S(1)}, u32[]{:S(2)}, u32[]{:S(2)}) collective-permute-start(bf16[8,16,1024]{2,1,0:T(8,128)(2,1)S(1)} %all-to-all-done.refs_0_), channel_id=1, source_target_pairs={{0,16},{2,18},{4,20},{6,22},{8,24},{10,26},{12,28},{14,30},{16,0},... | collective-permute-start | bytes 786440 | tf_op jit(solution)/shard_map/ppermute | solution.py:526
  24.2 1.9 %shard_map.84 = (bf16[4,16,1024]{2,1,0:T(8,128)(2,1)}, bf16[4,16,1024]{2,1,0:T(8,128)(2,1)}) custom-call(s32[1]{0:T(128)} %bitcast.core_ref, bf16[4,32768]{1,0:T(4,128)(2,1)} %refs_0_.2), custom_call_target="tpu_custom_call" | custom-call | flops 1 | bytes 1 | tf_op jit(solution)/shard_map/pallas_call | solution.py:235
  26.1 0.0 copy-start.1
  26.1 0.1 collective-permute-start.4
  26.2 0.5 collective-permute-start.2
  26.7 0.1 collective-permute-start.5
  26.8 0.0 copy-start.2
  26.8 0.7 copy-done.2
  27.5 0.3 shard_map.85.weight
  27.7 0.3 collective-permute-done.5.skip_other
  28.0 0.0 collective-permute-done.4.gate_other
  28.0 9.7 %collective-permute-done.3.refs_2_ = bf16[8,16,1024]{2,1,0:T(8,128)(2,1)S(1)} collective-permute-done((bf16[8,16,1024]{2,1,0:T(8,128)(2,1)S(1)}, bf16[8,16,1024]{2,1,0:T(8,128)(2,1)S(1)}, u32[]{:S(2)}, u32[]{:S(2)}) %collective-permute-start.3) | collective-permute-done | bytes 262176 | tf_op jit(solution)/shard_map/ppermute | solution.py:526
  37.7 0.0 collective-permute-start.6
  37.7 0.0 collective-permute-done.2.refs_1_
  37.7 1.5 %collective-permute-done.6.refs_3_ = bf16[8,16,1024]{2,1,0:T(8,128)(2,1)S(1)} collective-permute-done((bf16[8,16,1024]{2,1,0:T(8,128)(2,1)S(1)}, bf16[8,16,1024]{2,1,0:T(8,128)(2,1)S(1)}, u32[]{:S(2)}, u32[]{:S(2)}) %collective-permute-start.6) | collective-permute-done | bytes 262176 | tf_op jit(solution)/shard_map/ppermute | solution.py:529
  39.3 0.7 %all-to-all-done.1.refs_4_ = bf16[8,2,32,1024]{3,2,1,0:T(8,128)(2,1)S(1)} async-done(((bf16[8,2,32,1024]{3,2,1,0:T(8,128)(2,1)}), bf16[8,2,32,1024]{3,2,1,0:T(8,128)(2,1)S(1)}, u32[]{:S(2)}, u32[]{:S(2)}) %all-to-all-start.1) | async-done | bytes 1048608 | tf_op jit(solution)/shard_map/all_to_all | solution.py:525
  40.0 5.4 %shard_map.86 = (bf16[16,16,1024]{2,1,0:T(8,128)(2,1)S(1)}, bf16[16,16,1024]{2,1,0:T(8,128)(2,1)S(1)}) custom-call(s32[1]{0:T(128)} %bitcast.1.place_ref, bf16[8,16,1024]{2,1,0:T(8,128)(2,1)S(1)} %all-to-all-done.refs_0_, bf16[8,16,1024]{2,1,0:T(8,128)(2,1)S(1)} %collective-permute-done.2.refs_1_, bf16[8,16,1024]{2,1,0:T(8,128)(2,1)S(1)} %collective-permute-done.3.refs_2_, ...), custom_call_target="tpu_custom_call" | custom-call | flops 1 | bytes 1 | tf_op jit(solution)/shard_map/pallas_call | solution.py:432
  45.4 0.1 collective-permute-start.7
  45.5 1.9 %collective-permute-done.7 = bf16[16,16,1024]{2,1,0:T(8,128)(2,1)S(1)} collective-permute-done((bf16[16,16,1024]{2,1,0:T(8,128)(2,1)S(1)}, bf16[16,16,1024]{2,1,0:T(8,128)(2,1)S(1)}, u32[]{:S(2)}, u32[]{:S(2)}) %collective-permute-start.7) | collective-permute-done | bytes 524320 | tf_op jit(solution)/shard_map/ppermute | solution.py:529
  47.4 0.2 add_convert_fusion
  47.6 20.7 %all_to_all.15 = bf16[16,16,1024]{2,1,0:T(8,128)(2,1)S(1)} all-to-all(bf16[16,16,1024]{2,1,0:T(8,128)(2,1)S(1)} %add_convert_fusion), channel_id=1, replica_groups={{16,6,24,14,18,4,26,12,20,2,28,10,22,0,30,8},{17,7,25,15,19,5,27,13,21,..., dimensions={0} | all-to-all | bytes 1048576 | tf_op jit(solution)/shard_map/all_to_all | solution.py:557
  68.3 0.0 copy-done
  68.3 0.0 copy-done.3
  68.3 0.0 copy-done.1
  68.3 0.9 %shard_map.87 = (bf16[8,16384]{1,0:T(8,128)(2,1)S(1)}, bf16[8,16384]{1,0:T(8,128)(2,1)S(1)}) custom-call(s32[1]{0:T(128)} %bitcast.core_ref, bf16[4,4,16,1024]{3,2,1,0:T(8,128)(2,1)S(1)} %bitcast.3, bf16[8,16,1024]{2,1,0:T(8,128)(2,1)S(1)} %copy-done, bf16[4,16,1024]{2,1,0:T(8,128)(2,1)S(1)} %copy-done.1, ...), custom_call_target="tpu_custom_call" | custom-call | flops 1 | bytes 1 | tf_op jit(solution)/shard_map/pallas_call | solution.py:474
  69.2 0.1 collective-permute-start.8
  69.3 1.5 %collective-permute-done.8.came = bf16[8,16384]{1,0:T(8,128)(2,1)S(1)} collective-permute-done((bf16[8,16384]{1,0:T(8,128)(2,1)S(1)}, bf16[8,16384]{1,0:T(8,128)(2,1)S(1)}, u32[]{:S(2)}, u32[]{:S(2)}) %collective-permute-start.8) | collective-permute-done | bytes 262176 | tf_op jit(solution)/shard_map/ppermute | solution.py:529
  70.8 0.8 %shard_map.88 = bf16[8,32768]{1,0:T(8,128)(2,1)} custom-call(s32[1]{0:T(128)} %bitcast.core_ref, bf16[8,16384]{1,0:T(8,128)(2,1)S(1)} %get-tuple-element.47.kept, bf16[8,16384]{1,0:T(8,128)(2,1)S(1)} %collective-permute-done.8.came), custom_call_target="tpu_custom_call" | custom-call | flops 1 | bytes 1 | tf_op jit(solution)/shard_map/pallas_call | solution.py:498
Async XLA Ops:
  2.3 1.7 %collective-permute-start = (bf16[4,16,1024]{2,1,0:T(8,128)(2,1)}, bf16[4,16,1024]{2,1,0:T(8,128)(2,1)S(1)}, u32[]{:S(2)}, u32[]{:S(2)}) collective-permute-start(bf16[4,16,1024]{2,1,0:T(8,128)(2,1)} %get-tuple-element.28), channel_id=1, source_target_pairs={{0,1},{1,0},{2,3},{3,2},{4,5},{5,4},{6,7},{7,6},{8,9},{9,8},{10,11... | collective-permute-start | bytes 393224 | tf_op jit(solution)/shard_map/ppermute | solution.py:529
  4.6 63.7 %copy-start = (bf16[8,16,1024]{2,1,0:T(8,128)(2,1)S(1)}, bf16[8,16,1024]{2,1,0:T(8,128)(2,1)}, u32[]{:S(2)}) copy-start(bf16[8,16,1024]{2,1,0:T(8,128)(2,1)} %constant_dynamic-update-slice_fusion.prod) | copy-start | bytes 786436
  4.6 63.7 %copy-start.3 = (f32[4]{0:T(128)S(1)}, f32[4]{0:T(128)}, u32[]{:S(2)}) copy-start(f32[4]{0:T(128)} %skip) | copy-start | bytes 52
  4.6 6.3 %collective-permute-start.1 = (bf16[2,4,32,1024]{3,2,1,0:T(8,128)(2,1)}, bf16[2,4,32,1024]{3,2,1,0:T(8,128)(2,1)S(1)}, u32[]{:S(2)}, u32[]{:S(2)}) collective-permute-start(bf16[2,4,32,1024]{3,2,1,0:T(8,128)(2,1)} %get-tuple-element.32), channel_id=1, source_target_pairs={{0,1},{1,0},{2,3},{3,2},{4,5},{5,4},{6,7},{7,6},{8,9},{9,8},{10,11... | collective-permute-start | bytes 1572872 | tf_op jit(solution)/shard_map/ppermute | solution.py:529
  5.0 13.0 %all-to-all-start = ((bf16[8,16,1024]{2,1,0:T(8,128)(2,1)}), bf16[8,16,1024]{2,1,0:T(8,128)(2,1)S(1)}, u32[]{:S(2)}, u32[]{:S(2)}) async-start(bf16[8,16,1024]{2,1,0:T(8,128)(2,1)} %constant_dynamic-update-slice_fusion.prod), calls=%async_computation | async-start | bytes 524288 | tf_op jit(solution)/shard_map/all_to_all | solution.py:525
  10.9 0.8 %copy-start.4 = (bf16[2,4,32,1024]{3,2,1,0:T(8,128)(2,1)}, bf16[2,4,32,1024]{3,2,1,0:T(8,128)(2,1)S(1)}, u32[]{:S(2)}) copy-start(bf16[2,4,32,1024]{3,2,1,0:T(8,128)(2,1)S(1)} %collective-permute-done.1.came_ref) | copy-start | bytes 1572868
  18.0 22.0 %all-to-all-start.1 = ((bf16[8,2,32,1024]{3,2,1,0:T(8,128)(2,1)}), bf16[8,2,32,1024]{3,2,1,0:T(8,128)(2,1)S(1)}, u32[]{:S(2)}, u32[]{:S(2)}) async-start(bf16[8,2,32,1024]{3,2,1,0:T(8,128)(2,1)} %shard_map.83), calls=%async_computation.1 | async-start | bytes 2097152 | tf_op jit(solution)/shard_map/all_to_all | solution.py:525
  21.6 16.2 %collective-permute-start.3 = (bf16[8,16,1024]{2,1,0:T(8,128)(2,1)S(1)}, bf16[8,16,1024]{2,1,0:T(8,128)(2,1)S(1)}, u32[]{:S(2)}, u32[]{:S(2)}) collective-permute-start(bf16[8,16,1024]{2,1,0:T(8,128)(2,1)S(1)} %all-to-all-done.refs_0_), channel_id=1, source_target_pairs={{0,16},{2,18},{4,20},{6,22},{8,24},{10,26},{12,28},{14,30},{16,0},... | collective-permute-start | bytes 786440 | tf_op jit(solution)/shard_map/ppermute | solution.py:526
  26.1 42.2 %copy-start.1 = (bf16[4,16,1024]{2,1,0:T(8,128)(2,1)S(1)}, bf16[4,16,1024]{2,1,0:T(8,128)(2,1)}, u32[]{:S(2)}) copy-start(bf16[4,16,1024]{2,1,0:T(8,128)(2,1)} %get-tuple-element.43.gate) | copy-start | bytes 393220
  26.1 1.9 %collective-permute-start.4 = (bf16[4,16,1024]{2,1,0:T(8,128)(2,1)}, bf16[4,16,1024]{2,1,0:T(8,128)(2,1)S(1)}, u32[]{:S(2)}, u32[]{:S(2)}) collective-permute-start(bf16[4,16,1024]{2,1,0:T(8,128)(2,1)} %get-tuple-element.36), channel_id=1, source_target_pairs={{0,1},{1,0},{2,3},{3,2},{4,5},{5,4},{6,7},{7,6},{8,9},{9,8},{10,11... | collective-permute-start | bytes 393224 | tf_op jit(solution)/shard_map/ppermute | solution.py:529
  26.2 11.6 %collective-permute-start.2 = (bf16[8,16,1024]{2,1,0:T(8,128)(2,1)S(1)}, bf16[8,16,1024]{2,1,0:T(8,128)(2,1)S(1)}, u32[]{:S(2)}, u32[]{:S(2)}) collective-permute-start(bf16[8,16,1024]{2,1,0:T(8,128)(2,1)S(1)} %all-to-all-done.refs_0_), channel_id=1, source_target_pairs={{0,1},{1,0},{2,3},{3,2},{4,5},{5,4},{6,7},{7,6},{8,9},{9,8},{10,11... | collective-permute-start | bytes 786440 | tf_op jit(solution)/shard_map/ppermute | solution.py:529
  26.7 1.3 %collective-permute-start.5 = (f32[4]{0:T(128)}, f32[4]{0:T(128)S(1)}, u32[]{:S(2)}, u32[]{:S(2)}) collective-permute-start(f32[4]{0:T(128)} %skip), channel_id=1, source_target_pairs={{0,1},{1,0},{2,3},{3,2},{4,5},{5,4},{6,7},{7,6},{8,9},{9,8},{10,11... | collective-permute-start | bytes 56 | tf_op jit(solution)/shard_map/ppermute | solution.py:529
  26.8 0.7 copy-start.2
  37.7 1.5 %collective-permute-start.6 = (bf16[8,16,1024]{2,1,0:T(8,128)(2,1)S(1)}, bf16[8,16,1024]{2,1,0:T(8,128)(2,1)S(1)}, u32[]{:S(2)}, u32[]{:S(2)}) collective-permute-start(bf16[8,16,1024]{2,1,0:T(8,128)(2,1)S(1)} %collective-permute-done.3.refs_2_), channel_id=1, source_target_pairs={{0,1},{1,0},{2,3},{3,2},{4,5},{5,4},{6,7},{7,6},{8,9},{9,8},{10,11... | collective-permute-start | bytes 786440 | tf_op jit(solution)/shard_map/ppermute | solution.py:529
  45.4 2.0 %collective-permute-start.7 = (bf16[16,16,1024]{2,1,0:T(8,128)(2,1)S(1)}, bf16[16,16,1024]{2,1,0:T(8,128)(2,1)S(1)}, u32[]{:S(2)}, u32[]{:S(2)}) collective-permute-start(bf16[16,16,1024]{2,1,0:T(8,128)(2,1)S(1)} %get-tuple-element.42), channel_id=1, source_target_pairs={{0,1},{1,0},{2,3},{3,2},{4,5},{5,4},{6,7},{7,6},{8,9},{9,8},{10,11... | collective-permute-start | bytes 1572872 | tf_op jit(solution)/shard_map/ppermute | solution.py:529
  69.2 1.6 %collective-permute-start.8 = (bf16[8,16384]{1,0:T(8,128)(2,1)S(1)}, bf16[8,16384]{1,0:T(8,128)(2,1)S(1)}, u32[]{:S(2)}, u32[]{:S(2)}) collective-permute-start(bf16[8,16384]{1,0:T(8,128)(2,1)S(1)} %get-tuple-element.48), channel_id=1, source_target_pairs={{0,1},{1,0},{2,3},{3,2},{4,5},{5,4},{6,7},{7,6},{8,9},{9,8},{10,11... | collective-permute-start | bytes 786440 | tf_op jit(solution)/shard_map/ppermute | solution.py:529

commit v8 on v6

--- a/solution.py
+++ b/solution.py
@@ -120,7 +120,7 @@
 
 def last_order(members):
     size = members // 2
-    turns = lambda n: (2 * size + n, size - 1 - n, 3 * size + n, 2 * size - 1 - n)
+    turns = lambda n: (2 * size + n, 4 * size - 1 - n, n, 2 * size - 1 - n)
     return [device for n in range(size) for device in turns(n)]
 
 
@@ -457,7 +457,8 @@
     for side, (values, gains) in enumerate(((gate, skip), (gate_other, skip_other))):
         for n in range(here):
             high = jnp.bitwise_xor(core, side)
-            total = conv[n, 2 * high].astype(F32) + conv[here - 1 - n, 2 * high + 1].astype(F32)
+            at = jnp.where(high == 0, n, here - 1 - n)
+            total = conv[at, high].astype(F32) + conv[at, 2 + high].astype(F32)
             total = total + gains[n] * prod[high * here + n].astype(F32)
             pieces.append((values[n].astype(F32) * total).astype(BF16))
     gated = jnp.concatenate(pieces, axis=0)

time: 72 us -> 71.9 us (level)
  no operation moved by 1% of the time
where the time goes in v8:
time: 71.9 us; the launch traced here: 71.5 us
  blocking collectives  20.6 us (29%)
  waiting for transfers between devices  20.3 us (28%)
  Pallas kernels  14.4 us (20%)
  starting transfers between devices  13.8 us (19%)
  local copies, waits for them, and re-layouts  2.13 us (3%)
    all_to_all x1, blocking collectives, local_channels(): lax.all_to_all(total, 'ctx', 0, 0, axis_index_groups=[last_order(members)...  20.6 us
    ppermute x1, waiting for transfers between devices, local_channels(): lax.ppermute(x, 'ctx', [(d, (d + members) % ctx_count) for d in range(ctx...  9.74 us
    all_to_all x2, starting transfers between devices, local_channels(): lax.all_to_all(x, 'ctx', 0, 0, axis_index_groups=halves, tiled=True)  9.44 us
    ppermute x8, waiting for transfers between devices, local_channels(): swap = lambda x: lax.ppermute(x, 'tp', [(0, 1), (1, 0)])  6.42 us
    pallas_call x1, Pallas kernels, transform(): pl.pallas_call(transform_kernel, in_specs=[SMEM] + [ANYWHERE] * (len(piec...  5.36 us
    all_to_all x2, waiting for transfers between devices, local_channels(): lax.all_to_all(x, 'ctx', 0, 0, axis_index_groups=halves, tiled=True)  4.18 us
    pallas_call x2, Pallas kernels, as_rows(): pl.pallas_call(functools.partial(product_kernel, block, len(arrays)), out...  4.12 us
    pallas_call x1, Pallas kernels, arrange_spectrum(): pl.pallas_call(spectrum_kernel, out_shape=jax.ShapeDtypeStruct((2 * chann...  2.89 us
  transfers between devices with their start and end apart: 11, of which 8 were waited for; matrix products, arithmetic and copies ran while one was open for 0% of the time, Pallas kernels for 7%

profile of v8, /device:TPU:0, one launch (start us, length us, event | category | flops | bytes accessed | tf_op | source)
XLA Modules:
  0.0 71.5 jit_solution(3099479644446453288)
XLA Ops:
  0.0 2.3 %shard_map.82 = (bf16[8,16,1024]{2,1,0:T(8,128)(2,1)}, bf16[4,16,1024]{2,1,0:T(8,128)(2,1)}, bf16[2,4,32,1024]{3,2,1,0:T(8,128)(2,1)}) custom-call(s32[1]{0:T(128)} %bitcast.core_ref, bf16[4,32768]{1,0:T(4,128)(2,1)} %refs_0_.1, bf16[4,32768]{1,0:T(4,128)(2,1)} %refs_1_.1, bf16[2,4,64,1024]{3,2,1,0:T(8,128)(2,1)} %in_ref), custom_call_target="tpu_custom_call" | custom-call | flops 1 | bytes 1 | tf_op jit(solution)/shard_map/pallas_call | solution.py:235
  2.3 0.5 collective-permute-start
  2.8 1.2 %collective-permute-done = bf16[4,16,1024]{2,1,0:T(8,128)(2,1)S(1)} collective-permute-done((bf16[4,16,1024]{2,1,0:T(8,128)(2,1)}, bf16[4,16,1024]{2,1,0:T(8,128)(2,1)S(1)}, u32[]{:S(2)}, u32[]{:S(2)}) %collective-permute-start) | collective-permute-done | bytes 131104 | tf_op jit(solution)/shard_map/ppermute | solution.py:531
  4.0 0.6 constant_dynamic-update-slice_fusion.prod
  4.6 0.0 copy-start
  4.6 0.0 copy-start.3
  4.6 0.4 collective-permute-start.1
  5.0 5.9 %all-to-all-start = ((bf16[8,16,1024]{2,1,0:T(8,128)(2,1)}), bf16[8,16,1024]{2,1,0:T(8,128)(2,1)S(1)}, u32[]{:S(2)}, u32[]{:S(2)}) async-start(bf16[8,16,1024]{2,1,0:T(8,128)(2,1)} %constant_dynamic-update-slice_fusion.prod), calls=%async_computation | async-start | bytes 524288 | tf_op jit(solution)/shard_map/all_to_all | solution.py:527
  10.9 0.0 collective-permute-done.1.came_ref
  10.9 0.0 copy-start.4
  10.9 0.8 %copy-done.4 = bf16[2,4,32,1024]{3,2,1,0:T(8,128)(2,1)} copy-done((bf16[2,4,32,1024]{3,2,1,0:T(8,128)(2,1)}, bf16[2,4,32,1024]{3,2,1,0:T(8,128)(2,1)S(1)}, u32[]{:S(2)}) %copy-start.4) | copy-done | bytes 524312
  11.7 2.9 %shard_map.83 = bf16[8,2,32,1024]{3,2,1,0:T(8,128)(2,1)} custom-call(s32[1]{0:T(128)} %bitcast.core_ref, bf16[2,4,64,1024]{3,2,1,0:T(8,128)(2,1)} %in_ref, bf16[2,4,32,1024]{3,2,1,0:T(8,128)(2,1)} %copy-done.4, bf16[256,256]{1,0:T(8,128)(2,1)} %constant.36.clone.order_ref), custom_call_target="tpu_custom_call" | custom-call | flops 1 | bytes 1 | tf_op jit(solution)/shard_map/pallas_call | solution.py:282
  14.6 3.4 %all-to-all-done.refs_0_ = bf16[8,16,1024]{2,1,0:T(8,128)(2,1)S(1)} async-done(((bf16[8,16,1024]{2,1,0:T(8,128)(2,1)}), bf16[8,16,1024]{2,1,0:T(8,128)(2,1)S(1)}, u32[]{:S(2)}, u32[]{:S(2)}) %all-to-all-start) | async-done | bytes 262176 | tf_op jit(solution)/shard_map/all_to_all | solution.py:527
  18.0 3.6 %all-to-all-start.1 = ((bf16[8,2,32,1024]{3,2,1,0:T(8,128)(2,1)}), bf16[8,2,32,1024]{3,2,1,0:T(8,128)(2,1)S(1)}, u32[]{:S(2)}, u32[]{:S(2)}) async-start(bf16[8,2,32,1024]{3,2,1,0:T(8,128)(2,1)} %shard_map.83), calls=%async_computation.1 | async-start | bytes 2097152 | tf_op jit(solution)/shard_map/all_to_all | solution.py:527
  21.6 2.7 %collective-permute-start.3 = (bf16[8,16,1024]{2,1,0:T(8,128)(2,1)S(1)}, bf16[8,16,1024]{2,1,0:T(8,128)(2,1)S(1)}, u32[]{:S(2)}, u32[]{:S(2)}) collective-permute-start(bf16[8,16,1024]{2,1,0:T(8,128)(2,1)S(1)} %all-to-all-done.refs_0_), channel_id=1, source_target_pairs={{0,16},{2,18},{4,20},{6,22},{8,24},{10,26},{12,28},{14,30},{16,0},... | collective-permute-start | bytes 786440 | tf_op jit(solution)/shard_map/ppermute | solution.py:528
  24.2 1.9 %shard_map.84 = (bf16[4,16,1024]{2,1,0:T(8,128)(2,1)}, bf16[4,16,1024]{2,1,0:T(8,128)(2,1)}) custom-call(s32[1]{0:T(128)} %bitcast.core_ref, bf16[4,32768]{1,0:T(4,128)(2,1)} %refs_0_.2), custom_call_target="tpu_custom_call" | custom-call | flops 1 | bytes 1 | tf_op jit(solution)/shard_map/pallas_call | solution.py:235
  26.1 0.0 copy-start.1
  26.1 0.1 collective-permute-start.4
  26.2 0.5 collective-permute-start.2
  26.7 0.1 collective-permute-start.5
  26.8 0.0 copy-start.2
  26.8 0.7 copy-done.2
  27.5 0.3 shard_map.85.weight
  27.7 0.3 collective-permute-done.5.skip_other
  28.0 0.0 collective-permute-done.4.gate_other
  28.0 9.7 %collective-permute-done.3.refs_2_ = bf16[8,16,1024]{2,1,0:T(8,128)(2,1)S(1)} collective-permute-done((bf16[8,16,1024]{2,1,0:T(8,128)(2,1)S(1)}, bf16[8,16,1024]{2,1,0:T(8,128)(2,1)S(1)}, u32[]{:S(2)}, u32[]{:S(2)}) %collective-permute-start.3) | collective-permute-done | bytes 262176 | tf_op jit(solution)/shard_map/ppermute | solution.py:528
  37.7 0.0 collective-permute-start.6
  37.7 0.0 collective-permute-done.2.refs_1_
  37.7 1.5 %collective-permute-done.6.refs_3_ = bf16[8,16,1024]{2,1,0:T(8,128)(2,1)S(1)} collective-permute-done((bf16[8,16,1024]{2,1,0:T(8,128)(2,1)S(1)}, bf16[8,16,1024]{2,1,0:T(8,128)(2,1)S(1)}, u32[]{:S(2)}, u32[]{:S(2)}) %collective-permute-start.6) | collective-permute-done | bytes 262176 | tf_op jit(solution)/shard_map/ppermute | solution.py:531
  39.3 0.7 %all-to-all-done.1.refs_4_ = bf16[8,2,32,1024]{3,2,1,0:T(8,128)(2,1)S(1)} async-done(((bf16[8,2,32,1024]{3,2,1,0:T(8,128)(2,1)}), bf16[8,2,32,1024]{3,2,1,0:T(8,128)(2,1)S(1)}, u32[]{:S(2)}, u32[]{:S(2)}) %all-to-all-start.1) | async-done | bytes 1048608 | tf_op jit(solution)/shard_map/all_to_all | solution.py:527
  40.0 5.4 %shard_map.86 = (bf16[16,16,1024]{2,1,0:T(8,128)(2,1)S(1)}, bf16[16,16,1024]{2,1,0:T(8,128)(2,1)S(1)}) custom-call(s32[1]{0:T(128)} %bitcast.1.place_ref, bf16[8,16,1024]{2,1,0:T(8,128)(2,1)S(1)} %all-to-all-done.refs_0_, bf16[8,16,1024]{2,1,0:T(8,128)(2,1)S(1)} %collective-permute-done.2.refs_1_, bf16[8,16,1024]{2,1,0:T(8,128)(2,1)S(1)} %collective-permute-done.3.refs_2_, ...), custom_call_target="tpu_custom_call" | custom-call | flops 1 | bytes 1 | tf_op jit(solution)/shard_map/pallas_call | solution.py:433
  45.4 0.1 collective-permute-start.7
  45.5 1.9 %collective-permute-done.7 = bf16[16,16,1024]{2,1,0:T(8,128)(2,1)S(1)} collective-permute-done((bf16[16,16,1024]{2,1,0:T(8,128)(2,1)S(1)}, bf16[16,16,1024]{2,1,0:T(8,128)(2,1)S(1)}, u32[]{:S(2)}, u32[]{:S(2)}) %collective-permute-start.7) | collective-permute-done | bytes 524320 | tf_op jit(solution)/shard_map/ppermute | solution.py:531
  47.4 0.2 add_convert_fusion
  47.6 20.6 %all_to_all.15 = bf16[16,16,1024]{2,1,0:T(8,128)(2,1)S(1)} all-to-all(bf16[16,16,1024]{2,1,0:T(8,128)(2,1)S(1)} %add_convert_fusion), channel_id=1, replica_groups={{16,30,0,14,18,28,2,12,20,26,4,10,22,24,6,8},{17,31,1,15,19,29,3,13,21,..., dimensions={0} | all-to-all | bytes 1048576 | tf_op jit(solution)/shard_map/all_to_all | solution.py:559
  68.2 0.0 copy-done
  68.2 0.0 copy-done.3
  68.2 0.0 copy-done.1
  68.2 0.9 %shard_map.87 = (bf16[8,16384]{1,0:T(8,128)(2,1)S(1)}, bf16[8,16384]{1,0:T(8,128)(2,1)S(1)}) custom-call(s32[1]{0:T(128)} %bitcast.core_ref, bf16[4,4,16,1024]{3,2,1,0:T(8,128)(2,1)S(1)} %bitcast.3, bf16[8,16,1024]{2,1,0:T(8,128)(2,1)S(1)} %copy-done, bf16[4,16,1024]{2,1,0:T(8,128)(2,1)S(1)} %copy-done.1, ...), custom_call_target="tpu_custom_call" | custom-call | flops 1 | bytes 1 | tf_op jit(solution)/shard_map/pallas_call | solution.py:476
  69.1 0.1 collective-permute-start.8
  69.2 1.5 %collective-permute-done.8.came = bf16[8,16384]{1,0:T(8,128)(2,1)S(1)} collective-permute-done((bf16[8,16384]{1,0:T(8,128)(2,1)S(1)}, bf16[8,16384]{1,0:T(8,128)(2,1)S(1)}, u32[]{:S(2)}, u32[]{:S(2)}) %collective-permute-start.8) | collective-permute-done | bytes 262176 | tf_op jit(solution)/shard_map/ppermute | solution.py:531
  70.7 0.8 %shard_map.88 = bf16[8,32768]{1,0:T(8,128)(2,1)} custom-call(s32[1]{0:T(128)} %bitcast.core_ref, bf16[8,16384]{1,0:T(8,128)(2,1)S(1)} %get-tuple-element.47.kept, bf16[8,16384]{1,0:T(8,128)(2,1)S(1)} %collective-permute-done.8.came), custom_call_target="tpu_custom_call" | custom-call | flops 1 | bytes 1 | tf_op jit(solution)/shard_map/pallas_call | solution.py:500
Async XLA Ops:
  2.3 1.7 %collective-permute-start = (bf16[4,16,1024]{2,1,0:T(8,128)(2,1)}, bf16[4,16,1024]{2,1,0:T(8,128)(2,1)S(1)}, u32[]{:S(2)}, u32[]{:S(2)}) collective-permute-start(bf16[4,16,1024]{2,1,0:T(8,128)(2,1)} %get-tuple-element.28), channel_id=1, source_target_pairs={{0,1},{1,0},{2,3},{3,2},{4,5},{5,4},{6,7},{7,6},{8,9},{9,8},{10,11... | collective-permute-start | bytes 393224 | tf_op jit(solution)/shard_map/ppermute | solution.py:531
  4.6 63.6 %copy-start = (bf16[8,16,1024]{2,1,0:T(8,128)(2,1)S(1)}, bf16[8,16,1024]{2,1,0:T(8,128)(2,1)}, u32[]{:S(2)}) copy-start(bf16[8,16,1024]{2,1,0:T(8,128)(2,1)} %constant_dynamic-update-slice_fusion.prod) | copy-start | bytes 786436
  4.6 63.6 %copy-start.3 = (f32[4]{0:T(128)S(1)}, f32[4]{0:T(128)}, u32[]{:S(2)}) copy-start(f32[4]{0:T(128)} %skip) | copy-start | bytes 52
  4.6 6.3 %collective-permute-start.1 = (bf16[2,4,32,1024]{3,2,1,0:T(8,128)(2,1)}, bf16[2,4,32,1024]{3,2,1,0:T(8,128)(2,1)S(1)}, u32[]{:S(2)}, u32[]{:S(2)}) collective-permute-start(bf16[2,4,32,1024]{3,2,1,0:T(8,128)(2,1)} %get-tuple-element.32), channel_id=1, source_target_pairs={{0,1},{1,0},{2,3},{3,2},{4,5},{5,4},{6,7},{7,6},{8,9},{9,8},{10,11... | collective-permute-start | bytes 1572872 | tf_op jit(solution)/shard_map/ppermute | solution.py:531
  5.0 13.0 %all-to-all-start = ((bf16[8,16,1024]{2,1,0:T(8,128)(2,1)}), bf16[8,16,1024]{2,1,0:T(8,128)(2,1)S(1)}, u32[]{:S(2)}, u32[]{:S(2)}) async-start(bf16[8,16,1024]{2,1,0:T(8,128)(2,1)} %constant_dynamic-update-slice_fusion.prod), calls=%async_computation | async-start | bytes 524288 | tf_op jit(solution)/shard_map/all_to_all | solution.py:527
  10.9 0.8 %copy-start.4 = (bf16[2,4,32,1024]{3,2,1,0:T(8,128)(2,1)}, bf16[2,4,32,1024]{3,2,1,0:T(8,128)(2,1)S(1)}, u32[]{:S(2)}) copy-start(bf16[2,4,32,1024]{3,2,1,0:T(8,128)(2,1)S(1)} %collective-permute-done.1.came_ref) | copy-start | bytes 1572868
  18.0 22.0 %all-to-all-start.1 = ((bf16[8,2,32,1024]{3,2,1,0:T(8,128)(2,1)}), bf16[8,2,32,1024]{3,2,1,0:T(8,128)(2,1)S(1)}, u32[]{:S(2)}, u32[]{:S(2)}) async-start(bf16[8,2,32,1024]{3,2,1,0:T(8,128)(2,1)} %shard_map.83), calls=%async_computation.1 | async-start | bytes 2097152 | tf_op jit(solution)/shard_map/all_to_all | solution.py:527
  21.6 16.2 %collective-permute-start.3 = (bf16[8,16,1024]{2,1,0:T(8,128)(2,1)S(1)}, bf16[8,16,1024]{2,1,0:T(8,128)(2,1)S(1)}, u32[]{:S(2)}, u32[]{:S(2)}) collective-permute-start(bf16[8,16,1024]{2,1,0:T(8,128)(2,1)S(1)} %all-to-all-done.refs_0_), channel_id=1, source_target_pairs={{0,16},{2,18},{4,20},{6,22},{8,24},{10,26},{12,28},{14,30},{16,0},... | collective-permute-start | bytes 786440 | tf_op jit(solution)/shard_map/ppermute | solution.py:528
  26.1 42.1 %copy-start.1 = (bf16[4,16,1024]{2,1,0:T(8,128)(2,1)S(1)}, bf16[4,16,1024]{2,1,0:T(8,128)(2,1)}, u32[]{:S(2)}) copy-start(bf16[4,16,1024]{2,1,0:T(8,128)(2,1)} %get-tuple-element.43.gate) | copy-start | bytes 393220
  26.1 1.9 %collective-permute-start.4 = (bf16[4,16,1024]{2,1,0:T(8,128)(2,1)}, bf16[4,16,1024]{2,1,0:T(8,128)(2,1)S(1)}, u32[]{:S(2)}, u32[]{:S(2)}) collective-permute-start(bf16[4,16,1024]{2,1,0:T(8,128)(2,1)} %get-tuple-element.36), channel_id=1, source_target_pairs={{0,1},{1,0},{2,3},{3,2},{4,5},{5,4},{6,7},{7,6},{8,9},{9,8},{10,11... | collective-permute-start | bytes 393224 | tf_op jit(solution)/shard_map/ppermute | solution.py:531
  26.2 11.6 %collective-permute-start.2 = (bf16[8,16,1024]{2,1,0:T(8,128)(2,1)S(1)}, bf16[8,16,1024]{2,1,0:T(8,128)(2,1)S(1)}, u32[]{:S(2)}, u32[]{:S(2)}) collective-permute-start(bf16[8,16,1024]{2,1,0:T(8,128)(2,1)S(1)} %all-to-all-done.refs_0_), channel_id=1, source_target_pairs={{0,1},{1,0},{2,3},{3,2},{4,5},{5,4},{6,7},{7,6},{8,9},{9,8},{10,11... | collective-permute-start | bytes 786440 | tf_op jit(solution)/shard_map/ppermute | solution.py:531
  26.7 1.3 %collective-permute-start.5 = (f32[4]{0:T(128)}, f32[4]{0:T(128)S(1)}, u32[]{:S(2)}, u32[]{:S(2)}) collective-permute-start(f32[4]{0:T(128)} %skip), channel_id=1, source_target_pairs={{0,1},{1,0},{2,3},{3,2},{4,5},{5,4},{6,7},{7,6},{8,9},{9,8},{10,11... | collective-permute-start | bytes 56 | tf_op jit(solution)/shard_map/ppermute | solution.py:531
  26.8 0.7 copy-start.2
  37.7 1.5 %collective-permute-start.6 = (bf16[8,16,1024]{2,1,0:T(8,128)(2,1)S(1)}, bf16[8,16,1024]{2,1,0:T(8,128)(2,1)S(1)}, u32[]{:S(2)}, u32[]{:S(2)}) collective-permute-start(bf16[8,16,1024]{2,1,0:T(8,128)(2,1)S(1)} %collective-permute-done.3.refs_2_), channel_id=1, source_target_pairs={{0,1},{1,0},{2,3},{3,2},{4,5},{5,4},{6,7},{7,6},{8,9},{9,8},{10,11... | collective-permute-start | bytes 786440 | tf_op jit(solution)/shard_map/ppermute | solution.py:531
  45.4 2.0 %collective-permute-start.7 = (bf16[16,16,1024]{2,1,0:T(8,128)(2,1)S(1)}, bf16[16,16,1024]{2,1,0:T(8,128)(2,1)S(1)}, u32[]{:S(2)}, u32[]{:S(2)}) collective-permute-start(bf16[16,16,1024]{2,1,0:T(8,128)(2,1)S(1)} %get-tuple-element.42), channel_id=1, source_target_pairs={{0,1},{1,0},{2,3},{3,2},{4,5},{5,4},{6,7},{7,6},{8,9},{9,8},{10,11... | collective-permute-start | bytes 1572872 | tf_op jit(solution)/shard_map/ppermute | solution.py:531
  69.1 1.6 %collective-permute-start.8 = (bf16[8,16384]{1,0:T(8,128)(2,1)S(1)}, bf16[8,16384]{1,0:T(8,128)(2,1)S(1)}, u32[]{:S(2)}, u32[]{:S(2)}) collective-permute-start(bf16[8,16384]{1,0:T(8,128)(2,1)S(1)} %get-tuple-element.48), channel_id=1, source_target_pairs={{0,1},{1,0},{2,3},{3,2},{4,5},{5,4},{6,7},{7,6},{8,9},{9,8},{10,11... | collective-permute-start | bytes 786440 | tf_op jit(solution)/shard_map/ppermute | solution.py:531
